TPU v7x, 32 devices: a whole 2x2x4 slice. The times are simulated.
32 devices in a mesh: grp: 2 (over y), seq: 4 (over z), mdl: 4 (over x, core).
Axes of the slice: x: 2, y: 2, z: 4, core: 2. Of those that a mesh axis runs over, the one named last changes fastest.
Arguments:
- class_rows: bfloat16 [2048, 1536], P(('grp', 'seq')), parts along dimension 0, may hold values from -6 to 6
- destination: int32 [2048, 1], P(('grp', 'seq')), parts along dimension 0, may hold values from 0 to 3; in each aligned block of 256 rows (0 to 255, 256 to 511, ...) at most 128 rows name the same one
- norm1_gain: float32 [1536], replicated, may hold values from 0.5 to 1.5
- gate_weight: bfloat16 [1536, 4096], P(None, 'mdl'), may hold values from -0.15625 to 0.15625
- up_weight: bfloat16 [1536, 4096], P(None, 'mdl'), may hold values from -0.15625 to 0.15625
- down_weight: bfloat16 [4096, 1536], P('mdl'), may hold values from -0.09375 to 0.09375
- layer_scale: float32 [1536], replicated, may hold values from 0.3 to 1.5
- norm2_gain: float32 [1536], replicated, may hold values from 0.5 to 1.5
- proj_weight: bfloat16 [1536, 768], P(None, 'mdl'), may hold values from -0.15625 to 0.15625
- norm3_gain: float32 [768], replicated, may hold values from 0.5 to 1.5
- query_weight: bfloat16 [768, 768], P(None, 'mdl'), may hold values from -1 to 1
- key_weight: bfloat16 [768, 768], P(None, 'mdl'), may hold values from -1 to 1
- value_weight: bfloat16 [768, 768], P(None, 'mdl'), may hold values from -0.21875 to 0.21875
- out_weight: bfloat16 [768, 768], P('mdl'), may hold values from -0.21875 to 0.21875
Outputs:
- slide_out: bfloat16 [4096, 768], P(('grp', 'seq'), 'mdl'), parts along dimension 0
There are 2 independent parts, one for each index of `grp`. A program takes and returns all parts, laid end to end along the dimension named above; an argument that names none is the same for every part. Nothing has to cross between parts.
Inputs may be any that keep to these rules, and one draw needn't show every extreme that they name: `destination`: among the rows of one device each owner is named by at most 128 rows, and by exactly 128 in some device's rows; every owner is named by some row.
All inputs are finite; a program needn't handle non-finite values.
Results may differ from a plain program's by a relative error of at most 0.019.
Values may be sent and summed in bfloat16 or wider, within the bound.
No kernel may reach another device: no remote copies, remote signals or barrier semaphores. Data moves between devices by JAX's collectives and lax.ppermute only.
A program may use at most 128 MiB of HBM per device.

v0:
```python
import jax
import jax.numpy as jnp
from jax import lax
from jax.sharding import PartitionSpec as P

HD = 48
RATE = 4


epsilon = 1e-06
masked_score = -1e30


def layer_norm(features, norm_gain):
    middle = jnp.mean(features, axis=-1, keepdims=True)
    centred = features - middle
    spread = jnp.mean(centred * centred, axis=-1, keepdims=True)
    return centred * lax.rsqrt(spread + epsilon) * norm_gain


def encode(
    row_block, norm1_gain, gate_weight, up_weight, down_weight, layer_scale, norm2_gain, proj_weight
):
    normed = layer_norm(row_block.astype(jnp.float32), norm1_gain).astype(jnp.bfloat16)
    gate = jnp.dot(normed, gate_weight, preferred_element_type=jnp.float32)
    upward = jnp.dot(normed, up_weight, preferred_element_type=jnp.float32)
    hidden = (jax.nn.silu(gate) * upward).astype(jnp.bfloat16)
    partial_sums = jnp.dot(hidden, down_weight, preferred_element_type=jnp.float32)
    feedfwd = lax.psum(partial_sums, "mdl")
    stream = row_block.astype(jnp.float32) + layer_scale * feedfwd
    final = layer_norm(stream, norm2_gain).astype(jnp.bfloat16)
    return jnp.dot(final, proj_weight, preferred_element_type=jnp.float32).astype(jnp.bfloat16)


def per_device(
    class_rows,
    destination,
    norm1_gain,
    gate_weight,
    up_weight,
    down_weight,
    layer_scale,
    norm2_gain,
    proj_weight,
    norm3_gain,
    query_weight,
    key_weight,
    value_weight,
    out_weight,
):
    tile_count = class_rows.shape[0]
    seq_count = lax.axis_size("seq")
    capacity = 2 * tile_count // seq_count
    slot_count = seq_count * capacity
    target = destination[:, 0]
    onehot = (target[:, None] == jnp.arange(seq_count, dtype=jnp.int32)[None, :]).astype(jnp.int32)
    earlier = jnp.cumsum(onehot, axis=0) - onehot
    arrival = jnp.sum(earlier * onehot, axis=1)
    position = target * capacity + arrival
    filled = (
        jnp.zeros((slot_count,), jnp.bfloat16)
        .at[position]
        .set(jnp.ones((tile_count,), jnp.bfloat16))
    )
    own_embedded = encode(
        class_rows,
        norm1_gain,
        gate_weight,
        up_weight,
        down_weight,
        layer_scale,
        norm2_gain,
        proj_weight,
    )
    outgoing = (
        jnp.zeros((slot_count, own_embedded.shape[1]), jnp.bfloat16).at[position].set(own_embedded)
    )
    arrived, occupied = (
        lax.all_to_all(
            outgoing.reshape(seq_count, capacity, -1),
            "seq",
            split_axis=0,
            concat_axis=0,
            tiled=True,
        ),
        lax.all_to_all(
            filled.reshape(seq_count, capacity), "seq", split_axis=0, concat_axis=0, tiled=True
        ),
    )
    embedded = arrived.reshape(slot_count, -1)
    occupied = occupied.reshape(slot_count)
    emb_full = lax.all_gather(embedded, "mdl", axis=1, tiled=True)
    normed = layer_norm(emb_full.astype(jnp.float32), norm3_gain).astype(jnp.bfloat16)
    head_count = query_weight.shape[1] // HD
    queries = (
        jnp.dot(normed, query_weight, preferred_element_type=jnp.float32)
        .astype(jnp.bfloat16)
        .reshape(slot_count, head_count, HD)
    )
    keys = (
        jnp.dot(normed, key_weight, preferred_element_type=jnp.float32)
        .astype(jnp.bfloat16)
        .reshape(slot_count, head_count, HD)
    )
    values = (
        jnp.dot(normed, value_weight, preferred_element_type=jnp.float32)
        .astype(jnp.bfloat16)
        .reshape(slot_count, head_count, HD)
    )
    scale = HD ** (-0.5)
    alive = (occupied > 0)[None, None, :]
    scores = jnp.einsum("qhd,khd->hqk", queries, keys, preferred_element_type=jnp.float32) * scale
    scores = jnp.where(alive, scores, masked_score)
    peak_local = jnp.max(scores, axis=-1)
    weights = jnp.where(alive, jnp.exp(scores - peak_local[..., None]), 0.0)
    total_local = jnp.sum(weights, axis=-1).T
    summed_local = jnp.einsum(
        "hqk,khd->qhd", weights.astype(jnp.bfloat16), values, preferred_element_type=jnp.float32
    )
    peak_local = peak_local.T
    sparse_count = slot_count // RATE
    head_ids = lax.axis_index("mdl") * head_count + jnp.arange(head_count, dtype=jnp.int32)
    chosen = jnp.arange(RATE, dtype=jnp.int32)[:, None] == (head_ids % RATE)[None, :]

    def pick_heads(tensor):
        grouped = tensor.reshape(sparse_count, RATE, head_count, -1)
        return jnp.sum(
            jnp.where(chosen[None, :, :, None], grouped, jnp.zeros((), grouped.dtype)), axis=1
        )

    sparse_queries = pick_heads(queries)
    sparse_keys = pick_heads(keys)
    sparse_values = pick_heads(values)
    sparse_live = jnp.sum(
        jnp.where(
            chosen[None],
            occupied.reshape(sparse_count, RATE)[:, :, None],
            jnp.zeros((), jnp.bfloat16),
        ),
        axis=1,
    )
    running = jnp.full((sparse_count, head_count), masked_score, jnp.float32)
    piece_keys = lax.all_gather(sparse_keys, "seq", axis=0, tiled=True)
    piece_values = lax.all_gather(sparse_values, "seq", axis=0, tiled=True)
    piece_live = lax.all_gather(sparse_live, "seq", axis=0, tiled=True)
    piece_scores = (
        jnp.einsum("qhd,khd->qhk", sparse_queries, piece_keys, preferred_element_type=jnp.float32)
        * scale
    )
    piece_alive = (piece_live.T > 0)[None]
    piece_scores = jnp.where(piece_alive, piece_scores, masked_score)
    newest = jnp.maximum(running, jnp.max(piece_scores, axis=-1))
    piece_weights = jnp.where(piece_alive, jnp.exp(piece_scores - newest[..., None]), 0.0)
    summed = jnp.einsum(
        "qhk,khd->qhd",
        piece_weights.astype(jnp.bfloat16),
        piece_values,
        preferred_element_type=jnp.float32,
    )
    total = jnp.sum(piece_weights, axis=-1)
    spread_peak = jnp.where(chosen[None], newest[:, None, :], masked_score).reshape(
        slot_count, head_count
    )
    spread_total = jnp.where(chosen[None], total[:, None, :], 0.0).reshape(slot_count, head_count)
    spread_summed = jnp.where(chosen[None, :, :, None], summed[:, None, :, :], 0.0).reshape(
        slot_count, head_count, HD
    )
    highest = jnp.maximum(peak_local, spread_peak)
    first_weight = jnp.exp(peak_local - highest)
    second_weight = jnp.exp(spread_peak - highest)
    mixed = (first_weight[..., None] * summed_local + second_weight[..., None] * spread_summed) / (
        first_weight * total_local + second_weight * spread_total
    )[..., None]
    attended = mixed.reshape(slot_count, head_count * HD).astype(jnp.bfloat16)
    out_columns = lax.all_to_all(out_weight, "mdl", split_axis=1, concat_axis=0, tiled=True)
    projected = jnp.dot(
        lax.all_gather(attended, "mdl", axis=1, tiled=True),
        out_columns,
        preferred_element_type=jnp.float32,
    )
    result = (projected + embedded.astype(jnp.float32)) * occupied.astype(jnp.float32)[:, None]
    return result.astype(jnp.bfloat16)


def solution(mesh):
    return jax.shard_map(
        per_device,
        mesh=mesh,
        in_specs=(
            P(("grp", "seq"), None),
            P(("grp", "seq"), None),
            P(),
            P(None, "mdl"),
            P(None, "mdl"),
            P("mdl", None),
            P(),
            P(),
            P(None, "mdl"),
            P(),
            P(None, "mdl"),
            P(None, "mdl"),
            P(None, "mdl"),
            P("mdl", None),
        ),
        out_specs=P(("grp", "seq"), "mdl"),
        check_vma=False,
    )
```

profile of v0, /device:TPU:0, one launch (start us, length us, event | category | flops | bytes accessed | tf_op | source)
XLA Modules:
  0.0 178.6 jit_solution(15514931041192228653)
XLA Ops:
  6.5 1.5 convert_reduce_fusion
  8.0 1.5 fusion.10
  9.5 3.9 %fusion.67 = f32[256,1024]{1,0:T(8,128)} fusion(bf16[1536,1024]{1,0:T(8,128)(2,1)} %param.17, bf16[256,1536]{1,0:T(8,128)(2,1)S(1)} %copy-done.1, f32[1536]{0:T(1024)S(1)} %copy-done.22, f32[256]{0:T(256)S(1)} %add_rsqrt_fusion.2, f32[256]{0:T(256)S(1)} %broadcast_multiply_fusion.2), kind=kOutput, calls=%fused_computation.99 | convolution fusion | flops 807272448 | bytes 4988928 | tf_op jit(solution)/shard_map/dot_general | solution.py:25
  13.5 5.5 %fusion.38 = f32[256,1536]{1,0:T(8,128)} fusion(bf16[1024,1536]{1,0:T(8,128)(2,1)S(1)} %copy-done, bf16[1536,1024]{1,0:T(8,128)(2,1)} %param.18, f32[256,1024]{1,0:T(8,128)} %fusion.67, bf16[256,1536]{1,0:T(8,128)(2,1)} %param.14, f32[1536]{0:T(1024)S(1)} %copy-done.22, f32[256]{0:T(256)S(1)} %add_rsqrt_fusion.2, f32[256]{0:T(256)S(1)} %broadcast_multiply_fusion.2), kind=kOutput, calls=%fused_computation.47 | convolution fusion | flops 1614151680 | bytes 9707520 | tf_op jit(solution)/shard_map/dot_general | solution.py:28
  19.0 0.6 copy-done.10
  19.6 1.2 reduce-window.6
  21.3 2.2 %scatter_custom_fusion = bf16[512]{0:T(512)(128)(2,1)S(1)} fusion(s32[256]{0:T(256)S(1)} %bitcast.108, bf16[256]{0:T(256)(128)(2,1)S(1)} %broadcast.198, bf16[]{:T(256)} %constant.24.clone.1), kind=kCustom, calls=%fused_computation.92 | custom fusion | bytes 1026 | tf_op jit(solution)/shard_map/scatter | solution.py:63
  23.4 0.6 copy.52
  24.0 6.3 %all-to-all-start = ((bf16[4,1,128]{2,1,0:T(2,128)(2,1)}), bf16[4,1,128]{2,1,0:T(2,128)(2,1)S(1)}, u32[]{:S(2)}, u32[]{:S(2)}) async-start(bf16[4,1,128]{2,1,0:T(2,128)(2,1)} %copy.52), calls=%async_computation | async-start | bytes 4096 | tf_op jit(solution)/shard_map/all_to_all | solution.py:86
  30.4 0.5 copy-done.16
  31.0 0.8 broadcast_in_dim.184
  31.8 0.9 copy.67
  32.8 3.1 %all-to-all-done = bf16[4,1,128]{2,1,0:T(2,128)(2,1)S(1)} async-done(((bf16[4,1,128]{2,1,0:T(2,128)(2,1)}), bf16[4,1,128]{2,1,0:T(2,128)(2,1)S(1)}, u32[]{:S(2)}, u32[]{:S(2)}) %all-to-all-start) | async-done | bytes 1056 | tf_op jit(solution)/shard_map/all_to_all | solution.py:86
  35.8 3.5 %all-to-all-start.2 = ((bf16[192,4,192]{0,2,1:T(8,128)(2,1)}), bf16[192,4,192]{0,2,1:T(8,128)(2,1)S(1)}, u32[]{:S(2)}, u32[]{:S(2)}) async-start(bf16[192,4,192]{0,2,1:T(8,128)(2,1)} %bitcast.94), calls=%async_computation.2 | async-start | bytes 786432 | tf_op jit(solution)/shard_map/all_to_all | solution.py:175
  39.3 0.6 fusion.74
  39.9 0.7 broadcast_in_dim.185
  40.6 0.9 select_reduce_fusion.3
  41.5 8.3 %all_gather.16 = bf16[512,4]{0,1:T(4,128)(2,1)S(1)} all-gather(bf16[128,4]{0,1:T(4,128)(2,1)S(1)} %select_reduce_fusion.3), channel_id=1, replica_groups=mesh['grp'=2,'seq'=4,'mdl'=4] {'seq'}, dimensions={0}, use_global_device_ids=true | all-gather | bytes 5120 | tf_op jit(solution)/shard_map/all_gather | solution.py:145
  49.9 17.2 %all-reduce.2.cloned.1.call-done = f32[256,1536]{1,0:T(8,128)} async-done(((f32[256,1536]{1,0:T(8,128)}), f32[256,1536]{1,0:T(8,128)}) %all-reduce.2.cloned.1.call-update) | async-done | bytes 1572880 | tf_op jit(solution)/shard_map/psum | solution.py:29
  67.0 2.0 %fusion.47 = f32[256]{0:T(256)S(1)} fusion(f32[256,1536]{1,0:T(8,128)} %all-reduce.2.cloned.1.call-done, f32[1536]{0:T(1024)S(1)} %copy-done.9, bf16[256,1536]{1,0:T(8,128)(2,1)} %param.14), kind=kLoop, calls=%fused_computation.58 | loop fusion | flops 1572608 | bytes 2366464 | tf_op jit(solution)/shard_map/reduce_sum | solution.py:15
  69.1 0.3 copy-done.3
  69.4 0.4 multiply_reduce_fusion
  69.8 0.4 copy-done.18
  70.2 1.2 convolution_convert_fusion.3
  71.4 1.7 copy.53
  73.1 2.5 %scatter_custom_fusion.1 = bf16[512,192]{1,0:T(8,128)(2,1)} fusion(s32[256]{0:T(256)} %bitcast.109, bf16[256,192]{1,0:T(8,128)(2,1)} %copy.53, bf16[]{:T(256)} %constant.24.clone.1), kind=kCustom, calls=%fused_computation.62 | custom fusion | bytes 197120 | tf_op jit(solution)/shard_map/scatter | solution.py:76
  75.6 1.8 copy.54
  77.3 0.7 copy-done.4
  78.1 4.6 %all-to-all-start.1 = ((bf16[4,128,192]{1,2,0:T(8,128)(2,1)}), bf16[4,128,192]{1,2,0:T(8,128)(2,1)S(1)}, u32[]{:S(2)}, u32[]{:S(2)}) async-start(bf16[4,128,192]{1,2,0:T(8,128)(2,1)} %copy.54), calls=%async_computation.1 | async-start | bytes 393216 | tf_op jit(solution)/shard_map/all_to_all | solution.py:79
  82.7 0.6 compare_reduce_fusion
  83.3 2.0 %copy.68 = bf16[4,192,192]{1,0,2:T(4,128)(2,1)} copy(bf16[4,192,192]{1,2,0:T(8,128)(2,1)} %bitcast.93) | data formatting | bytes 589824 | tf_op jit(solution)/shard_map/all_to_all | solution.py:175
  85.3 2.0 %all_to_all.29 = bf16[768,192]{0,1:T(8,128)(2,1)} reshape(bf16[4,192,192]{1,0,2:T(4,128)(2,1)} %copy.68) | data formatting | bytes 589824 | tf_op jit(solution)/shard_map/all_to_all | solution.py:175
  87.4 2.6 %all-to-all-done.1 = bf16[4,128,192]{1,2,0:T(8,128)(2,1)S(1)} async-done(((bf16[4,128,192]{1,2,0:T(8,128)(2,1)}), bf16[4,128,192]{1,2,0:T(8,128)(2,1)S(1)}, u32[]{:S(2)}, u32[]{:S(2)}) %all-to-all-start.1) | async-done | bytes 196640 | tf_op jit(solution)/shard_map/all_to_all | solution.py:79
  90.0 8.4 %all_gather.15 = bf16[512,768]{0,1:T(8,128)(2,1)S(1)} all-gather(bf16[512,192]{0,1:T(8,128)(2,1)S(1)} %copy_bitcast_fusion), channel_id=1, replica_groups=mesh['grp'=2,'seq'=4,'mdl'=4] {'mdl'}, dimensions={1}, use_global_device_ids=true | all-gather | bytes 983040 | tf_op jit(solution)/shard_map/all_gather | solution.py:92
  98.6 0.3 fusion.13
  98.8 0.5 convolution_convert_fusion.1
  99.5 1.1 convolution_convert_fusion.2
  100.7 1.1 convolution_convert_fusion
  101.8 1.8 copy.62
  103.5 2.0 %reshape_reshape.11 = bf16[128,4,4,48]{3,2,1,0:T(4,128)(2,1)} reshape(bf16[512,192]{1,0:T(8,128)(2,1)} %copy.62) | data formatting | bytes 393216 | tf_op jit(solution)/shard_map/reshape;reshape | solution.py:126
  105.6 1.8 copy.59
  107.3 2.0 %reshape_reshape.10 = bf16[128,4,4,48]{3,2,1,0:T(4,128)(2,1)} reshape(bf16[512,192]{1,0:T(8,128)(2,1)} %copy.59) | data formatting | bytes 393216 | tf_op jit(solution)/shard_map/reshape;reshape | solution.py:126
  109.4 0.8 copy.57
  110.2 2.1 %reshape_reshape.9 = bf16[128,4,4,48]{3,2,1,0:T(4,128)(2,1)} reshape(bf16[512,192]{1,0:T(8,128)(2,1)} %copy.57) | data formatting | bytes 393216 | tf_op jit(solution)/shard_map/reshape;reshape | solution.py:126
  112.3 3.8 %select_reduce_fusion.1 = (bf16[128,4,48]{2,1,0:T(4,128)(2,1)}, bf16[128,4,48]{2,1,0:T(4,128)(2,1)}, bf16[128,4,48]{2,1,0:T(4,128)(2,1)}) fusion(bf16[128,4,4,48]{3,2,1,0:T(4,128)(2,1)} %reshape_reshape.10, pred[4,4]{1,0:T(4,128)(4,1)S(1)} %copy-done.17, bf16[128,4,4,48]{3,2,1,0:T(4,128)(2,1)} %reshape_reshape.11, bf16[128,4,4,48]{3,2,1,0:T(4,128)(2,1)} %reshape_reshape.9), kind=kLoop, calls=%fused_computation.54 | loop fusion | flops 516096 | bytes 737296 | tf_op jit(solution)/shard_map/reduce_sum | solution.py:127
  116.1 1.6 copy.63
  117.7 1.6 copy.58
  119.3 13.1 %all_gather.17 = bf16[512,4,48]{0,2,1:T(8,128)(2,1)S(1)} all-gather(bf16[128,4,48]{0,2,1:T(8,128)(2,1)} %copy.58), channel_id=1, replica_groups=mesh['grp'=2,'seq'=4,'mdl'=4] {'seq'}, dimensions={0}, use_global_device_ids=true | all-gather | bytes 245760 | tf_op jit(solution)/shard_map/all_gather | solution.py:143
  132.5 12.7 %all_gather.18 = bf16[512,4,48]{0,2,1:T(8,128)(2,1)S(1)} all-gather(bf16[128,4,48]{0,2,1:T(8,128)(2,1)} %copy.63), channel_id=1, replica_groups=mesh['grp'=2,'seq'=4,'mdl'=4] {'seq'}, dimensions={0}, use_global_device_ids=true | all-gather | bytes 245760 | tf_op jit(solution)/shard_map/all_gather | solution.py:144
  145.2 1.4 fusion.75
  146.6 0.4 fusion.36
  147.0 1.1 convolution_bitcast_fusion
  148.1 1.7 copy.65
  149.8 0.8 broadcast_in_dim.193
  150.7 1.1 broadcast_in_dim.194
  151.8 0.8 broadcast_in_dim.203
  152.6 1.1 broadcast_in_dim.204
  153.8 2.1 %broadcast_in_dim.200 = f32[128,4,4,48]{3,1,0,2:T(4,128)} broadcast(f32[128,4,48]{2,0,1:T(8,128)} %copy.65), dimensions={0,2,3} | broadcast | bytes 491520 | tf_op jit(solution)/shard_map/jit(_where)/broadcast_in_dim | solution.py:165
  155.9 2.3 %copy.66 = f32[512,4,48]{0,2,1:T(8,128)} copy(f32[512,4,48]{2,0,1:T(8,128)} %bitcast.92) | data formatting | bytes 786432 | tf_op jit(solution)/shard_map/jit(_where)/broadcast_in_dim | solution.py:165
  158.2 2.0 %fusion = (f32[4,512]{1,0:T(4,128)S(1)}, f32[4,512,512]{1,2,0:T(8,128)S(1)}) fusion(pred[512]{0:T(512)(128)(4,1)} %bitcast.103, bf16[512,4,48]{0,2,1:T(8,128)(2,1)} %bitcast.97, bf16[512,4,48]{0,2,1:T(8,128)(2,1)S(1)} %bitcast.96), kind=kOutput, calls=%fused_computation.4 | convolution fusion | flops 103806976 | bytes 4596224 | tf_op jit(solution)/shard_map/qhd,khd->hqk/dot_general | solution.py:112
  160.2 1.1 fusion.1
  161.5 1.1 fusion.33
  162.6 8.2 %all_gather.19 = bf16[512,768]{0,1:T(8,128)(2,1)S(1)} all-gather(bf16[512,192]{0,1:T(8,128)(2,1)S(1)} %bitcast.99), channel_id=1, replica_groups=mesh['grp'=2,'seq'=4,'mdl'=4] {'mdl'}, dimensions={1}, use_global_device_ids=true | all-gather | bytes 983040 | tf_op jit(solution)/shard_map/all_gather | solution.py:177
  170.8 1.0 fusion.29
  (73 shorter events, 1.2 us)
Async XLA Ops:
  6.5 6.9 %copy-start = (bf16[1024,1536]{1,0:T(8,128)(2,1)S(1)}, bf16[1024,1536]{1,0:T(8,128)(2,1)}, u32[]{:S(2)}) copy-start(bf16[1024,1536]{1,0:T(8,128)(2,1)} %param.19) | copy-start | bytes 9437188
  6.5 3.0 %copy-start.22 = (f32[1536]{0:T(1024)S(1)}, f32[1536]{0:T(1024)}, u32[]{:S(2)}) copy-start(f32[1536]{0:T(1024)} %param.16) | copy-start | bytes 18436
  6.5 60.5 %all-reduce.2.cloned.1.call-start = ((), (), s32[]{:S(2)}) async-start(), calls=%async_computation.3 | async-start | bytes 3145728 | tf_op jit(solution)/shard_map/psum | solution.py:29
  6.5 3.0 %copy-start.1 = (bf16[256,1536]{1,0:T(8,128)(2,1)S(1)}, bf16[256,1536]{1,0:T(8,128)(2,1)}, u32[]{:S(2)}) copy-start(bf16[256,1536]{1,0:T(8,128)(2,1)} %param.14) | copy-start | bytes 2359300
  18.9 0.7 copy-start.10
  18.9 12.9 %copy-start.7 = (bf16[192,768]{1,0:T(8,128)(2,1)S(1)}, bf16[192,768]{1,0:T(8,128)(2,1)}, u32[]{:S(2)}) copy-start(bf16[192,768]{1,0:T(8,128)(2,1)} %param.27) | copy-start | bytes 884740
  18.9 48.1 %copy-start.9 = (f32[1536]{0:T(1024)S(1)}, f32[1536]{0:T(1024)}, u32[]{:S(2)}) copy-start(f32[1536]{0:T(1024)} %param.20) | copy-start | bytes 18436
  21.3 9.1 %copy-start.15 = (s32[256,1]{0,1:T(1,128)}, s32[256,1]{0,1:T(1,128)S(1)}, u32[]{:S(2)}) copy-start(s32[256,1]{0,1:T(1,128)S(1)} %compare_select_fusion) | copy-start | bytes 3076
  24.0 11.8 %all-to-all-start = ((bf16[4,1,128]{2,1,0:T(2,128)(2,1)}), bf16[4,1,128]{2,1,0:T(2,128)(2,1)S(1)}, u32[]{:S(2)}, u32[]{:S(2)}) async-start(bf16[4,1,128]{2,1,0:T(2,128)(2,1)} %copy.52), calls=%async_computation | async-start | bytes 4096 | tf_op jit(solution)/shard_map/all_to_all | solution.py:86
  30.4 0.5 copy-start.16
  31.0 4.8 %copy-start.14 = (pred[4,4]{0,1:T(4,128)(4,1)}, pred[4,4]{0,1:T(4,128)(4,1)S(1)}, u32[]{:S(2)}) copy-start(pred[4,4]{0,1:T(4,128)(4,1)S(1)} %copy.56) | copy-start | bytes 52
  35.8 41.5 %all-to-all-start.2 = ((bf16[192,4,192]{0,2,1:T(8,128)(2,1)}), bf16[192,4,192]{0,2,1:T(8,128)(2,1)S(1)}, u32[]{:S(2)}, u32[]{:S(2)}) async-start(bf16[192,4,192]{0,2,1:T(8,128)(2,1)} %bitcast.94), calls=%async_computation.2 | async-start | bytes 786432 | tf_op jit(solution)/shard_map/all_to_all | solution.py:175
  67.0 2.1 %copy-start.2 = (bf16[256,1536]{1,0:T(8,128)(2,1)S(1)}, bf16[256,1536]{1,0:T(8,128)(2,1)}, u32[]{:S(2)}) copy-start(bf16[256,1536]{1,0:T(8,128)(2,1)} %param.14) | copy-start | bytes 2359300
  67.0 2.4 %copy-start.3 = (f32[256,1536]{1,0:T(8,128)S(1)}, f32[256,1536]{1,0:T(8,128)}, u32[]{:S(2)}) copy-start(f32[256,1536]{1,0:T(8,128)} %all-reduce.2.cloned.1.call-done) | copy-start | bytes 4718596
  69.1 1.1 copy-start.18
  69.1 1.1 copy-start.23
  77.3 0.7 copy-start.4
  78.1 11.9 %all-to-all-start.1 = ((bf16[4,128,192]{1,2,0:T(8,128)(2,1)}), bf16[4,128,192]{1,2,0:T(8,128)(2,1)S(1)}, u32[]{:S(2)}, u32[]{:S(2)}) async-start(bf16[4,128,192]{1,2,0:T(8,128)(2,1)} %copy.54), calls=%async_computation.1 | async-start | bytes 393216 | tf_op jit(solution)/shard_map/all_to_all | solution.py:79
  87.4 11.5 %copy-start.24 = (f32[768]{0:T(1024)S(1)}, f32[768]{0:T(1024)}, u32[]{:S(2)}) copy-start(f32[768]{0:T(1024)} %param.23) | copy-start | bytes 9220
  90.0 8.8 %copy-start.19 = (bf16[768,192]{0,1:T(8,128)(2,1)S(1)}, bf16[768,192]{0,1:T(8,128)(2,1)}, u32[]{:S(2)}) copy-start(bf16[768,192]{0,1:T(8,128)(2,1)} %param.25) | copy-start | bytes 884740
  98.5 1.0 copy-start.20
  99.5 1.1 copy-start.21
  103.5 8.8 %copy-start.17 = (pred[4,4]{1,0:T(4,128)(4,1)S(1)}, pred[4,4]{1,0:T(4,128)(4,1)}, u32[]{:S(2)}) copy-start(pred[4,4]{1,0:T(4,128)(4,1)} %copy-done.16) | copy-start | bytes 52
  158.2 2.0 %copy-start.13 = (pred[4,128]{1,0:T(4,128)(4,1)S(1)}, pred[4,128]{1,0:T(4,128)(4,1)}, u32[]{:S(2)}) copy-start(pred[4,128]{1,0:T(4,128)(4,1)} %compare_reduce_fusion) | copy-start | bytes 1540
  160.2 1.2 copy-start.12
  160.2 1.2 copy-start.6
  160.2 1.2 copy-start.8
  161.5 9.3 %copy-start.5 = (bf16[768,192]{0,1:T(8,128)(2,1)S(1)}, bf16[768,192]{0,1:T(8,128)(2,1)}, u32[]{:S(2)}) copy-start(bf16[768,192]{0,1:T(8,128)(2,1)} %all_to_all.29) | copy-start | bytes 884740
  161.5 9.3 %copy-start.11 = (f32[4,1,128]{2,1,0:T(1,128)S(1)}, f32[4,1,128]{2,1,0:T(1,128)}, u32[]{:S(2)}) copy-start(f32[4,1,128]{2,1,0:T(1,128)} %get-tuple-element.11) | copy-start | bytes 6148
Sparse Core Ops, SparseCore 0:
  19.1 47.8 all-reduce.1
where the time goes:
time: 180 us; the launch traced here: 179 us
  blocking collectives  50.7 us (28%)
  local copies, waits for them, and re-layouts  42.3 us (24%)
  waiting for transfers between devices  22.9 us (13%)
  matrix products  20 us (11%)
  other arithmetic  14.7 us (8%)
  starting transfers between devices  14.4 us (8%)
  between operations  13.7 us (8%)
    psum x1, waiting for transfers between devices, encode(): feedfwd = lax.psum(partial_sums, 'mdl')  17.2 us
    all_gather x1, blocking collectives, per_device(): piece_keys = lax.all_gather(sparse_keys, 'seq', axis=0, tiled=True)  13.1 us
    all_gather x1, blocking collectives, per_device(): piece_values = lax.all_gather(sparse_values, 'seq', axis=0, tiled=True)  12.7 us
    all_gather x1, blocking collectives, per_device(): emb_full = lax.all_gather(embedded, 'mdl', axis=1, tiled=True)  8.36 us
    all_gather x1, blocking collectives, per_device(): piece_live = lax.all_gather(sparse_live, 'seq', axis=0, tiled=True)  8.33 us
    all_gather x1, blocking collectives, per_device(): lax.all_gather(attended, 'mdl', axis=1, tiled=True)  8.16 us
    all_to_all x1, starting transfers between devices, per_device(): lax.all_to_all(filled.reshape(seq_count, capacity), 'seq', split_axis=0,...  6.32 us
    another operation x3, local copies, waits for them, and re-layouts, pick_heads(): grouped = tensor.reshape(sparse_count, RATE, head_count, -1)  6.13 us
  transfers between devices with their start and end apart: 4, of which 3 were waited for; matrix products, arithmetic and copies ran while one was open for 12% of the time, Pallas kernels for 0%

commit v1 on v0

v1 whole, which is shorter than its diff:
```python
import functools

import jax
import jax.numpy as jnp
from jax import lax
from jax.experimental import pallas as pl
from jax.experimental.pallas import tpu as pltpu
from jax.sharding import PartitionSpec as P

HD = 48
RATE = 4
EPSILON = 1e-06
MASKED = -1e30
VMEM_LIMIT = 48 * 1024 * 1024
LOG2E = 1.4426950408889634

f32 = jnp.float32
bf16 = jnp.bfloat16


def layer_norm(features, norm_gain):
    middle = jnp.mean(features, axis=-1, keepdims=True)
    centred = features - middle
    spread = jnp.mean(centred * centred, axis=-1, keepdims=True)
    return centred * lax.rsqrt(spread + EPSILON) * norm_gain


def dot(a, b):
    return jnp.dot(a, b, preferred_element_type=f32)


def dot_t(a, b):
    return lax.dot_general(a, b, (((1,), (1,)), ((), ())), preferred_element_type=f32)


def whole(shape):
    return pl.BlockSpec(shape, lambda *_: (0,) * len(shape))


SMEM = pl.BlockSpec(memory_space=pltpu.SMEM)
VMEM = pl.BlockSpec(memory_space=pltpu.VMEM)


def ffn_kernel(where_ref, rows_ref, gain_ref, gate_ref, up_ref, down_ref, keep_ref, send_ref, normed, total):
    step = pl.program_id(0)
    me = where_ref[0]
    share = rows_ref.shape[0] // 4

    @pl.when(step == 0)
    def _():
        for place, other in enumerate((0, 2, 1, 3)):
            start = pl.multiple_of((me ^ other) * share, share)
            rows = rows_ref[pl.ds(start, share), :].astype(f32)
            normed[place * share : (place + 1) * share, :] = layer_norm(rows, gain_ref[...]).astype(bf16)

    gate = dot(normed[...], gate_ref[...])
    upward = dot(normed[...], up_ref[...])
    hidden = (gate * jax.nn.sigmoid(gate) * upward).astype(bf16)
    part = dot(hidden, down_ref[...])

    @pl.when(step == 0)
    def _():
        total[...] = part

    @pl.when(step > 0)
    def _():
        total[...] += part

    @pl.when(step == pl.num_programs(0) - 1)
    def _():
        keep_ref[...] = total[: 2 * share, :]
        send_ref[...] = total[2 * share :, :].astype(bf16)


def feed_forward(where, rows, gain, gate_weight, up_weight, down_weight):
    tiles, width = rows.shape
    hidden = gate_weight.shape[1]
    steps = 4
    chunk = hidden // steps
    half = tiles // 2
    return pl.pallas_call(
        ffn_kernel,
        grid=(steps,),
        in_specs=[
            SMEM,
            whole((tiles, width)),
            whole((1, width)),
            pl.BlockSpec((width, chunk), lambda i: (0, i)),
            pl.BlockSpec((width, chunk), lambda i: (0, i)),
            pl.BlockSpec((chunk, width), lambda i: (i, 0)),
        ],
        out_specs=[whole((half, width)), whole((half, width))],
        out_shape=[jax.ShapeDtypeStruct((half, width), f32), jax.ShapeDtypeStruct((half, width), bf16)],
        scratch_shapes=[pltpu.VMEM((tiles, width), bf16), pltpu.VMEM((tiles, width), f32)],
        compiler_params=pltpu.CompilerParams(vmem_limit_bytes=VMEM_LIMIT),
        cost_estimate=pl.CostEstimate(
            flops=6 * tiles * width * hidden, bytes_accessed=6 * width * hidden, transcendentals=tiles * hidden
        ),
        name="feed_forward",
    )(where, rows, gain, gate_weight, up_weight, down_weight)


def embed_kernel(
    where_ref, rows_ref, keep_ref, near_ref, far_ref, scale_ref, gain_ref, p0, p1, p2, p3, out_ref, blocks
):
    me = where_ref[0]
    share = out_ref.shape[0]
    start = pl.multiple_of(me * share, share)
    rows = rows_ref[pl.ds(start, share), :].astype(f32)
    feedfwd = keep_ref[...] + near_ref[...].astype(f32) + far_ref[...].astype(f32)
    stream = rows + scale_ref[...] * feedfwd
    final = layer_norm(stream, gain_ref[...]).astype(bf16)
    for other, weight in enumerate((p0, p1, p2, p3)):
        blocks[me ^ other] = dot(final, weight[...])
    out_ref[...] = jnp.concatenate([blocks[k] for k in range(4)], axis=1).astype(bf16)


def embed(where, rows, keep, near, far, scale, gain, pieces):
    tiles, width = rows.shape
    share = far.shape[0]
    columns = pieces[0].shape[1]
    first = pl.BlockSpec((share, width), lambda i: (0, 0))
    return pl.pallas_call(
        embed_kernel,
        grid=(1,),
        in_specs=[SMEM, whole((tiles, width)), first, first, whole((share, width)), whole((1, width)), whole((1, width))]
        + [whole((width, columns))] * 4,
        out_specs=whole((share, 4 * columns)),
        out_shape=jax.ShapeDtypeStruct((share, 4 * columns), bf16),
        scratch_shapes=[pltpu.VMEM((4, share, columns), f32)],
        compiler_params=pltpu.CompilerParams(vmem_limit_bytes=VMEM_LIMIT),
        cost_estimate=pl.CostEstimate(
            flops=8 * share * width * columns, bytes_accessed=8 * width * columns, transcendentals=0
        ),
        name="embed",
    )(where, rows, keep, near, far, scale, gain, *pieces)


def loop(count, body):
    if count <= 4:
        for i in range(count):
            body(i)
    else:
        pl.loop(0, count)(body)


def attend_kernel(n, piece_count, *refs):
    where_ref = refs[0]
    pieces = refs[1 : 1 + piece_count]
    owners = refs[1 + piece_count : 1 + 2 * piece_count] if piece_count == 1 else refs[1 + piece_count : 1 + piece_count + n]
    rest = refs[1 + piece_count + len(owners) :]
    gain_ref, wq, wk, wv, att_ref, res_ref = rest[:6]
    emb, named, kall, vall, qloc, kloc, vloc, occ, cls = rest[6:15]
    scores_sc = rest[15]
    me, here = where_ref[0], where_ref[1]
    tiles = emb.shape[1]
    cap = qloc.shape[1]
    columns = wq.shape[1]
    width = emb.shape[2]
    heads = columns // HD
    slots = n * cap

    if piece_count == 1:
        source, named_of = pieces[0], owners[0]
    else:
        source, named_of = emb, named
        share = tiles // 4
        for kz in range(n):
            named[here ^ kz] = owners[kz][...]
            for km in range(4):
                at = pl.multiple_of((me ^ km) * share, share)
                emb[here ^ kz, pl.ds(at, share), :] = pieces[kz * 4 + km][...]

    earlier_of = lax.broadcasted_iota(jnp.int32, (tiles, tiles), 0) < lax.broadcasted_iota(
        jnp.int32, (tiles, tiles), 1
    )
    before = jnp.where(earlier_of, 1.0, 0.0).astype(bf16)
    mine = (
        lax.broadcasted_iota(jnp.int32, (width, columns), 0)
        == lax.broadcasted_iota(jnp.int32, (width, columns), 1) + me * columns
    )
    pick_columns = jnp.where(mine, 1.0, 0.0).astype(bf16)
    n_pad = max(n, 8)
    owner_ids = lax.broadcasted_iota(jnp.int32, (n_pad, tiles), 0)
    slot_ids = lax.broadcasted_iota(jnp.int32, (cap, tiles), 0)

    def block(b):
        owner = named_of[b]
        onehot = jnp.where(owner_ids == owner, 1.0, 0.0)
        earlier = dot(onehot.astype(bf16), before)
        arrival = jnp.sum(onehot * earlier, axis=0, keepdims=True).astype(jnp.int32)
        cls[b] = arrival & (RATE - 1)
        chosen = jnp.where((slot_ids == arrival) & (owner == here), 1.0, 0.0)
        occ[b] = jnp.broadcast_to(jnp.sum(chosen, axis=1, keepdims=True), (cap, 128)).astype(bf16)
        chosen = chosen.astype(bf16)
        rows = source[b]
        res_ref[b] = dot(chosen, dot(rows, pick_columns).astype(bf16)).astype(bf16)
        normed = layer_norm(rows.astype(f32), gain_ref[...]).astype(bf16)
        queries = dot(normed, wq[...]).astype(bf16)
        keys = dot(normed, wk[...]).astype(bf16)
        values = dot(normed, wv[...]).astype(bf16)
        kall[b] = keys
        vall[b] = values
        qloc[b] = dot(chosen, queries).astype(bf16)
        kloc[b] = dot(chosen, keys).astype(bf16)
        vloc[b] = dot(chosen, values).astype(bf16)

    loop(n, block)

    factor = HD ** (-0.5) * LOG2E
    key_local = kloc[...].reshape(slots, columns)
    value_local = vloc[...].reshape(slots, columns)
    live = dot_t(jnp.full((8, 128), 1.0, bf16), occ[...].reshape(slots, 128))[0:1, :]
    bias_local = jnp.where(live > 0.5, 0.0, MASKED)
    chunk = slots // 4
    per = min(n, 4)
    parts = n // per
    span = per * tiles
    head_of = lax.broadcasted_iota(jnp.int32, (chunk, columns), 1) // HD
    row_class = lax.broadcasted_iota(jnp.int32, (chunk, 1), 0) & (RATE - 1)
    blocks_per = max(n // 4, 1)

    for c in range(4):
        if n >= 4:
            q = qloc[c * blocks_per : (c + 1) * blocks_per].reshape(chunk, columns)
            occupied = occ[c * blocks_per : (c + 1) * blocks_per].reshape(chunk, 128)[:, 0:1]
        else:
            q = qloc[...].reshape(slots, columns)[c * chunk : (c + 1) * chunk]
            occupied = occ[...].reshape(slots, 128)[c * chunk : (c + 1) * chunk, 0:1]
        picked = jnp.where(head_of == row_class, q, jnp.zeros((), bf16))

        def classes(s):
            return jnp.concatenate([cls[s * per + i] for i in range(per)], axis=1)

        if parts == 1:
            keys = kall[...].reshape(span, columns)
            sparse = jnp.where(row_class == classes(0), dot_t(picked, keys) * factor, MASKED)
            peak_sparse = jnp.max(sparse, axis=1, keepdims=True)
            weights = jnp.exp2(sparse - peak_sparse)
            total_sparse = jnp.sum(weights, axis=1, keepdims=True)
            summed_sparse = dot(weights.astype(bf16), vall[...].reshape(span, columns))
        else:

            def first(s, peak):
                keys = kall[pl.ds(s * per, per)].reshape(span, columns)
                sparse = jnp.where(row_class == classes(s), dot_t(picked, keys) * factor, MASKED)
                scores_sc[s] = sparse
                return jnp.maximum(peak, jnp.max(sparse, axis=1, keepdims=True))

            peak_sparse = lax.fori_loop(0, parts, first, jnp.full((chunk, 1), MASKED, f32))

            def second(s, carry):
                total, summed = carry
                weights = jnp.exp2(scores_sc[s] - peak_sparse)
                values = vall[pl.ds(s * per, per)].reshape(span, columns)
                return (
                    total + jnp.sum(weights, axis=1, keepdims=True),
                    summed + dot(weights.astype(bf16), values),
                )

            total_sparse, summed_sparse = lax.fori_loop(
                0, parts, second, (jnp.zeros((chunk, 1), f32), jnp.zeros((chunk, columns), f32))
            )

        mixed = jnp.zeros((chunk, columns), f32)
        for h in range(heads):
            query = jnp.where(head_of == h, q, jnp.zeros((), bf16))
            scores = dot_t(query, key_local) * factor + bias_local
            peak = jnp.max(scores, axis=1, keepdims=True)
            weights = jnp.exp2(scores - peak)
            total = jnp.sum(weights, axis=1, keepdims=True)
            summed = dot(weights.astype(bf16), value_local)
            has = row_class == (h % RATE)
            highest = jnp.where(has, jnp.maximum(peak, peak_sparse), peak)
            first_weight = jnp.exp2(peak - highest)
            second_weight = jnp.where(has, jnp.exp2(peak_sparse - highest), 0.0)
            share_of = 1.0 / (first_weight * total + second_weight * total_sparse)
            both = (first_weight * share_of) * summed + (second_weight * share_of) * summed_sparse
            mixed = jnp.where(head_of == h, both, mixed)
        att_ref[c * chunk : (c + 1) * chunk, :] = jnp.where(occupied > 0.5, mixed, 0.0).astype(bf16)


def attend(where, pieces, owners, gain, wq, wk, wv, n, tiles):
    width, columns = wq.shape
    slots = 2 * tiles
    cap = slots // n
    per = min(n, 4)
    parts = n // per
    loose = len(pieces) > 1
    args = [where, *pieces, *owners, gain, wq, wk, wv]
    return pl.pallas_call(
        functools.partial(attend_kernel, n, len(pieces)),
        in_specs=[SMEM] + [VMEM] * (len(args) - 1),
        out_specs=[VMEM, VMEM],
        out_shape=[jax.ShapeDtypeStruct((slots, columns), bf16), jax.ShapeDtypeStruct((n, cap, columns), bf16)],
        scratch_shapes=[
            pltpu.VMEM((n if loose else 1, tiles, width), bf16),
            pltpu.VMEM((n if loose else 1, 1, tiles), jnp.int32),
            pltpu.VMEM((n, tiles, columns), bf16),
            pltpu.VMEM((n, tiles, columns), bf16),
            pltpu.VMEM((n, cap, columns), bf16),
            pltpu.VMEM((n, cap, columns), bf16),
            pltpu.VMEM((n, cap, columns), bf16),
            pltpu.VMEM((n, cap, 128), bf16),
            pltpu.VMEM((n, 1, tiles), jnp.int32),
            pltpu.VMEM((parts if parts > 1 else 1, slots // 4 if parts > 1 else 8, per * tiles), f32),
        ],
        compiler_params=pltpu.CompilerParams(vmem_limit_bytes=VMEM_LIMIT),
        cost_estimate=pl.CostEstimate(
            flops=2 * n * tiles * width * columns * 3, bytes_accessed=2 * n * tiles * width, transcendentals=slots * slots * 4
        ),
        name="attend",
    )(*args)


def output_kernel(a0, a1, a2, a3, w0, w1, w2, w3, res_ref, out_ref):
    total = dot(a0[...], w0[...]) + dot(a1[...], w1[...]) + dot(a2[...], w2[...]) + dot(a3[...], w3[...])
    out_ref[...] = (total + res_ref[...].astype(f32)).astype(bf16)


def project_out(attended, weights, residual):
    return pl.pallas_call(
        output_kernel,
        in_specs=[VMEM] * 9,
        out_specs=VMEM,
        out_shape=jax.ShapeDtypeStruct(residual.shape, bf16),
        compiler_params=pltpu.CompilerParams(vmem_limit_bytes=VMEM_LIMIT),
        name="project_out",
    )(*attended, *weights, residual)


def per_device(
    class_rows,
    destination,
    norm1_gain,
    gate_weight,
    up_weight,
    down_weight,
    layer_scale,
    norm2_gain,
    proj_weight,
    norm3_gain,
    query_weight,
    key_weight,
    value_weight,
    out_weight,
):
    tiles = class_rows.shape[0]
    n = lax.axis_size("seq")
    me = lax.axis_index("mdl")
    here = lax.axis_index("seq")
    where = jnp.stack([me, here]).astype(jnp.int32)
    columns = query_weight.shape[1]
    share = tiles // 4

    def over_mdl(value, k):
        return lax.ppermute(value, "mdl", [(i, i ^ k) for i in range(4)])

    def over_seq(value, k):
        return lax.ppermute(value, "seq", [(i, i ^ k) for i in range(n)])

    proj_far = over_mdl(proj_weight, 2)
    proj_near = over_mdl(proj_weight, 1)
    proj_cross = over_mdl(proj_far, 1)

    owner = destination.reshape(1, tiles)
    few = n <= 4
    if few:
        owners = [owner] + [over_seq(owner, k) for k in range(1, n)]
    else:
        owners = [lax.all_gather(owner, "seq", axis=0)]

    keep, send = feed_forward(
        where, class_rows, norm1_gain[None], gate_weight, up_weight, down_weight
    )
    near = over_mdl(send, 1)
    onward = (keep[share:] + near[share:].astype(f32)).astype(bf16)
    far = over_mdl(onward, 2)
    embedded = embed(
        where,
        class_rows,
        keep,
        near,
        far,
        layer_scale[None],
        norm2_gain[None],
        (proj_weight, proj_near, proj_far, proj_cross),
    )
    if few:
        pieces = []
        for k in range(n):
            own = over_seq(embedded, k) if k else embedded
            across = over_mdl(own, 2)
            pieces += [own, over_mdl(own, 1), across, over_mdl(across, 1)]
    else:
        gathered = lax.all_gather(lax.all_gather(embedded, "mdl", axis=0, tiled=True), "seq", axis=0)
        pieces = [gathered]
    attended, residual = attend(
        where, pieces, owners, norm3_gain[None], query_weight, key_weight, value_weight, n, tiles
    )
    residual = residual.reshape(attended.shape)

    def out_block(k):
        return lax.dynamic_slice_in_dim(out_weight, (me ^ k) * columns, columns, axis=1)

    out_blocks = [out_block(0)] + [over_mdl(out_block(k), k) for k in (1, 2, 3)]
    beyond = over_mdl(attended, 2)
    gathered = [attended, over_mdl(attended, 1), beyond, over_mdl(beyond, 1)]
    return project_out(gathered, out_blocks, residual)


def solution(mesh):
    return jax.shard_map(
        per_device,
        mesh=mesh,
        in_specs=(
            P(("grp", "seq"), None),
            P(("grp", "seq"), None),
            P(),
            P(None, "mdl"),
            P(None, "mdl"),
            P("mdl", None),
            P(),
            P(),
            P(None, "mdl"),
            P(),
            P(None, "mdl"),
            P(None, "mdl"),
            P(None, "mdl"),
            P("mdl", None),
        ),
        out_specs=P(("grp", "seq"), "mdl"),
        check_vma=False,
    )
```

time: 180 us -> 83.8 us (0.47)
  blocking collectives: 50.7 us -> 0 us
  local copies, waits for them, and re-layouts: 42.3 us -> 17 us
  Pallas kernels: 0 us -> 20.4 us
  matrix products: 20 us -> 0 us
  other arithmetic: 14.7 us -> 0.8 us
  between operations: 13.7 us -> 0.25 us
  starting transfers between devices: 14.4 us -> 22.4 us
    all_gather x5 -> x0, blocking collectives: 50.7 us -> none  [the longest x1 13.1 us: per_device(): piece_keys = lax.all_gather(sparse_keys, 'seq', axis=0, tiled=True)]
    ppermute x0 -> x29, starting transfers between devices: none -> 22.4 us  [the longest x23 13.5 us: over_mdl(): return lax.ppermute(value, 'mdl', [(i, i ^ k) for i in range(4)])]
    ppermute x0 -> x29, waiting for transfers between devices: none -> 22.1 us  [the longest x23 17.5 us: over_mdl(): return lax.ppermute(value, 'mdl', [(i, i ^ k) for i in range(4)])]
    pallas_call x0 -> x4, Pallas kernels: none -> 20.4 us  [the longest x1 11.2 us: attend(): pl.pallas_call(functools.partial(attend_kernel, n, len(pieces)), in_specs...]
    dot_general x11 -> x0, matrix products: 20 us -> none  [the longest x1 5.48 us: encode(): jnp.dot(hidden, down_weight, preferred_element_type=jnp.float32)]
    psum x1 -> x0, waiting for transfers between devices: 17.2 us -> none  [encode(): feedfwd = lax.psum(partial_sums, 'mdl')]
    all_to_all x3 -> x0, starting transfers between devices: 14.4 us -> none  [the longest x1 6.32 us: per_device(): lax.all_to_all(filled.reshape(seq_count, capacity), 'seq', split_axis=0,...]
    reduce_sum x11 -> x0, other arithmetic: 12 us -> none  [the longest x1 3.84 us: pick_heads(): jnp.sum(jnp.where(chosen[None, :, :, None], grouped, jnp.zeros((), groupe...]
  transfers between devices with their start and end apart: 4 -> 29, of which waited for: 3 -> 8; matrix products, arithmetic and copies ran while one was open for 12% -> 11% of each run, Pallas kernels for 0% -> 11%
where the time goes in v1:
time: 83.8 us; the launch traced here: 82.9 us
  starting transfers between devices  22.4 us (27%)
  waiting for transfers between devices  22.1 us (26%)
  Pallas kernels  20.4 us (24%)
  local copies, waits for them, and re-layouts  17 us (20%)
    ppermute x23, waiting for transfers between devices, over_mdl(): return lax.ppermute(value, 'mdl', [(i, i ^ k) for i in range(4)])  17.5 us
    ppermute x23, starting transfers between devices, over_mdl(): return lax.ppermute(value, 'mdl', [(i, i ^ k) for i in range(4)])  13.5 us
    unnamed x32, local copies, waits for them, and re-layouts  11.6 us
    pallas_call x1, Pallas kernels, attend(): pl.pallas_call(functools.partial(attend_kernel, n, len(pieces)), in_specs...  11.2 us
    ppermute x6, starting transfers between devices, over_seq(): return lax.ppermute(value, 'seq', [(i, i ^ k) for i in range(n)])  8.9 us
    pallas_call x1, Pallas kernels, feed_forward(): pl.pallas_call(ffn_kernel, grid=(steps,), in_specs=[SMEM, whole((tiles, w...  6.89 us
    ppermute x6, waiting for transfers between devices, over_seq(): return lax.ppermute(value, 'seq', [(i, i ^ k) for i in range(n)])  4.59 us
    ppermute x3, local copies, waits for them, and re-layouts, over_mdl(): return lax.ppermute(value, 'mdl', [(i, i ^ k) for i in range(4)])  2.94 us
  transfers between devices with their start and end apart: 29, of which 8 were waited for; matrix products, arithmetic and copies ran while one was open for 11% of the time, Pallas kernels for 11%

profile of v1, /device:TPU:0, one launch (start us, length us, event | category | flops | bytes accessed | tf_op | source)
XLA Modules:
  0.0 82.9 jit_solution(2507098776251089549)
XLA Ops:
  0.0 2.9 %collective-permute-start.3 = (bf16[1536,192]{0,1:T(8,128)(2,1)}, bf16[1536,192]{0,1:T(8,128)(2,1)S(1)}, u32[]{:S(2)}, u32[]{:S(2)}) collective-permute-start(bf16[1536,192]{0,1:T(8,128)(2,1)} %param.22), channel_id=1, source_target_pairs={{0,2},{1,3},{2,0},{3,1},{4,6},{5,7},{6,4},{7,5},{8,10},{9,11},{10,... | collective-permute-start | bytes 1769480 | tf_op jit(solution)/shard_map/ppermute | solution.py:357
  2.9 0.7 broadcast_in_dim.12.gain_ref
  3.6 0.1 pad_add_fusion.where_ref.refs_0_
  3.7 1.9 %copy-done = bf16[1536,1024]{1,0:T(8,128)(2,1)S(1)} copy-done((bf16[1536,1024]{1,0:T(8,128)(2,1)S(1)}, bf16[1536,1024]{1,0:T(8,128)(2,1)}, u32[]{:S(2)}) %copy-start) | copy-done | bytes 3145752
  5.6 1.1 %copy-done.1 = bf16[256,1536]{1,0:T(8,128)(2,1)S(1)} copy-done((bf16[256,1536]{1,0:T(8,128)(2,1)S(1)}, bf16[256,1536]{1,0:T(8,128)(2,1)}, u32[]{:S(2)}) %copy-start.1) | copy-done | bytes 786456
  6.8 6.9 %feed_forward.1 = (f32[128,1536]{1,0:T(8,128)S(1)}, bf16[128,1536]{1,0:T(8,128)(2,1)S(1)}) custom-call(s32[2]{0:T(128)S(1)} %pad_add_fusion.where_ref.refs_0_, bf16[256,1536]{1,0:T(8,128)(2,1)S(1)} %copy-done.1, f32[1,1536]{1,0:T(1,128)S(1)} %broadcast_in_dim.12.gain_ref, bf16[1536,1024]{1,0:T(8,128)(2,1)S(1)} %copy-done, bf16[1536,1024]{1,0:T(8,128)(2,1)} %up_ref.1, ...), custom_call_target="tpu_custom_call" | custom-call | flops 2415919104 | bytes 9437184 | tf_op jit(solution)/shard_map/feed_forward/pallas_call | solution.py:81
  13.7 0.1 collective-permute-start
  13.8 0.5 collective-permute-start.2
  14.3 2.2 %collective-permute-done.3 = bf16[1536,192]{0,1:T(8,128)(2,1)S(1)} collective-permute-done((bf16[1536,192]{0,1:T(8,128)(2,1)}, bf16[1536,192]{0,1:T(8,128)(2,1)S(1)}, u32[]{:S(2)}, u32[]{:S(2)}) %collective-permute-start.3) | collective-permute-done | bytes 589856 | tf_op jit(solution)/shard_map/ppermute | solution.py:357
  16.5 0.7 add_convert_fusion
  17.2 1.7 %collective-permute-start.1 = (bf16[64,1536]{1,0:T(8,128)(2,1)}, bf16[64,1536]{1,0:T(8,128)(2,1)}, u32[]{:S(2)}, u32[]{:S(2)}) collective-permute-start(bf16[64,1536]{1,0:T(8,128)(2,1)} %add_convert_fusion), channel_id=1, source_target_pairs={{0,2},{1,3},{2,0},{3,1},{4,6},{5,7},{6,4},{7,5},{8,10},{9,11},{10,... | collective-permute-start | bytes 589832 | tf_op jit(solution)/shard_map/ppermute | solution.py:357
  19.0 1.6 %collective-permute-start.20 = (s32[1,256]{1,0:T(1,128)}, s32[1,256]{1,0:T(1,128)}, u32[]{:S(2)}, u32[]{:S(2)}) collective-permute-start(s32[1,256]{1,0:T(1,128)} %bitcast.2.refs_17_), channel_id=1, source_target_pairs={{0,4},{4,0},{8,12},{12,8},{1,5},{5,1},{9,13},{13,9},{2,6},{6,2},{1... | collective-permute-start | bytes 3080 | tf_op jit(solution)/shard_map/ppermute | solution.py:360
  20.5 2.6 %collective-permute-start.21 = (s32[1,256]{1,0:T(1,128)}, s32[1,256]{1,0:T(1,128)}, u32[]{:S(2)}, u32[]{:S(2)}) collective-permute-start(s32[1,256]{1,0:T(1,128)} %bitcast.2.refs_17_), channel_id=1, source_target_pairs={{0,8},{4,12},{8,0},{12,4},{1,9},{5,13},{9,1},{13,5},{2,10},{6,14},... | collective-permute-start | bytes 3080 | tf_op jit(solution)/shard_map/ppermute | solution.py:360
  23.1 0.3 copy.22.p0
  23.4 0.3 copy.24.p2
  23.7 0.0 collective-permute-done.2
  23.7 0.3 collective-permute-start.22
  24.0 1.3 %copy.23.p1 = bf16[1536,192]{1,0:T(8,128)(2,1)S(1)} copy(bf16[1536,192]{0,1:T(8,128)(2,1)} %collective-permute-done.2) | data formatting | bytes 1179648 | tf_op jit(solution)/shard_map/ppermute | solution.py:357
  25.4 0.0 collective-permute-done.4
  25.4 1.3 %copy.25.p3 = bf16[1536,192]{1,0:T(8,128)(2,1)S(1)} copy(bf16[1536,192]{0,1:T(8,128)(2,1)} %collective-permute-done.4) | data formatting | bytes 1179648 | tf_op jit(solution)/shard_map/ppermute | solution.py:357
  26.7 0.0 collective-permute-done.1.far_ref
  26.7 0.0 copy-start.2
  26.7 1.1 %copy-done.2 = bf16[256,1536]{1,0:T(8,128)(2,1)S(1)} copy-done((bf16[256,1536]{1,0:T(8,128)(2,1)S(1)}, bf16[256,1536]{1,0:T(8,128)(2,1)}, u32[]{:S(2)}) %copy-start.2) | copy-done | bytes 786456
  27.9 1.1 %copy-done.4 = f32[128,1536]{1,0:T(8,128)S(1)} copy-done((f32[128,1536]{1,0:T(8,128)S(1)}, f32[128,1536]{1,0:T(8,128)}, u32[]{:S(2)}) %copy-start.4) | copy-done | bytes 786456
  29.0 0.6 copy-done.8
  29.6 1.9 %embed.1.refs_1_ = bf16[64,768]{1,0:T(8,128)(2,1)S(1)} custom-call(s32[2]{0:T(128)S(1)} %copy-done.8, bf16[256,1536]{1,0:T(8,128)(2,1)S(1)} %copy-done.2, f32[128,1536]{1,0:T(8,128)S(1)} %copy-done.4, bf16[128,1536]{1,0:T(8,128)(2,1)S(1)} %collective-permute-done.near_ref, bf16[64,1536]{1,0:T(8,128)(2,1)} %collective-permute-done.1.far_ref, ...), custom_call_target="tpu_custom_call" | custom-call | flops 150994944 | bytes 2359296 | tf_op jit(solution)/shard_map/embed/pallas_call | solution.py:123
  31.5 0.0 copy-start.11
  31.5 0.7 collective-permute-start.8
  32.2 3.5 %collective-permute-start.12 = (bf16[64,768]{1,0:T(8,128)(2,1)S(1)}, bf16[64,768]{1,0:T(8,128)(2,1)S(1)}, u32[]{:S(2)}, u32[]{:S(2)}) collective-permute-start(bf16[64,768]{1,0:T(8,128)(2,1)S(1)} %embed.1.refs_1_), channel_id=1, source_target_pairs={{0,8},{4,12},{8,0},{12,4},{1,9},{5,13},{9,1},{13,5},{2,10},{6,14},... | collective-permute-start | bytes 294920 | tf_op jit(solution)/shard_map/ppermute | solution.py:360
  35.7 0.0 collective-permute-done.20.refs_18_
  35.7 0.2 collective-permute-start.16
  36.0 0.0 collective-permute-done.21.refs_19_
  36.0 0.4 collective-permute-start.6
  36.4 0.6 copy-done.5
  37.0 0.2 collective-permute-done.8.refs_5_
  37.2 1.5 %collective-permute-start.10 = (bf16[64,768]{1,0:T(8,128)(2,1)S(1)}, bf16[64,768]{1,0:T(8,128)(2,1)S(1)}, u32[]{:S(2)}, u32[]{:S(2)}) collective-permute-start(bf16[64,768]{1,0:T(8,128)(2,1)S(1)} %collective-permute-done.8.refs_5_), channel_id=1, source_target_pairs={{0,2},{1,3},{2,0},{3,1},{4,6},{5,7},{6,4},{7,5},{8,10},{9,11},{10,... | collective-permute-start | bytes 294920 | tf_op jit(solution)/shard_map/ppermute | solution.py:357
  38.6 4.4 %collective-permute-done.12.refs_9_ = bf16[64,768]{1,0:T(8,128)(2,1)S(1)} collective-permute-done((bf16[64,768]{1,0:T(8,128)(2,1)S(1)}, bf16[64,768]{1,0:T(8,128)(2,1)S(1)}, u32[]{:S(2)}, u32[]{:S(2)}) %collective-permute-start.12) | collective-permute-done | bytes 98336 | tf_op jit(solution)/shard_map/ppermute | solution.py:360
  43.1 0.5 collective-permute-start.14
  43.6 1.5 %collective-permute-start.18 = (bf16[64,768]{1,0:T(8,128)(2,1)S(1)}, bf16[64,768]{1,0:T(8,128)(2,1)S(1)}, u32[]{:S(2)}, u32[]{:S(2)}) collective-permute-start(bf16[64,768]{1,0:T(8,128)(2,1)S(1)} %collective-permute-done.16.refs_13_), channel_id=1, source_target_pairs={{0,2},{1,3},{2,0},{3,1},{4,6},{5,7},{6,4},{7,5},{8,10},{9,11},{10,... | collective-permute-start | bytes 294920 | tf_op jit(solution)/shard_map/ppermute | solution.py:357
  45.1 0.5 collective-permute-start.17
  45.6 0.1 collective-permute-start.9
  45.7 2.0 %collective-permute-done.14.refs_11_ = bf16[64,768]{1,0:T(8,128)(2,1)S(1)} collective-permute-done((bf16[64,768]{1,0:T(8,128)(2,1)S(1)}, bf16[64,768]{1,0:T(8,128)(2,1)S(1)}, u32[]{:S(2)}, u32[]{:S(2)}) %collective-permute-start.14) | collective-permute-done | bytes 98336 | tf_op jit(solution)/shard_map/ppermute | solution.py:357
  47.7 1.0 %collective-permute-done.18.refs_15_ = bf16[64,768]{1,0:T(8,128)(2,1)S(1)} collective-permute-done((bf16[64,768]{1,0:T(8,128)(2,1)S(1)}, bf16[64,768]{1,0:T(8,128)(2,1)S(1)}, u32[]{:S(2)}, u32[]{:S(2)}) %collective-permute-start.18) | collective-permute-done | bytes 98336 | tf_op jit(solution)/shard_map/ppermute | solution.py:357
  48.7 0.5 collective-permute-start.15
  49.2 0.1 collective-permute-start.19
  49.3 1.1 %copy.26.refs_22_ = bf16[768,192]{1,0:T(8,128)(2,1)S(1)} copy(bf16[768,192]{0,1:T(8,128)(2,1)} %param.24) | data formatting | bytes 589824 | tf_op args[10]
  50.5 1.1 %copy.27.refs_23_ = bf16[768,192]{1,0:T(8,128)(2,1)S(1)} copy(bf16[768,192]{0,1:T(8,128)(2,1)} %param.25) | data formatting | bytes 589824 | tf_op args[11]
  51.6 1.1 %copy.28.refs_24_ = bf16[768,192]{1,0:T(8,128)(2,1)S(1)} copy(bf16[768,192]{0,1:T(8,128)(2,1)} %param.26) | data formatting | bytes 589824 | tf_op args[12]
  52.7 0.7 broadcast_in_dim.15.refs_21_
  53.5 0.0 copy-start.6
  53.5 0.9 %copy-done.6 = bf16[64,768]{1,0:T(8,128)(2,1)S(1)} copy-done((bf16[64,768]{1,0:T(8,128)(2,1)S(1)}, bf16[64,768]{1,0:T(8,128)(2,1)}, u32[]{:S(2)}) %copy-start.6) | copy-done | bytes 98328
  54.4 0.6 copy-done.9
  54.9 11.2 %attend.1 = (bf16[512,192]{1,0:T(8,128)(2,1)S(1)}, bf16[4,128,192]{2,1,0:T(8,128)(2,1)S(1)}) custom-call(s32[2]{0:T(128)S(1)} %copy-done.9, bf16[64,768]{1,0:T(8,128)(2,1)S(1)} %copy-done.6, bf16[64,768]{1,0:T(8,128)(2,1)S(1)} %collective-permute-done.5.refs_2_, bf16[64,768]{1,0:T(8,128)(2,1)S(1)} %collective-permute-done.6.refs_3_, ...), custom_call_target="tpu_custom_call" | custom-call | flops 905969664 | bytes 1572864 | tf_op jit(solution)/shard_map/attend/pallas_call | solution.py:291
  66.1 1.0 %collective-permute-start.24 = (bf16[512,192]{1,0:T(8,128)(2,1)S(1)}, bf16[512,192]{1,0:T(8,128)(2,1)S(1)}, u32[]{:S(2)}, u32[]{:S(2)}) collective-permute-start(bf16[512,192]{1,0:T(8,128)(2,1)S(1)} %get-tuple-element.11.a0), channel_id=1, source_target_pairs={{0,2},{1,3},{2,0},{3,1},{4,6},{5,7},{6,4},{7,5},{8,10},{9,11},{10,... | collective-permute-start | bytes 589832 | tf_op jit(solution)/shard_map/ppermute | solution.py:357
  67.2 0.2 collective-permute-start.23
  67.3 7.5 %collective-permute-done.24.a2 = bf16[512,192]{1,0:T(8,128)(2,1)S(1)} collective-permute-done((bf16[512,192]{1,0:T(8,128)(2,1)S(1)}, bf16[512,192]{1,0:T(8,128)(2,1)S(1)}, u32[]{:S(2)}, u32[]{:S(2)}) %collective-permute-start.24) | collective-permute-done | bytes 196640 | tf_op jit(solution)/shard_map/ppermute | solution.py:357
  74.8 0.2 constant_dynamic-slice_fusion
  75.0 0.6 collective-permute-start.26
  75.6 1.0 %collective-permute-start.27 = (bf16[192,192]{1,0:T(8,128)(2,1)S(1)}, bf16[192,192]{1,0:T(8,128)(2,1)S(1)}, u32[]{:S(2)}, u32[]{:S(2)}) collective-permute-start(bf16[192,192]{1,0:T(8,128)(2,1)S(1)} %get-tuple-element.16), channel_id=1, source_target_pairs={{0,2},{1,3},{2,0},{3,1},{4,6},{5,7},{6,4},{7,5},{8,10},{9,11},{10,... | collective-permute-start | bytes 221192 | tf_op jit(solution)/shard_map/ppermute | solution.py:357
  76.6 0.4 collective-permute-start.28
  77.0 4.2 %collective-permute-done.27.w2 = bf16[192,192]{1,0:T(8,128)(2,1)S(1)} collective-permute-done((bf16[192,192]{1,0:T(8,128)(2,1)S(1)}, bf16[192,192]{1,0:T(8,128)(2,1)S(1)}, u32[]{:S(2)}, u32[]{:S(2)}) %collective-permute-start.27) | collective-permute-done | bytes 73760 | tf_op jit(solution)/shard_map/ppermute | solution.py:357
  81.2 0.5 collective-permute-done.28.w3
  81.7 0.4 project_out.1
  82.1 0.8 copy.29
  (41 shorter events, 0.1 us)
Async XLA Ops:
  0.0 16.5 %collective-permute-start.3 = (bf16[1536,192]{0,1:T(8,128)(2,1)}, bf16[1536,192]{0,1:T(8,128)(2,1)S(1)}, u32[]{:S(2)}, u32[]{:S(2)}) collective-permute-start(bf16[1536,192]{0,1:T(8,128)(2,1)} %param.22), channel_id=1, source_target_pairs={{0,2},{1,3},{2,0},{3,1},{4,6},{5,7},{6,4},{7,5},{8,10},{9,11},{10,... | collective-permute-start | bytes 1769480 | tf_op jit(solution)/shard_map/ppermute | solution.py:357
  3.7 1.9 %copy-start = (bf16[1536,1024]{1,0:T(8,128)(2,1)S(1)}, bf16[1536,1024]{1,0:T(8,128)(2,1)}, u32[]{:S(2)}) copy-start(bf16[1536,1024]{1,0:T(8,128)(2,1)} %gate_ref.1) | copy-start | bytes 9437188
  5.6 1.1 %copy-start.1 = (bf16[256,1536]{1,0:T(8,128)(2,1)S(1)}, bf16[256,1536]{1,0:T(8,128)(2,1)}, u32[]{:S(2)}) copy-start(bf16[256,1536]{1,0:T(8,128)(2,1)} %rows_ref.3) | copy-start | bytes 2359300
  6.7 6.9 %copy-start.7 = (s32[2]{0:T(128)}, s32[2]{0:T(128)S(1)}, u32[]{:S(2)}) copy-start(s32[2]{0:T(128)S(1)} %pad_add_fusion.where_ref.refs_0_) | copy-start | bytes 28
  6.7 7.0 %copy-start.10 = (bf16[1536,192]{0,1:T(8,128)(2,1)S(1)}, bf16[1536,192]{0,1:T(8,128)(2,1)}, u32[]{:S(2)}) copy-start(bf16[1536,192]{0,1:T(8,128)(2,1)} %param.22) | copy-start | bytes 1769476
  6.7 16.7 %copy-start.12 = (f32[1536]{0:T(1024)S(1)}, f32[1536]{0:T(1024)}, u32[]{:S(2)}) copy-start(f32[1536]{0:T(1024)} %param.20) | copy-start | bytes 18436
  6.7 16.7 %copy-start.13 = (f32[1536]{0:T(1024)S(1)}, f32[1536]{0:T(1024)}, u32[]{:S(2)}) copy-start(f32[1536]{0:T(1024)} %param.21) | copy-start | bytes 18436
  13.7 6.9 %copy-start.3 = (f32[128,1536]{1,0:T(8,128)}, f32[128,1536]{1,0:T(8,128)S(1)}, u32[]{:S(2)}) copy-start(f32[128,1536]{1,0:T(8,128)S(1)} %get-tuple-element.9.keep_ref) | copy-start | bytes 2359300
  13.7 2.8 %collective-permute-start = (bf16[128,1536]{1,0:T(8,128)(2,1)S(1)}, bf16[128,1536]{1,0:T(8,128)(2,1)S(1)}, u32[]{:S(2)}, u32[]{:S(2)}) collective-permute-start(bf16[128,1536]{1,0:T(8,128)(2,1)S(1)} %get-tuple-element.10), channel_id=1, source_target_pairs={{0,1},{1,0},{2,3},{3,2},{4,5},{5,4},{6,7},{7,6},{8,9},{9,8},{10,11... | collective-permute-start | bytes 1179656 | tf_op jit(solution)/shard_map/ppermute | solution.py:357
  13.8 10.0 %collective-permute-start.2 = (bf16[1536,192]{0,1:T(8,128)(2,1)S(1)}, bf16[1536,192]{0,1:T(8,128)(2,1)}, u32[]{:S(2)}, u32[]{:S(2)}) collective-permute-start(bf16[1536,192]{0,1:T(8,128)(2,1)S(1)} %copy-done.10), channel_id=1, source_target_pairs={{0,1},{1,0},{2,3},{3,2},{4,5},{5,4},{6,7},{7,6},{8,9},{9,8},{10,11... | collective-permute-start | bytes 1769480 | tf_op jit(solution)/shard_map/ppermute | solution.py:357
  16.5 8.9 %collective-permute-start.4 = (bf16[1536,192]{0,1:T(8,128)(2,1)S(1)}, bf16[1536,192]{0,1:T(8,128)(2,1)}, u32[]{:S(2)}, u32[]{:S(2)}) collective-permute-start(bf16[1536,192]{0,1:T(8,128)(2,1)S(1)} %collective-permute-done.3), channel_id=1, source_target_pairs={{0,1},{1,0},{2,3},{3,2},{4,5},{5,4},{6,7},{7,6},{8,9},{9,8},{10,11... | collective-permute-start | bytes 1769480 | tf_op jit(solution)/shard_map/ppermute | solution.py:357
  17.2 9.5 %collective-permute-start.1 = (bf16[64,1536]{1,0:T(8,128)(2,1)}, bf16[64,1536]{1,0:T(8,128)(2,1)}, u32[]{:S(2)}, u32[]{:S(2)}) collective-permute-start(bf16[64,1536]{1,0:T(8,128)(2,1)} %add_convert_fusion), channel_id=1, source_target_pairs={{0,2},{1,3},{2,0},{3,1},{4,6},{5,7},{6,4},{7,5},{8,10},{9,11},{10,... | collective-permute-start | bytes 589832 | tf_op jit(solution)/shard_map/ppermute | solution.py:357
  19.0 16.8 %collective-permute-start.20 = (s32[1,256]{1,0:T(1,128)}, s32[1,256]{1,0:T(1,128)}, u32[]{:S(2)}, u32[]{:S(2)}) collective-permute-start(s32[1,256]{1,0:T(1,128)} %bitcast.2.refs_17_), channel_id=1, source_target_pairs={{0,4},{4,0},{8,12},{12,8},{1,5},{5,1},{9,13},{13,9},{2,6},{6,2},{1... | collective-permute-start | bytes 3080 | tf_op jit(solution)/shard_map/ppermute | solution.py:360
  20.5 15.4 %collective-permute-start.21 = (s32[1,256]{1,0:T(1,128)}, s32[1,256]{1,0:T(1,128)}, u32[]{:S(2)}, u32[]{:S(2)}) collective-permute-start(s32[1,256]{1,0:T(1,128)} %bitcast.2.refs_17_), channel_id=1, source_target_pairs={{0,8},{4,12},{8,0},{12,4},{1,9},{5,13},{9,1},{13,5},{2,10},{6,14},... | collective-permute-start | bytes 3080 | tf_op jit(solution)/shard_map/ppermute | solution.py:360
  23.7 12.6 %collective-permute-start.22 = (s32[1,256]{1,0:T(1,128)}, s32[1,256]{1,0:T(1,128)}, u32[]{:S(2)}, u32[]{:S(2)}) collective-permute-start(s32[1,256]{1,0:T(1,128)} %bitcast.2.refs_17_), channel_id=1, source_target_pairs={{0,12},{4,8},{8,4},{12,0},{1,13},{5,9},{9,5},{13,1},{2,14},{6,10},... | collective-permute-start | bytes 3080 | tf_op jit(solution)/shard_map/ppermute | solution.py:360
  26.7 1.1 %copy-start.2 = (bf16[256,1536]{1,0:T(8,128)(2,1)S(1)}, bf16[256,1536]{1,0:T(8,128)(2,1)}, u32[]{:S(2)}) copy-start(bf16[256,1536]{1,0:T(8,128)(2,1)} %rows_ref.3) | copy-start | bytes 2359300
  27.9 1.1 %copy-start.4 = (f32[128,1536]{1,0:T(8,128)S(1)}, f32[128,1536]{1,0:T(8,128)}, u32[]{:S(2)}) copy-start(f32[128,1536]{1,0:T(8,128)} %copy-done.3) | copy-start | bytes 2359300
  29.0 0.6 copy-start.8
  31.5 43.4 %copy-start.11 = (bf16[192,768]{1,0:T(8,128)(2,1)S(1)}, bf16[192,768]{1,0:T(8,128)(2,1)}, u32[]{:S(2)}) copy-start(bf16[192,768]{1,0:T(8,128)(2,1)} %param.27) | copy-start | bytes 884740
  31.5 5.7 %collective-permute-start.8 = (bf16[64,768]{1,0:T(8,128)(2,1)S(1)}, bf16[64,768]{1,0:T(8,128)(2,1)S(1)}, u32[]{:S(2)}, u32[]{:S(2)}) collective-permute-start(bf16[64,768]{1,0:T(8,128)(2,1)S(1)} %embed.1.refs_1_), channel_id=1, source_target_pairs={{0,4},{4,0},{8,12},{12,8},{1,5},{5,1},{9,13},{13,9},{2,6},{6,2},{1... | collective-permute-start | bytes 294920 | tf_op jit(solution)/shard_map/ppermute | solution.py:360
  32.2 10.8 %collective-permute-start.12 = (bf16[64,768]{1,0:T(8,128)(2,1)S(1)}, bf16[64,768]{1,0:T(8,128)(2,1)S(1)}, u32[]{:S(2)}, u32[]{:S(2)}) collective-permute-start(bf16[64,768]{1,0:T(8,128)(2,1)S(1)} %embed.1.refs_1_), channel_id=1, source_target_pairs={{0,8},{4,12},{8,0},{12,4},{1,9},{5,13},{9,1},{13,5},{2,10},{6,14},... | collective-permute-start | bytes 294920 | tf_op jit(solution)/shard_map/ppermute | solution.py:360
  35.7 7.9 %collective-permute-start.16 = (bf16[64,768]{1,0:T(8,128)(2,1)S(1)}, bf16[64,768]{1,0:T(8,128)(2,1)S(1)}, u32[]{:S(2)}, u32[]{:S(2)}) collective-permute-start(bf16[64,768]{1,0:T(8,128)(2,1)S(1)} %embed.1.refs_1_), channel_id=1, source_target_pairs={{0,12},{4,8},{8,4},{12,0},{1,13},{5,9},{9,5},{13,1},{2,14},{6,10},... | collective-permute-start | bytes 294920 | tf_op jit(solution)/shard_map/ppermute | solution.py:360
  36.0 9.1 %collective-permute-start.6 = (bf16[64,768]{1,0:T(8,128)(2,1)S(1)}, bf16[64,768]{1,0:T(8,128)(2,1)S(1)}, u32[]{:S(2)}, u32[]{:S(2)}) collective-permute-start(bf16[64,768]{1,0:T(8,128)(2,1)S(1)} %embed.1.refs_1_), channel_id=1, source_target_pairs={{0,2},{1,3},{2,0},{3,1},{4,6},{5,7},{6,4},{7,5},{8,10},{9,11},{10,... | collective-permute-start | bytes 294920 | tf_op jit(solution)/shard_map/ppermute | solution.py:357
  36.4 8.8 %collective-permute-start.5 = (bf16[64,768]{1,0:T(8,128)(2,1)S(1)}, bf16[64,768]{1,0:T(8,128)(2,1)S(1)}, u32[]{:S(2)}, u32[]{:S(2)}) collective-permute-start(bf16[64,768]{1,0:T(8,128)(2,1)S(1)} %embed.1.refs_1_), channel_id=1, source_target_pairs={{0,1},{1,0},{2,3},{3,2},{4,5},{5,4},{6,7},{7,6},{8,9},{9,8},{10,11... | collective-permute-start | bytes 294920 | tf_op jit(solution)/shard_map/ppermute | solution.py:357
  36.4 0.6 copy-start.5
  37.2 8.5 %collective-permute-start.10 = (bf16[64,768]{1,0:T(8,128)(2,1)S(1)}, bf16[64,768]{1,0:T(8,128)(2,1)S(1)}, u32[]{:S(2)}, u32[]{:S(2)}) collective-permute-start(bf16[64,768]{1,0:T(8,128)(2,1)S(1)} %collective-permute-done.8.refs_5_), channel_id=1, source_target_pairs={{0,2},{1,3},{2,0},{3,1},{4,6},{5,7},{6,4},{7,5},{8,10},{9,11},{10,... | collective-permute-start | bytes 294920 | tf_op jit(solution)/shard_map/ppermute | solution.py:357
  43.1 4.6 %collective-permute-start.14 = (bf16[64,768]{1,0:T(8,128)(2,1)S(1)}, bf16[64,768]{1,0:T(8,128)(2,1)S(1)}, u32[]{:S(2)}, u32[]{:S(2)}) collective-permute-start(bf16[64,768]{1,0:T(8,128)(2,1)S(1)} %collective-permute-done.12.refs_9_), channel_id=1, source_target_pairs={{0,2},{1,3},{2,0},{3,1},{4,6},{5,7},{6,4},{7,5},{8,10},{9,11},{10,... | collective-permute-start | bytes 294920 | tf_op jit(solution)/shard_map/ppermute | solution.py:357
  43.6 5.1 %collective-permute-start.18 = (bf16[64,768]{1,0:T(8,128)(2,1)S(1)}, bf16[64,768]{1,0:T(8,128)(2,1)S(1)}, u32[]{:S(2)}, u32[]{:S(2)}) collective-permute-start(bf16[64,768]{1,0:T(8,128)(2,1)S(1)} %collective-permute-done.16.refs_13_), channel_id=1, source_target_pairs={{0,2},{1,3},{2,0},{3,1},{4,6},{5,7},{6,4},{7,5},{8,10},{9,11},{10,... | collective-permute-start | bytes 294920 | tf_op jit(solution)/shard_map/ppermute | solution.py:357
  45.1 3.6 %collective-permute-start.13 = (bf16[64,768]{1,0:T(8,128)(2,1)S(1)}, bf16[64,768]{1,0:T(8,128)(2,1)S(1)}, u32[]{:S(2)}, u32[]{:S(2)}) collective-permute-start(bf16[64,768]{1,0:T(8,128)(2,1)S(1)} %collective-permute-done.12.refs_9_), channel_id=1, source_target_pairs={{0,1},{1,0},{2,3},{3,2},{4,5},{5,4},{6,7},{7,6},{8,9},{9,8},{10,11... | collective-permute-start | bytes 294920 | tf_op jit(solution)/shard_map/ppermute | solution.py:357
  45.1 4.1 %collective-permute-start.17 = (bf16[64,768]{1,0:T(8,128)(2,1)S(1)}, bf16[64,768]{1,0:T(8,128)(2,1)S(1)}, u32[]{:S(2)}, u32[]{:S(2)}) collective-permute-start(bf16[64,768]{1,0:T(8,128)(2,1)S(1)} %collective-permute-done.16.refs_13_), channel_id=1, source_target_pairs={{0,1},{1,0},{2,3},{3,2},{4,5},{5,4},{6,7},{7,6},{8,9},{9,8},{10,11... | collective-permute-start | bytes 294920 | tf_op jit(solution)/shard_map/ppermute | solution.py:357
  45.6 7.8 %collective-permute-start.9 = (bf16[64,768]{1,0:T(8,128)(2,1)S(1)}, bf16[64,768]{1,0:T(8,128)(2,1)S(1)}, u32[]{:S(2)}, u32[]{:S(2)}) collective-permute-start(bf16[64,768]{1,0:T(8,128)(2,1)S(1)} %collective-permute-done.8.refs_5_), channel_id=1, source_target_pairs={{0,1},{1,0},{2,3},{3,2},{4,5},{5,4},{6,7},{7,6},{8,9},{9,8},{10,11... | collective-permute-start | bytes 294920 | tf_op jit(solution)/shard_map/ppermute | solution.py:357
  47.7 5.7 %collective-permute-start.7 = (bf16[64,768]{1,0:T(8,128)(2,1)S(1)}, bf16[64,768]{1,0:T(8,128)(2,1)S(1)}, u32[]{:S(2)}, u32[]{:S(2)}) collective-permute-start(bf16[64,768]{1,0:T(8,128)(2,1)S(1)} %collective-permute-done.6.refs_3_), channel_id=1, source_target_pairs={{0,1},{1,0},{2,3},{3,2},{4,5},{5,4},{6,7},{7,6},{8,9},{9,8},{10,11... | collective-permute-start | bytes 294920 | tf_op jit(solution)/shard_map/ppermute | solution.py:357
  48.7 4.7 %collective-permute-start.11 = (bf16[64,768]{1,0:T(8,128)(2,1)S(1)}, bf16[64,768]{1,0:T(8,128)(2,1)S(1)}, u32[]{:S(2)}, u32[]{:S(2)}) collective-permute-start(bf16[64,768]{1,0:T(8,128)(2,1)S(1)} %collective-permute-done.10.refs_7_), channel_id=1, source_target_pairs={{0,1},{1,0},{2,3},{3,2},{4,5},{5,4},{6,7},{7,6},{8,9},{9,8},{10,11... | collective-permute-start | bytes 294920 | tf_op jit(solution)/shard_map/ppermute | solution.py:357
  48.7 4.7 %collective-permute-start.15 = (bf16[64,768]{1,0:T(8,128)(2,1)S(1)}, bf16[64,768]{1,0:T(8,128)(2,1)S(1)}, u32[]{:S(2)}, u32[]{:S(2)}) collective-permute-start(bf16[64,768]{1,0:T(8,128)(2,1)S(1)} %collective-permute-done.14.refs_11_), channel_id=1, source_target_pairs={{0,1},{1,0},{2,3},{3,2},{4,5},{5,4},{6,7},{7,6},{8,9},{9,8},{10,11... | collective-permute-start | bytes 294920 | tf_op jit(solution)/shard_map/ppermute | solution.py:357
  49.2 4.2 %collective-permute-start.19 = (bf16[64,768]{1,0:T(8,128)(2,1)S(1)}, bf16[64,768]{1,0:T(8,128)(2,1)S(1)}, u32[]{:S(2)}, u32[]{:S(2)}) collective-permute-start(bf16[64,768]{1,0:T(8,128)(2,1)S(1)} %collective-permute-done.18.refs_15_), channel_id=1, source_target_pairs={{0,1},{1,0},{2,3},{3,2},{4,5},{5,4},{6,7},{7,6},{8,9},{9,8},{10,11... | collective-permute-start | bytes 294920 | tf_op jit(solution)/shard_map/ppermute | solution.py:357
  53.5 0.9 %copy-start.6 = (bf16[64,768]{1,0:T(8,128)(2,1)S(1)}, bf16[64,768]{1,0:T(8,128)(2,1)}, u32[]{:S(2)}) copy-start(bf16[64,768]{1,0:T(8,128)(2,1)} %copy-done.5) | copy-start | bytes 294916
  54.4 0.6 copy-start.9
  66.1 8.7 %collective-permute-start.24 = (bf16[512,192]{1,0:T(8,128)(2,1)S(1)}, bf16[512,192]{1,0:T(8,128)(2,1)S(1)}, u32[]{:S(2)}, u32[]{:S(2)}) collective-permute-start(bf16[512,192]{1,0:T(8,128)(2,1)S(1)} %get-tuple-element.11.a0), channel_id=1, source_target_pairs={{0,2},{1,3},{2,0},{3,1},{4,6},{5,7},{6,4},{7,5},{8,10},{9,11},{10,... | collective-permute-start | bytes 589832 | tf_op jit(solution)/shard_map/ppermute | solution.py:357
  67.2 14.5 %collective-permute-start.23 = (bf16[512,192]{1,0:T(8,128)(2,1)S(1)}, bf16[512,192]{1,0:T(8,128)(2,1)S(1)}, u32[]{:S(2)}, u32[]{:S(2)}) collective-permute-start(bf16[512,192]{1,0:T(8,128)(2,1)S(1)} %get-tuple-element.11.a0), channel_id=1, source_target_pairs={{0,1},{1,0},{2,3},{3,2},{4,5},{5,4},{6,7},{7,6},{8,9},{9,8},{10,11... | collective-permute-start | bytes 589832 | tf_op jit(solution)/shard_map/ppermute | solution.py:357
  74.8 6.9 %collective-permute-start.25 = (bf16[512,192]{1,0:T(8,128)(2,1)S(1)}, bf16[512,192]{1,0:T(8,128)(2,1)S(1)}, u32[]{:S(2)}, u32[]{:S(2)}) collective-permute-start(bf16[512,192]{1,0:T(8,128)(2,1)S(1)} %collective-permute-done.24.a2), channel_id=1, source_target_pairs={{0,1},{1,0},{2,3},{3,2},{4,5},{5,4},{6,7},{7,6},{8,9},{9,8},{10,11... | collective-permute-start | bytes 589832 | tf_op jit(solution)/shard_map/ppermute | solution.py:357
  75.0 2.0 %collective-permute-start.26 = (bf16[192,192]{1,0:T(8,128)(2,1)S(1)}, bf16[192,192]{1,0:T(8,128)(2,1)S(1)}, u32[]{:S(2)}, u32[]{:S(2)}) collective-permute-start(bf16[192,192]{1,0:T(8,128)(2,1)S(1)} %get-tuple-element.14), channel_id=1, source_target_pairs={{0,1},{1,0},{2,3},{3,2},{4,5},{5,4},{6,7},{7,6},{8,9},{9,8},{10,11... | collective-permute-start | bytes 221192 | tf_op jit(solution)/shard_map/ppermute | solution.py:357
  75.6 5.6 %collective-permute-start.27 = (bf16[192,192]{1,0:T(8,128)(2,1)S(1)}, bf16[192,192]{1,0:T(8,128)(2,1)S(1)}, u32[]{:S(2)}, u32[]{:S(2)}) collective-permute-start(bf16[192,192]{1,0:T(8,128)(2,1)S(1)} %get-tuple-element.16), channel_id=1, source_target_pairs={{0,2},{1,3},{2,0},{3,1},{4,6},{5,7},{6,4},{7,5},{8,10},{9,11},{10,... | collective-permute-start | bytes 221192 | tf_op jit(solution)/shard_map/ppermute | solution.py:357
  76.6 5.1 %collective-permute-start.28 = (bf16[192,192]{1,0:T(8,128)(2,1)S(1)}, bf16[192,192]{1,0:T(8,128)(2,1)S(1)}, u32[]{:S(2)}, u32[]{:S(2)}) collective-permute-start(bf16[192,192]{1,0:T(8,128)(2,1)S(1)} %get-tuple-element.13), channel_id=1, source_target_pairs={{0,3},{1,2},{2,1},{3,0},{4,7},{5,6},{6,5},{7,4},{8,11},{9,10},{10,... | collective-permute-start | bytes 221192 | tf_op jit(solution)/shard_map/ppermute | solution.py:357

commit v2 on v1

v2 whole, which is shorter than its diff:
```python
import functools

import jax
import jax.numpy as jnp
from jax import lax
from jax.experimental import pallas as pl
from jax.experimental.pallas import tpu as pltpu
from jax.sharding import PartitionSpec as P

HD = 48
RATE = 4
EPSILON = 1e-06
MASKED = -1e30
MIB = 1024 * 1024
LOG2E = 1.4426950408889634

f32 = jnp.float32
bf16 = jnp.bfloat16


def layer_norm(features, norm_gain):
    middle = jnp.mean(features, axis=-1, keepdims=True)
    centred = features - middle
    spread = jnp.mean(centred * centred, axis=-1, keepdims=True)
    return centred * lax.rsqrt(spread + EPSILON) * norm_gain


def dot(a, b):
    return jnp.dot(a, b, preferred_element_type=f32)


def dot_t(a, b):
    return lax.dot_general(a, b, (((1,), (1,)), ((), ())), preferred_element_type=f32)


def whole(shape):
    return pl.BlockSpec(shape, lambda *_: (0,) * len(shape))


VMEM = pl.BlockSpec(memory_space=pltpu.VMEM)


def mdl_index():
    return lax.axis_index("mdl")


def seq_index():
    return lax.axis_index("seq")


def row(ref):
    return ref[...].reshape(1, ref.shape[0])


def ffn_kernel(steps, rows_ref, gain_ref, gate_ref, up_ref, down_ref, keep_ref, send_ref, normed, hidden):
    step = pl.program_id(0)
    me = mdl_index()
    share = rows_ref.shape[0] // 4
    chunk = gate_ref.shape[1]

    @pl.when(step == 0)
    def _():
        for place, other in enumerate((0, 2, 1, 3)):
            start = pl.multiple_of((me ^ other) * share, share)
            rows = rows_ref[pl.ds(start, share), :].astype(f32)
            normed[place * share : (place + 1) * share, :] = layer_norm(rows, row(gain_ref)).astype(bf16)

    for i in range(steps):

        @pl.when(step == i)
        def _(i=i):
            gate = dot(normed[...], gate_ref[...])
            upward = dot(normed[...], up_ref[...])
            hidden[:, i * chunk : (i + 1) * chunk] = (gate * jax.nn.sigmoid(gate) * upward).astype(bf16)

    @pl.when(step >= steps)
    def _():
        total = dot(hidden[...], down_ref[...])
        keep_ref[...] = total[: 2 * share, :]
        send_ref[...] = total[2 * share :, :].astype(bf16)


def feed_forward(rows, gain, gate_weight, up_weight, down_weight):
    tiles, width = rows.shape
    hidden = gate_weight.shape[1]
    steps, later = 4, 4
    chunk = hidden // steps
    part = width // later
    half = tiles // 2

    def early(i):
        return (0, jnp.minimum(i, steps - 1))

    def late(i):
        return (0, jnp.maximum(i - steps, 0))

    return pl.pallas_call(
        functools.partial(ffn_kernel, steps),
        grid=(steps + later,),
        in_specs=[
            whole((tiles, width)),
            whole((width,)),
            pl.BlockSpec((width, chunk), early),
            pl.BlockSpec((width, chunk), early),
            pl.BlockSpec((hidden, part), late),
        ],
        out_specs=[pl.BlockSpec((half, part), late), pl.BlockSpec((half, part), late)],
        out_shape=[jax.ShapeDtypeStruct((half, width), f32), jax.ShapeDtypeStruct((half, width), bf16)],
        scratch_shapes=[pltpu.VMEM((tiles, width), bf16), pltpu.VMEM((tiles, hidden), bf16)],
        compiler_params=pltpu.CompilerParams(vmem_limit_bytes=60 * MIB),
        cost_estimate=pl.CostEstimate(
            flops=6 * tiles * width * hidden, bytes_accessed=6 * width * hidden, transcendentals=tiles * hidden
        ),
        name="feed_forward",
    )(rows, gain, gate_weight, up_weight, down_weight)


def embed_kernel(rows_ref, keep_ref, near_ref, far_ref, scale_ref, gain_ref, p0, p1, p2, p3, out_ref, blocks):
    me = mdl_index()
    share = out_ref.shape[0]
    start = pl.multiple_of(me * share, share)
    rows = rows_ref[pl.ds(start, share), :].astype(f32)
    feedfwd = keep_ref[...] + near_ref[...].astype(f32) + far_ref[...].astype(f32)
    stream = rows + row(scale_ref) * feedfwd
    final = layer_norm(stream, row(gain_ref)).astype(bf16)
    for other, weight in enumerate((p0, p1, p2, p3)):
        blocks[me ^ other] = dot_t(final, weight[...])
    out_ref[...] = jnp.concatenate([blocks[k] for k in range(4)], axis=1).astype(bf16)


def embed(rows, keep, near, far, scale, gain, pieces):
    tiles, width = rows.shape
    share = far.shape[0]
    columns = pieces[0].shape[0]
    first = pl.BlockSpec((share, width), lambda i: (0, 0))
    return pl.pallas_call(
        embed_kernel,
        grid=(1,),
        in_specs=[whole((tiles, width)), first, first, whole((share, width)), whole((width,)), whole((width,))]
        + [whole((columns, width))] * 4,
        out_specs=whole((share, 4 * columns)),
        out_shape=jax.ShapeDtypeStruct((share, 4 * columns), bf16),
        scratch_shapes=[pltpu.VMEM((4, share, columns), f32)],
        compiler_params=pltpu.CompilerParams(vmem_limit_bytes=16 * MIB),
        cost_estimate=pl.CostEstimate(
            flops=8 * share * width * columns, bytes_accessed=8 * width * columns, transcendentals=0
        ),
        name="embed",
    )(rows, keep, near, far, scale, gain, *pieces)


LANES = 256


def prepare_kernel(loose, *refs):
    pieces = refs[:loose]
    owner_ref, gain_ref, wq, wk, wv, local_ref, all_ref, class_ref, residual_ref, block = refs[loose:]
    me, here = mdl_index(), seq_index()
    tiles, width = block.shape
    columns = wq.shape[0]
    cap = local_ref.shape[0]
    if loose > 1:
        share = tiles // 4
        for km in range(4):
            at = pl.multiple_of((me ^ km) * share, share)
            block[pl.ds(at, share), :] = pieces[km][...]
        rows = block[...]
    else:
        rows = pieces[0][...]
    owner = owner_ref[...]
    count = max(8, 2 * tiles // cap)
    onehot = jnp.where(lax.broadcasted_iota(jnp.int32, (count, tiles), 0) == owner, 1.0, 0.0)
    earlier_of = lax.broadcasted_iota(jnp.int32, (tiles, tiles), 0) < lax.broadcasted_iota(
        jnp.int32, (tiles, tiles), 1
    )
    earlier = dot(onehot.astype(bf16), jnp.where(earlier_of, 1.0, 0.0).astype(bf16))
    arrival = jnp.sum(onehot * earlier, axis=0, keepdims=True).astype(jnp.int32)
    class_ref[...] = arrival & (RATE - 1)
    slot_ids = lax.broadcasted_iota(jnp.int32, (cap, tiles), 0)
    chosen = jnp.where((slot_ids == arrival) & (owner == here), 1.0, 0.0)
    occupied = jnp.sum(chosen, axis=1, keepdims=True)
    chosen = chosen.astype(bf16)
    mine = (
        lax.broadcasted_iota(jnp.int32, (columns, width), 1)
        == lax.broadcasted_iota(jnp.int32, (columns, width), 0) + me * columns
    )
    picked = jnp.where(mine, 1.0, 0.0).astype(bf16)
    residual_ref[...] = dot_t(dot_t(picked, rows).astype(bf16), chosen).astype(bf16)
    normed = layer_norm(rows.astype(f32), row(gain_ref)).astype(bf16)
    queries = dot_t(normed, wq[...]).astype(bf16)
    keys = dot_t(normed, wk[...]).astype(bf16)
    values = dot_t(normed, wv[...]).astype(bf16)
    all_ref[:, :columns] = keys
    all_ref[:, LANES : LANES + columns] = values
    local_ref[:, :columns] = dot(chosen, queries).astype(bf16)
    local_ref[:, columns:LANES] = jnp.broadcast_to(occupied, (cap, LANES - columns)).astype(bf16)
    local_ref[:, LANES : LANES + columns] = dot(chosen, keys).astype(bf16)
    local_ref[:, 2 * LANES : 2 * LANES + columns] = dot(chosen, values).astype(bf16)


def prepare(pieces, owner, gain, weights, cap):
    columns, width = weights[0].shape
    loose = len(pieces)
    if loose > 1:
        count, tiles = 1, owner.shape[1]
        first = [whole(pieces[0].shape)] * loose + [whole((1, tiles))]
        lead, block = (), whole
    else:
        count, _, tiles = owner.shape
        lead = (count,)

        def block(shape):
            return pl.BlockSpec((None, *shape), lambda b: (b, 0, 0))

        first = [block((tiles, width)), block((1, tiles))]
    outs = [((cap, 3 * LANES), bf16), ((tiles, 2 * LANES), bf16), ((1, tiles), jnp.int32), ((columns, cap), bf16)]
    return pl.pallas_call(
        functools.partial(prepare_kernel, loose),
        grid=(count,),
        in_specs=first + [whole((width,))] + [whole((columns, width))] * 3,
        out_specs=[block(shape) for shape, _ in outs],
        out_shape=[jax.ShapeDtypeStruct(lead + shape, kind) for shape, kind in outs],
        scratch_shapes=[pltpu.VMEM((tiles, width), bf16)],
        compiler_params=pltpu.CompilerParams(vmem_limit_bytes=16 * MIB),
        cost_estimate=pl.CostEstimate(
            flops=6 * count * tiles * width * columns, bytes_accessed=6 * width * columns, transcendentals=0
        ),
        name="prepare",
    )(*pieces, owner, gain, *weights)


def attend_kernel(n, groups, columns, *refs):
    local = refs[:groups]
    every = refs[groups : 2 * groups]
    classes = refs[2 * groups : 3 * groups]
    att_ref, scores_sc = refs[3 * groups :]
    heads = columns // HD
    slots = att_ref.shape[1]
    factor = HD ** (-0.5) * LOG2E

    def taken(start, size):
        parts = [ref[..., start : start + size] for ref in local]
        parts = [part.reshape(-1, size) for part in parts]
        return parts[0] if groups == 1 else jnp.concatenate(parts, axis=0)

    q = taken(0, columns)
    key_local = taken(LANES, columns)
    value_local = taken(2 * LANES, columns)
    flags = taken(LANES - 128, 128)
    last = jnp.where(lax.broadcasted_iota(jnp.int32, (8, 128), 1) == 127, 1.0, 0.0).astype(bf16)
    live = dot_t(last, flags)[0:1, :]
    occupied = flags[:, 127:128]
    bias_local = jnp.where(live > 0.5, 0.0, MASKED)
    head_of = lax.broadcasted_iota(jnp.int32, (slots, columns), 1) // HD
    row_class = lax.broadcasted_iota(jnp.int32, (slots, 1), 0) & (RATE - 1)
    picked = jnp.where((head_of & (RATE - 1)) == row_class, q, jnp.zeros((), bf16))

    if groups > 1 or n == 1:
        class_row = jnp.concatenate([ref[...].reshape(1, -1) for ref in classes], axis=1)
        keys = jnp.concatenate([ref[..., :columns].reshape(-1, columns) for ref in every], axis=0)
        values = jnp.concatenate([ref[..., LANES : LANES + columns].reshape(-1, columns) for ref in every], axis=0)
        sparse = jnp.where(row_class == class_row, dot_t(picked, keys) * factor, MASKED)
        peak_sparse = jnp.max(sparse, axis=1, keepdims=True)
        weights = jnp.exp2(sparse - peak_sparse)
        total_sparse = jnp.sum(weights, axis=1, keepdims=True)
        summed_sparse = dot(weights.astype(bf16), values)
    else:

        def first(b, peak):
            keys = every[0][b, :, :columns]
            sparse = jnp.where(row_class == classes[0][b], dot_t(picked, keys) * factor, MASKED)
            scores_sc[b] = sparse
            return jnp.maximum(peak, jnp.max(sparse, axis=1, keepdims=True))

        peak_sparse = lax.fori_loop(0, n, first, jnp.full((slots, 1), MASKED, f32))

        def second(b, carry):
            total, summed = carry
            weights = jnp.exp2(scores_sc[b] - peak_sparse)
            values = every[0][b, :, LANES : LANES + columns]
            return total + jnp.sum(weights, axis=1, keepdims=True), summed + dot(weights.astype(bf16), values)

        total_sparse, summed_sparse = lax.fori_loop(
            0, n, second, (jnp.zeros((slots, 1), f32), jnp.zeros((slots, columns), f32))
        )

    mixed = jnp.zeros((slots, columns), f32)
    for h in range(heads):
        query = jnp.where(head_of == h, q, jnp.zeros((), bf16))
        scores = dot_t(query, key_local) * factor + bias_local
        peak = jnp.max(scores, axis=1, keepdims=True)
        weights = jnp.exp2(scores - peak)
        total = jnp.sum(weights, axis=1, keepdims=True)
        summed = dot(weights.astype(bf16), value_local)
        has = row_class == (h & (RATE - 1))
        highest = jnp.where(has, jnp.maximum(peak, peak_sparse), peak)
        first_weight = jnp.exp2(peak - highest)
        second_weight = jnp.where(has, jnp.exp2(peak_sparse - highest), 0.0)
        share_of = 1.0 / (first_weight * total + second_weight * total_sparse)
        both = (first_weight * share_of) * summed + (second_weight * share_of) * summed_sparse
        mixed = jnp.where(head_of == h, both, mixed)
    att_ref[...] = jnp.where(occupied > 0.5, mixed, 0.0).T.astype(bf16)


def attend(local, every, classes, n, slots, columns):
    groups = len(local)
    tiles = every[0].shape[-2]
    stored = (n, slots, tiles) if groups == 1 and n > 1 else (1, 8, 128)
    return pl.pallas_call(
        functools.partial(attend_kernel, n, groups, columns),
        in_specs=[VMEM] * (3 * groups),
        out_specs=VMEM,
        out_shape=jax.ShapeDtypeStruct((columns, slots), bf16),
        scratch_shapes=[pltpu.VMEM(stored, f32)],
        compiler_params=pltpu.CompilerParams(vmem_limit_bytes=(24 if n <= 4 else 48) * MIB),
        cost_estimate=pl.CostEstimate(
            flops=4 * slots * columns * (4 * slots + n * tiles),
            bytes_accessed=2 * n * tiles * columns,
            transcendentals=slots * (4 * slots + n * tiles),
        ),
        name="attend",
    )(*local, *every, *classes)


def output_kernel(groups, a0, a1, a2, a3, w0, w1, w2, w3, *refs):
    residual, out_ref = refs[:groups], refs[groups]
    here = seq_index()
    total = None
    for weight, piece in ((w0, a0), (w1, a1), (w2, a2), (w3, a3)):
        part = lax.dot_general(weight[...], piece[...], (((0,), (0,)), ((), ())), preferred_element_type=f32)
        total = part if total is None else total + part
    if groups == 1:
        out_ref[...] = (total + residual[0][...].astype(f32)).astype(bf16)
    else:
        cap = residual[0].shape[1]
        for k in range(groups):
            at = pl.multiple_of((here ^ k) * cap, cap)
            block = total[:, k * cap : (k + 1) * cap] + residual[k][...].astype(f32)
            out_ref[:, pl.ds(at, cap)] = block.astype(bf16)


def project_out(attended, weights, residual):
    return pl.pallas_call(
        functools.partial(output_kernel, len(residual)),
        in_specs=[VMEM] * (8 + len(residual)),
        out_specs=VMEM,
        out_shape=jax.ShapeDtypeStruct((weights[0].shape[1], attended[0].shape[1]), bf16),
        compiler_params=pltpu.CompilerParams(vmem_limit_bytes=16 * MIB),
        name="project_out",
    )(*attended, *weights, *residual)


def per_device(
    class_rows,
    destination,
    norm1_gain,
    gate_weight,
    up_weight,
    down_weight,
    layer_scale,
    norm2_gain,
    proj_weight,
    norm3_gain,
    query_weight,
    key_weight,
    value_weight,
    out_weight,
):
    tiles = class_rows.shape[0]
    n = lax.axis_size("seq")
    me = lax.axis_index("mdl")
    columns = query_weight.shape[1]
    share = tiles // 4
    slots = 2 * tiles
    cap = slots // n
    few = n <= 4

    def over_mdl(value, k):
        return lax.ppermute(value, "mdl", [(i, i ^ k) for i in range(4)])

    def over_seq(value, k):
        return lax.ppermute(value, "seq", [(i, i ^ k) for i in range(n)])

    proj = proj_weight.T
    proj_far = over_mdl(proj, 2)
    proj_near = over_mdl(proj, 1)
    proj_cross = over_mdl(proj_far, 1)

    owner = destination.reshape(1, tiles)
    if few:
        owners = [owner] + [over_seq(owner, k) for k in range(1, n)]
    else:
        owners = [lax.all_gather(owner, "seq", axis=0)]

    keep, send = feed_forward(class_rows, norm1_gain, gate_weight, up_weight, down_weight)
    near = over_mdl(send, 1)
    onward = (keep[share:] + near[share:].astype(f32)).astype(bf16)
    far = over_mdl(onward, 2)
    embedded = embed(
        class_rows, keep, near, far, layer_scale, norm2_gain, (proj, proj_near, proj_far, proj_cross)
    )

    out_late, _ = lax.optimization_barrier((out_weight, embedded))

    def out_block(k):
        return lax.dynamic_slice_in_dim(out_late, (me ^ k) * columns, columns, axis=1)

    out_blocks = [out_block(0)] + [over_mdl(out_block(k), k) for k in (1, 2, 3)]

    weights = (query_weight.T, key_weight.T, value_weight.T)
    if few:
        ready = []
        for k in range(n):
            own = over_seq(embedded, k) if k else embedded
            across = over_mdl(own, 2)
            pieces = [own, over_mdl(own, 1), across, over_mdl(across, 1)]
            ready.append(prepare(pieces, owners[k], norm3_gain, weights, cap))
    else:
        gathered = lax.all_gather(lax.all_gather(embedded, "mdl", axis=0, tiled=True), "seq", axis=0)
        ready = [prepare([gathered], owners[0], norm3_gain, weights, cap)]
    local, every, classes, residual = (list(items) for items in zip(*ready))
    local, out_blocks = lax.optimization_barrier((local, out_blocks))
    attended = attend(local, every, classes, n, slots, columns)
    if not few:
        residual = [residual[0].transpose(1, 0, 2).reshape(columns, slots)]

    beyond = over_mdl(attended, 2)
    gathered = [attended, over_mdl(attended, 1), beyond, over_mdl(beyond, 1)]
    return project_out(gathered, out_blocks, residual).T


def solution(mesh):
    return jax.shard_map(
        per_device,
        mesh=mesh,
        in_specs=(
            P(("grp", "seq"), None),
            P(("grp", "seq"), None),
            P(),
            P(None, "mdl"),
            P(None, "mdl"),
            P("mdl", None),
            P(),
            P(),
            P(None, "mdl"),
            P(),
            P(None, "mdl"),
            P(None, "mdl"),
            P(None, "mdl"),
            P("mdl", None),
        ),
        out_specs=P(("grp", "seq"), "mdl"),
        check_vma=False,
    )
```

time: 83.8 us -> 68.5 us (0.82)
  local copies, waits for them, and re-layouts: 17 us -> 1.36 us
  starting transfers between devices: 22.4 us -> 25 us
  waiting for transfers between devices: 22.1 us -> 20.5 us
    unnamed x32 -> x22, local copies, waits for them, and re-layouts: 11.6 us -> 1.17 us
    ppermute x3 -> x0, local copies, waits for them, and re-layouts: 2.94 us -> none  [over_mdl(): return lax.ppermute(value, 'mdl', [(i, i ^ k) for i in range(4)])]
    ppermute x23, starting transfers between devices: 13.5 us -> 15.1 us  [over_mdl(): return lax.ppermute(value, 'mdl', [(i, i ^ k) for i in range(4)])]
    broadcast_in_dim x4 -> x0, local copies, waits for them, and re-layouts: 1.41 us -> none  [the longest x1 0.7 us: per_device(): norm1_gain[None]]
    ppermute x6, starting transfers between devices: 8.9 us -> 9.88 us  [over_seq(): return lax.ppermute(value, 'seq', [(i, i ^ k) for i in range(n)])]
    ppermute x23, waiting for transfers between devices: 17.5 us -> 16.5 us  [over_mdl(): return lax.ppermute(value, 'mdl', [(i, i ^ k) for i in range(4)])]
    pallas_call x4 -> x8, Pallas kernels: 20.4 us -> 20.1 us  [the longest x1 10.1 us: feed_forward(): pl.pallas_call(functools.partial(ffn_kernel, steps), grid=(steps + later,...]
  transfers between devices with their start and end apart: 29 -> 29, of which waited for: 8 -> 9; matrix products, arithmetic and copies ran while one was open for 11% -> 2% of each run, Pallas kernels for 11% -> 23%
where the time goes in v2:
time: 68.5 us; the launch traced here: 68.2 us
  starting transfers between devices  25 us (36%)
  waiting for transfers between devices  20.5 us (30%)
  Pallas kernels  20.1 us (29%)
  local copies, waits for them, and re-layouts  1.36 us (2%)
  other arithmetic  1.03 us (2%)
    ppermute x23, waiting for transfers between devices, over_mdl(): return lax.ppermute(value, 'mdl', [(i, i ^ k) for i in range(4)])  16.5 us
    ppermute x23, starting transfers between devices, over_mdl(): return lax.ppermute(value, 'mdl', [(i, i ^ k) for i in range(4)])  15.1 us
    pallas_call x1, Pallas kernels, feed_forward(): pl.pallas_call(functools.partial(ffn_kernel, steps), grid=(steps + later,...  10.1 us
    ppermute x6, starting transfers between devices, over_seq(): return lax.ppermute(value, 'seq', [(i, i ^ k) for i in range(n)])  9.88 us
    pallas_call x4, Pallas kernels, prepare(): pl.pallas_call(functools.partial(prepare_kernel, loose), grid=(count,), i...  4.35 us
    ppermute x6, waiting for transfers between devices, over_seq(): return lax.ppermute(value, 'seq', [(i, i ^ k) for i in range(n)])  3.94 us
    pallas_call x1, Pallas kernels, attend(): pl.pallas_call(functools.partial(attend_kernel, n, groups, columns), in_s...  3.4 us
  transfers between devices with their start and end apart: 29, of which 9 were waited for; matrix products, arithmetic and copies ran while one was open for 2% of the time, Pallas kernels for 23%

profile of v2, /device:TPU:0, one launch (start us, length us, event | category | flops | bytes accessed | tf_op | source)
XLA Modules:
  0.0 68.2 jit_solution(18379102180445731524)
XLA Ops:
  0.0 3.0 %collective-permute-start.3 = (bf16[192,1536]{1,0:T(8,128)(2,1)}, bf16[192,1536]{1,0:T(8,128)(2,1)S(1)}, u32[]{:S(2)}, u32[]{:S(2)}) collective-permute-start(bf16[192,1536]{1,0:T(8,128)(2,1)} %bitcast.18), channel_id=1, source_target_pairs={{0,2},{1,3},{2,0},{3,1},{4,6},{5,7},{6,4},{7,5},{8,10},{9,11},{10,... | collective-permute-start | bytes 1769480 | tf_op jit(solution)/shard_map/ppermute | solution.py:379
  3.0 10.1 %feed_forward.1 = (f32[128,1536]{1,0:T(8,128)}, bf16[128,1536]{1,0:T(8,128)(2,1)}) custom-call(bf16[256,1536]{1,0:T(8,128)(2,1)} %rows_ref.3, f32[1536]{0:T(1024)} %gain_ref.2, bf16[1536,1024]{1,0:T(8,128)(2,1)} %gate_ref.1, bf16[1536,1024]{1,0:T(8,128)(2,1)} %up_ref.1, bf16[1024,1536]{1,0:T(8,128)(2,1)} %down_ref.1), custom_call_target="tpu_custom_call" | custom-call | flops 2415919104 | bytes 9437184 | tf_op jit(solution)/shard_map/feed_forward/pallas_call | solution.py:97
  13.1 0.0 copy-start.2
  13.1 0.1 collective-permute-start
  13.2 0.5 collective-permute-start.2
  13.7 2.8 %collective-permute-done.3.p2 = bf16[192,1536]{1,0:T(8,128)(2,1)S(1)} collective-permute-done((bf16[192,1536]{1,0:T(8,128)(2,1)}, bf16[192,1536]{1,0:T(8,128)(2,1)S(1)}, u32[]{:S(2)}, u32[]{:S(2)}) %collective-permute-start.3) | collective-permute-done | bytes 589856 | tf_op jit(solution)/shard_map/ppermute | solution.py:379
  16.6 0.0 collective-permute-start.4
  16.6 0.0 collective-permute-done.near_ref
  16.6 1.0 %add_convert_fusion = bf16[64,1536]{1,0:T(8,128)(2,1)S(1)} fusion(f32[128,1536]{1,0:T(8,128)} %get-tuple-element.32.keep_ref, bf16[128,1536]{1,0:T(8,128)(2,1)S(1)} %collective-permute-done.near_ref), kind=kLoop, calls=%fused_computation | loop fusion | flops 294912 | bytes 786432 | tf_op jit(solution)/shard_map/convert_element_type | solution.py:397
  17.6 1.8 %collective-permute-start.1 = (bf16[64,1536]{1,0:T(8,128)(2,1)S(1)}, bf16[64,1536]{1,0:T(8,128)(2,1)S(1)}, u32[]{:S(2)}, u32[]{:S(2)}) collective-permute-start(bf16[64,1536]{1,0:T(8,128)(2,1)S(1)} %add_convert_fusion), channel_id=1, source_target_pairs={{0,2},{1,3},{2,0},{3,1},{4,6},{5,7},{6,4},{7,5},{8,10},{9,11},{10,... | collective-permute-start | bytes 589832 | tf_op jit(solution)/shard_map/ppermute | solution.py:379
  19.4 3.6 %collective-permute-start.22 = (s32[1,256]{1,0:T(1,128)S(1)}, s32[1,256]{1,0:T(1,128)S(1)}, u32[]{:S(2)}, u32[]{:S(2)}) collective-permute-start(s32[1,256]{1,0:T(1,128)S(1)} %bitcast.21), channel_id=1, source_target_pairs={{0,12},{4,8},{8,4},{12,0},{1,13},{5,9},{9,5},{13,1},{2,14},{6,10},... | collective-permute-start | bytes 3080 | tf_op jit(solution)/shard_map/ppermute | solution.py:382
  23.0 0.0 collective-permute-start.17
  23.0 2.0 %collective-permute-done.1.far_ref = bf16[64,1536]{1,0:T(8,128)(2,1)S(1)} collective-permute-done((bf16[64,1536]{1,0:T(8,128)(2,1)S(1)}, bf16[64,1536]{1,0:T(8,128)(2,1)S(1)}, u32[]{:S(2)}, u32[]{:S(2)}) %collective-permute-start.1) | collective-permute-done | bytes 196640 | tf_op jit(solution)/shard_map/ppermute | solution.py:379
  25.0 1.8 %collective-permute-start.12 = (s32[1,256]{1,0:T(1,128)S(1)}, s32[1,256]{1,0:T(1,128)S(1)}, u32[]{:S(2)}, u32[]{:S(2)}) collective-permute-start(s32[1,256]{1,0:T(1,128)S(1)} %bitcast.23), channel_id=1, source_target_pairs={{0,4},{4,0},{8,12},{12,8},{1,5},{5,1},{9,13},{13,9},{2,6},{6,2},{1... | collective-permute-start | bytes 3080 | tf_op jit(solution)/shard_map/ppermute | solution.py:382
  26.8 0.0 collective-permute-done.2.p1
  26.8 0.0 collective-permute-done.4.p3
  26.9 1.1 %copy-done.4 = f32[128,1536]{1,0:T(8,128)S(1)} copy-done((f32[128,1536]{1,0:T(8,128)S(1)}, f32[128,1536]{1,0:T(8,128)}, u32[]{:S(2)}) %copy-start.4) | copy-done | bytes 786456
  28.0 1.1 %embed.1.refs_0_ = bf16[64,768]{1,0:T(8,128)(2,1)S(1)} custom-call(bf16[256,1536]{1,0:T(8,128)(2,1)S(1)} %copy-done.3, f32[128,1536]{1,0:T(8,128)S(1)} %copy-done.4, bf16[128,1536]{1,0:T(8,128)(2,1)S(1)} %collective-permute-done.near_ref, bf16[64,1536]{1,0:T(8,128)(2,1)S(1)} %collective-permute-done.1.far_ref, f32[1536]{0:T(1024)S(1)} %copy-done.7, ...), custom_call_target="tpu_custom_call" | custom-call | flops 150994944 | bytes 2359296 | tf_op jit(solution)/shard_map/embed/pallas_call | solution.py:136
  29.1 2.5 %collective-permute-start.18 = (bf16[64,768]{1,0:T(8,128)(2,1)S(1)}, bf16[64,768]{1,0:T(8,128)(2,1)S(1)}, u32[]{:S(2)}, u32[]{:S(2)}) collective-permute-start(bf16[64,768]{1,0:T(8,128)(2,1)S(1)} %embed.1.refs_0_), channel_id=1, source_target_pairs={{0,12},{4,8},{8,4},{12,0},{1,13},{5,9},{9,5},{13,1},{2,14},{6,10},... | collective-permute-start | bytes 294920 | tf_op jit(solution)/shard_map/ppermute | solution.py:382
  31.7 0.2 collective-permute-start.13
  31.9 0.0 collective-permute-done.22.refs_4_
  31.9 1.7 %collective-permute-start.8 = (bf16[64,768]{1,0:T(8,128)(2,1)S(1)}, bf16[64,768]{1,0:T(8,128)(2,1)S(1)}, u32[]{:S(2)}, u32[]{:S(2)}) collective-permute-start(bf16[64,768]{1,0:T(8,128)(2,1)S(1)} %embed.1.refs_0_), channel_id=1, source_target_pairs={{0,4},{4,0},{8,12},{12,8},{1,5},{5,1},{9,13},{13,9},{2,6},{6,2},{1... | collective-permute-start | bytes 294920 | tf_op jit(solution)/shard_map/ppermute | solution.py:382
  33.6 0.0 collective-permute-done.17.refs_4_
  33.6 1.5 %collective-permute-start.6 = (bf16[64,768]{1,0:T(8,128)(2,1)S(1)}, bf16[64,768]{1,0:T(8,128)(2,1)S(1)}, u32[]{:S(2)}, u32[]{:S(2)}) collective-permute-start(bf16[64,768]{1,0:T(8,128)(2,1)S(1)} %embed.1.refs_0_), channel_id=1, source_target_pairs={{0,2},{1,3},{2,0},{3,1},{4,6},{5,7},{6,4},{7,5},{8,10},{9,11},{10,... | collective-permute-start | bytes 294920 | tf_op jit(solution)/shard_map/ppermute | solution.py:379
  35.1 0.0 collective-permute-done.12.refs_4_
  35.1 0.0 collective-permute-start.5
  35.1 1.6 %collective-permute-done.18.refs_0_ = bf16[64,768]{1,0:T(8,128)(2,1)S(1)} collective-permute-done((bf16[64,768]{1,0:T(8,128)(2,1)S(1)}, bf16[64,768]{1,0:T(8,128)(2,1)S(1)}, u32[]{:S(2)}, u32[]{:S(2)}) %collective-permute-start.18) | collective-permute-done | bytes 98336 | tf_op jit(solution)/shard_map/ppermute | solution.py:382
  36.7 1.5 %collective-permute-start.20 = (bf16[64,768]{1,0:T(8,128)(2,1)S(1)}, bf16[64,768]{1,0:T(8,128)(2,1)S(1)}, u32[]{:S(2)}, u32[]{:S(2)}) collective-permute-start(bf16[64,768]{1,0:T(8,128)(2,1)S(1)} %collective-permute-done.18.refs_0_), channel_id=1, source_target_pairs={{0,2},{1,3},{2,0},{3,1},{4,6},{5,7},{6,4},{7,5},{8,10},{9,11},{10,... | collective-permute-start | bytes 294920 | tf_op jit(solution)/shard_map/ppermute | solution.py:379
  38.2 2.4 %collective-permute-done.13.refs_0_ = bf16[64,768]{1,0:T(8,128)(2,1)S(1)} collective-permute-done((bf16[64,768]{1,0:T(8,128)(2,1)S(1)}, bf16[64,768]{1,0:T(8,128)(2,1)S(1)}, u32[]{:S(2)}, u32[]{:S(2)}) %collective-permute-start.13) | collective-permute-done | bytes 98336 | tf_op jit(solution)/shard_map/ppermute | solution.py:382
  40.5 0.0 collective-permute-start.19
  40.5 0.0 collective-permute-done.8.refs_0_
  40.5 1.5 %collective-permute-start.15 = (bf16[64,768]{1,0:T(8,128)(2,1)S(1)}, bf16[64,768]{1,0:T(8,128)(2,1)S(1)}, u32[]{:S(2)}, u32[]{:S(2)}) collective-permute-start(bf16[64,768]{1,0:T(8,128)(2,1)S(1)} %collective-permute-done.13.refs_0_), channel_id=1, source_target_pairs={{0,2},{1,3},{2,0},{3,1},{4,6},{5,7},{6,4},{7,5},{8,10},{9,11},{10,... | collective-permute-start | bytes 294920 | tf_op jit(solution)/shard_map/ppermute | solution.py:379
  42.0 0.0 collective-permute-done.6.refs_2_
  42.0 0.2 collective-permute-start.14
  42.2 0.0 collective-permute-done.5.refs_1_
  42.2 0.5 collective-permute-start.10
  42.8 0.0 collective-permute-done.20.refs_2_
  42.8 0.0 collective-permute-start.9
  42.8 0.0 collective-permute-done.19.refs_1_
  42.8 0.5 collective-permute-start.7
  43.3 2.8 %collective-permute-done.15.refs_2_ = bf16[64,768]{1,0:T(8,128)(2,1)S(1)} collective-permute-done((bf16[64,768]{1,0:T(8,128)(2,1)S(1)}, bf16[64,768]{1,0:T(8,128)(2,1)S(1)}, u32[]{:S(2)}, u32[]{:S(2)}) %collective-permute-start.15) | collective-permute-done | bytes 98336 | tf_op jit(solution)/shard_map/ppermute | solution.py:379
  46.1 0.0 collective-permute-start.21
  46.1 0.0 collective-permute-done.14.refs_1_
  46.1 0.5 collective-permute-start.16
  46.6 1.2 %collective-permute-done.10.refs_2_ = bf16[64,768]{1,0:T(8,128)(2,1)S(1)} collective-permute-done((bf16[64,768]{1,0:T(8,128)(2,1)S(1)}, bf16[64,768]{1,0:T(8,128)(2,1)S(1)}, u32[]{:S(2)}, u32[]{:S(2)}) %collective-permute-start.10) | collective-permute-done | bytes 98336 | tf_op jit(solution)/shard_map/ppermute | solution.py:379
  47.8 0.0 collective-permute-start.11
  47.8 0.2 constant_dynamic-slice_fusion
  48.0 0.0 collective-permute-done.7.refs_3_
  48.0 0.6 collective-permute-start.23
  48.6 0.0 collective-permute-done.21.refs_3_
  48.6 1.5 %collective-permute-start.24 = (bf16[192,192]{1,0:T(8,128)(2,1)S(1)}, bf16[192,192]{1,0:T(8,128)(2,1)S(1)}, u32[]{:S(2)}, u32[]{:S(2)}) collective-permute-start(bf16[192,192]{1,0:T(8,128)(2,1)S(1)} %get-tuple-element.60), channel_id=1, source_target_pairs={{0,2},{1,3},{2,0},{3,1},{4,6},{5,7},{6,4},{7,5},{8,10},{9,11},{10,... | collective-permute-start | bytes 221192 | tf_op jit(solution)/shard_map/ppermute | solution.py:379
  50.1 0.0 collective-permute-done.16.refs_3_
  50.2 1.1 %prepare.4 = (bf16[128,768]{1,0:T(8,128)(2,1)S(1)}, bf16[256,512]{1,0:T(8,128)(2,1)S(1)}, s32[1,256]{1,0:T(1,128)S(1)}, bf16[192,128]{1,0:T(8,128)(2,1)S(1)}) custom-call(bf16[64,768]{1,0:T(8,128)(2,1)S(1)} %embed.1.refs_0_, bf16[64,768]{1,0:T(8,128)(2,1)S(1)} %collective-permute-done.5.refs_1_, bf16[64,768]{1,0:T(8,128)(2,1)S(1)} %collective-permute-done.6.refs_2_, ...), custom_call_target="tpu_custom_call" | custom-call | flops 226492416 | bytes 884736 | tf_op jit(solution)/shard_map/prepare/pallas_call | solution.py:217
  51.3 1.1 %prepare.7 = (bf16[128,768]{1,0:T(8,128)(2,1)S(1)}, bf16[256,512]{1,0:T(8,128)(2,1)S(1)}, s32[1,256]{1,0:T(1,128)S(1)}, bf16[192,128]{1,0:T(8,128)(2,1)S(1)}) custom-call(bf16[64,768]{1,0:T(8,128)(2,1)S(1)} %collective-permute-done.18.refs_0_, bf16[64,768]{1,0:T(8,128)(2,1)S(1)} %collective-permute-done.19.refs_1_, ...), custom_call_target="tpu_custom_call" | custom-call | flops 226492416 | bytes 884736 | tf_op jit(solution)/shard_map/prepare/pallas_call | solution.py:217
  52.4 1.1 %prepare.6 = (bf16[128,768]{1,0:T(8,128)(2,1)S(1)}, bf16[256,512]{1,0:T(8,128)(2,1)S(1)}, s32[1,256]{1,0:T(1,128)S(1)}, bf16[192,128]{1,0:T(8,128)(2,1)S(1)}) custom-call(bf16[64,768]{1,0:T(8,128)(2,1)S(1)} %collective-permute-done.13.refs_0_, bf16[64,768]{1,0:T(8,128)(2,1)S(1)} %collective-permute-done.14.refs_1_, ...), custom_call_target="tpu_custom_call" | custom-call | flops 226492416 | bytes 884736 | tf_op jit(solution)/shard_map/prepare/pallas_call | solution.py:217
  53.5 0.0 collective-permute-done.11.refs_3_
  53.5 1.1 %prepare.5 = (bf16[128,768]{1,0:T(8,128)(2,1)S(1)}, bf16[256,512]{1,0:T(8,128)(2,1)S(1)}, s32[1,256]{1,0:T(1,128)S(1)}, bf16[192,128]{1,0:T(8,128)(2,1)S(1)}) custom-call(bf16[64,768]{1,0:T(8,128)(2,1)S(1)} %collective-permute-done.8.refs_0_, bf16[64,768]{1,0:T(8,128)(2,1)S(1)} %collective-permute-done.9.refs_1_, ...), custom_call_target="tpu_custom_call" | custom-call | flops 226492416 | bytes 884736 | tf_op jit(solution)/shard_map/prepare/pallas_call | solution.py:217
  54.6 0.6 collective-permute-done.25.w3
  55.2 3.4 %attend.1.a0 = bf16[192,512]{1,0:T(8,128)(2,1)S(1)} custom-call(bf16[128,768]{1,0:T(8,128)(2,1)S(1)} %get-tuple-element.39.refs_0_, bf16[128,768]{1,0:T(8,128)(2,1)S(1)} %get-tuple-element.40.refs_1_, bf16[128,768]{1,0:T(8,128)(2,1)S(1)} %get-tuple-element.41.refs_2_, bf16[128,768]{1,0:T(8,128)(2,1)S(1)} %get-tuple-element.42.refs_3_, ...), custom_call_target="tpu_custom_call" | custom-call | flops 1207959552 | bytes 393216 | tf_op jit(solution)/shard_map/attend/pallas_call | solution.py:309
  58.6 1.0 %collective-permute-start.27 = (bf16[192,512]{1,0:T(8,128)(2,1)S(1)}, bf16[192,512]{1,0:T(8,128)(2,1)S(1)}, u32[]{:S(2)}, u32[]{:S(2)}) collective-permute-start(bf16[192,512]{1,0:T(8,128)(2,1)S(1)} %attend.1.a0), channel_id=1, source_target_pairs={{0,2},{1,3},{2,0},{3,1},{4,6},{5,7},{6,4},{7,5},{8,10},{9,11},{10,... | collective-permute-start | bytes 589832 | tf_op jit(solution)/shard_map/ppermute | solution.py:379
  59.6 0.4 collective-permute-start.26
  60.0 5.6 %collective-permute-done.27.a2 = bf16[192,512]{1,0:T(8,128)(2,1)S(1)} collective-permute-done((bf16[192,512]{1,0:T(8,128)(2,1)S(1)}, bf16[192,512]{1,0:T(8,128)(2,1)S(1)}, u32[]{:S(2)}, u32[]{:S(2)}) %collective-permute-start.27) | collective-permute-done | bytes 196640 | tf_op jit(solution)/shard_map/ppermute | solution.py:379
  65.6 1.4 %collective-permute-done.28.a3 = bf16[192,512]{1,0:T(8,128)(2,1)S(1)} collective-permute-done((bf16[192,512]{1,0:T(8,128)(2,1)S(1)}, bf16[192,512]{1,0:T(8,128)(2,1)S(1)}, u32[]{:S(2)}, u32[]{:S(2)}) %collective-permute-start.28) | collective-permute-done | bytes 196640 | tf_op jit(solution)/shard_map/ppermute | solution.py:379
  67.1 1.1 %project_out.1 = bf16[192,512]{1,0:T(8,128)(2,1)} custom-call(bf16[192,512]{1,0:T(8,128)(2,1)S(1)} %attend.1.a0, bf16[192,512]{1,0:T(8,128)(2,1)S(1)} %collective-permute-done.26.a1, bf16[192,512]{1,0:T(8,128)(2,1)S(1)} %collective-permute-done.27.a2, bf16[192,512]{1,0:T(8,128)(2,1)S(1)} %collective-permute-done.28.a3, ...), custom_call_target="tpu_custom_call" | custom-call | tf_op jit(solution)/shard_map/project_out/pallas_call | solution.py:343
  (26 shorter events, 0.1 us)
Async XLA Ops:
  0.0 13.2 %copy-start.5 = (bf16[1536,192]{0,1:T(8,128)(2,1)S(1)}, bf16[1536,192]{0,1:T(8,128)(2,1)}, u32[]{:S(2)}) copy-start(bf16[1536,192]{0,1:T(8,128)(2,1)} %param.22) | copy-start | bytes 1769476
  0.0 19.4 %copy-start.9 = (s32[256,1]{0,1:T(1,128)S(1)}, s32[256,1]{0,1:T(1,128)}, u32[]{:S(2)}) copy-start(s32[256,1]{0,1:T(1,128)} %param.15) | copy-start | bytes 3076
  0.0 26.8 %copy-start.3 = (bf16[256,1536]{1,0:T(8,128)(2,1)S(1)}, bf16[256,1536]{1,0:T(8,128)(2,1)}, u32[]{:S(2)}) copy-start(bf16[256,1536]{1,0:T(8,128)(2,1)} %rows_ref.3) | copy-start | bytes 2359300
  0.0 26.8 %copy-start.7 = (f32[1536]{0:T(1024)S(1)}, f32[1536]{0:T(1024)}, u32[]{:S(2)}) copy-start(f32[1536]{0:T(1024)} %scale_ref.1) | copy-start | bytes 18436
  0.0 26.8 %copy-start.8 = (f32[1536]{0:T(1024)S(1)}, f32[1536]{0:T(1024)}, u32[]{:S(2)}) copy-start(f32[1536]{0:T(1024)} %gain_ref.3) | copy-start | bytes 18436
  0.0 16.6 %collective-permute-start.3 = (bf16[192,1536]{1,0:T(8,128)(2,1)}, bf16[192,1536]{1,0:T(8,128)(2,1)S(1)}, u32[]{:S(2)}, u32[]{:S(2)}) collective-permute-start(bf16[192,1536]{1,0:T(8,128)(2,1)} %bitcast.18), channel_id=1, source_target_pairs={{0,2},{1,3},{2,0},{3,1},{4,6},{5,7},{6,4},{7,5},{8,10},{9,11},{10,... | collective-permute-start | bytes 1769480 | tf_op jit(solution)/shard_map/ppermute | solution.py:379
  3.0 44.8 %copy-start.10 = (bf16[192,768]{1,0:T(8,128)(2,1)S(1)}, bf16[192,768]{1,0:T(8,128)(2,1)}, u32[]{:S(2)}) copy-start(bf16[192,768]{1,0:T(8,128)(2,1)} %param.27) | copy-start | bytes 884740
  3.0 47.1 %copy-start.6 = (f32[768]{0:T(1024)S(1)}, f32[768]{0:T(1024)}, u32[]{:S(2)}) copy-start(f32[768]{0:T(1024)} %refs_5_.7) | copy-start | bytes 9220
  13.1 37.0 %copy-start = (bf16[768,192]{0,1:T(8,128)(2,1)S(1)}, bf16[768,192]{0,1:T(8,128)(2,1)}, u32[]{:S(2)}) copy-start(bf16[768,192]{0,1:T(8,128)(2,1)} %param.24) | copy-start | bytes 884740
  13.1 37.0 %copy-start.1 = (bf16[768,192]{0,1:T(8,128)(2,1)S(1)}, bf16[768,192]{0,1:T(8,128)(2,1)}, u32[]{:S(2)}) copy-start(bf16[768,192]{0,1:T(8,128)(2,1)} %param.25) | copy-start | bytes 884740
  13.1 37.0 %copy-start.2 = (bf16[768,192]{0,1:T(8,128)(2,1)S(1)}, bf16[768,192]{0,1:T(8,128)(2,1)}, u32[]{:S(2)}) copy-start(bf16[768,192]{0,1:T(8,128)(2,1)} %param.26) | copy-start | bytes 884740
  13.1 3.4 %collective-permute-start = (bf16[128,1536]{1,0:T(8,128)(2,1)}, bf16[128,1536]{1,0:T(8,128)(2,1)S(1)}, u32[]{:S(2)}, u32[]{:S(2)}) collective-permute-start(bf16[128,1536]{1,0:T(8,128)(2,1)} %get-tuple-element.33), channel_id=1, source_target_pairs={{0,1},{1,0},{2,3},{3,2},{4,5},{5,4},{6,7},{7,6},{8,9},{9,8},{10,11... | collective-permute-start | bytes 1179656 | tf_op jit(solution)/shard_map/ppermute | solution.py:379
  13.2 13.6 %collective-permute-start.2 = (bf16[192,1536]{1,0:T(8,128)(2,1)S(1)}, bf16[192,1536]{1,0:T(8,128)(2,1)S(1)}, u32[]{:S(2)}, u32[]{:S(2)}) collective-permute-start(bf16[192,1536]{1,0:T(8,128)(2,1)S(1)} %bitcast.19), channel_id=1, source_target_pairs={{0,1},{1,0},{2,3},{3,2},{4,5},{5,4},{6,7},{7,6},{8,9},{9,8},{10,11... | collective-permute-start | bytes 1769480 | tf_op jit(solution)/shard_map/ppermute | solution.py:379
  16.6 10.3 %collective-permute-start.4 = (bf16[192,1536]{1,0:T(8,128)(2,1)S(1)}, bf16[192,1536]{1,0:T(8,128)(2,1)S(1)}, u32[]{:S(2)}, u32[]{:S(2)}) collective-permute-start(bf16[192,1536]{1,0:T(8,128)(2,1)S(1)} %collective-permute-done.3.p2), channel_id=1, source_target_pairs={{0,1},{1,0},{2,3},{3,2},{4,5},{5,4},{6,7},{7,6},{8,9},{9,8},{10,11... | collective-permute-start | bytes 1769480 | tf_op jit(solution)/shard_map/ppermute | solution.py:379
  17.6 7.4 %collective-permute-start.1 = (bf16[64,1536]{1,0:T(8,128)(2,1)S(1)}, bf16[64,1536]{1,0:T(8,128)(2,1)S(1)}, u32[]{:S(2)}, u32[]{:S(2)}) collective-permute-start(bf16[64,1536]{1,0:T(8,128)(2,1)S(1)} %add_convert_fusion), channel_id=1, source_target_pairs={{0,2},{1,3},{2,0},{3,1},{4,6},{5,7},{6,4},{7,5},{8,10},{9,11},{10,... | collective-permute-start | bytes 589832 | tf_op jit(solution)/shard_map/ppermute | solution.py:379
  19.4 12.4 %collective-permute-start.22 = (s32[1,256]{1,0:T(1,128)S(1)}, s32[1,256]{1,0:T(1,128)S(1)}, u32[]{:S(2)}, u32[]{:S(2)}) collective-permute-start(s32[1,256]{1,0:T(1,128)S(1)} %bitcast.21), channel_id=1, source_target_pairs={{0,12},{4,8},{8,4},{12,0},{1,13},{5,9},{9,5},{13,1},{2,14},{6,10},... | collective-permute-start | bytes 3080 | tf_op jit(solution)/shard_map/ppermute | solution.py:382
  23.0 10.6 %collective-permute-start.17 = (s32[1,256]{1,0:T(1,128)S(1)}, s32[1,256]{1,0:T(1,128)S(1)}, u32[]{:S(2)}, u32[]{:S(2)}) collective-permute-start(s32[1,256]{1,0:T(1,128)S(1)} %bitcast.22), channel_id=1, source_target_pairs={{0,8},{4,12},{8,0},{12,4},{1,9},{5,13},{9,1},{13,5},{2,10},{6,14},... | collective-permute-start | bytes 3080 | tf_op jit(solution)/shard_map/ppermute | solution.py:382
  25.0 10.1 %collective-permute-start.12 = (s32[1,256]{1,0:T(1,128)S(1)}, s32[1,256]{1,0:T(1,128)S(1)}, u32[]{:S(2)}, u32[]{:S(2)}) collective-permute-start(s32[1,256]{1,0:T(1,128)S(1)} %bitcast.23), channel_id=1, source_target_pairs={{0,4},{4,0},{8,12},{12,8},{1,5},{5,1},{9,13},{13,9},{2,6},{6,2},{1... | collective-permute-start | bytes 3080 | tf_op jit(solution)/shard_map/ppermute | solution.py:382
  26.9 1.1 %copy-start.4 = (f32[128,1536]{1,0:T(8,128)S(1)}, f32[128,1536]{1,0:T(8,128)}, u32[]{:S(2)}) copy-start(f32[128,1536]{1,0:T(8,128)} %get-tuple-element.32.keep_ref) | copy-start | bytes 2359300
  29.1 7.5 %collective-permute-start.18 = (bf16[64,768]{1,0:T(8,128)(2,1)S(1)}, bf16[64,768]{1,0:T(8,128)(2,1)S(1)}, u32[]{:S(2)}, u32[]{:S(2)}) collective-permute-start(bf16[64,768]{1,0:T(8,128)(2,1)S(1)} %embed.1.refs_0_), channel_id=1, source_target_pairs={{0,12},{4,8},{8,4},{12,0},{1,13},{5,9},{9,5},{13,1},{2,14},{6,10},... | collective-permute-start | bytes 294920 | tf_op jit(solution)/shard_map/ppermute | solution.py:382
  31.7 8.8 %collective-permute-start.13 = (bf16[64,768]{1,0:T(8,128)(2,1)S(1)}, bf16[64,768]{1,0:T(8,128)(2,1)S(1)}, u32[]{:S(2)}, u32[]{:S(2)}) collective-permute-start(bf16[64,768]{1,0:T(8,128)(2,1)S(1)} %embed.1.refs_0_), channel_id=1, source_target_pairs={{0,8},{4,12},{8,0},{12,4},{1,9},{5,13},{9,1},{13,5},{2,10},{6,14},... | collective-permute-start | bytes 294920 | tf_op jit(solution)/shard_map/ppermute | solution.py:382
  31.9 8.6 %collective-permute-start.8 = (bf16[64,768]{1,0:T(8,128)(2,1)S(1)}, bf16[64,768]{1,0:T(8,128)(2,1)S(1)}, u32[]{:S(2)}, u32[]{:S(2)}) collective-permute-start(bf16[64,768]{1,0:T(8,128)(2,1)S(1)} %embed.1.refs_0_), channel_id=1, source_target_pairs={{0,4},{4,0},{8,12},{12,8},{1,5},{5,1},{9,13},{13,9},{2,6},{6,2},{1... | collective-permute-start | bytes 294920 | tf_op jit(solution)/shard_map/ppermute | solution.py:382
  33.6 8.4 %collective-permute-start.6 = (bf16[64,768]{1,0:T(8,128)(2,1)S(1)}, bf16[64,768]{1,0:T(8,128)(2,1)S(1)}, u32[]{:S(2)}, u32[]{:S(2)}) collective-permute-start(bf16[64,768]{1,0:T(8,128)(2,1)S(1)} %embed.1.refs_0_), channel_id=1, source_target_pairs={{0,2},{1,3},{2,0},{3,1},{4,6},{5,7},{6,4},{7,5},{8,10},{9,11},{10,... | collective-permute-start | bytes 294920 | tf_op jit(solution)/shard_map/ppermute | solution.py:379
  35.1 7.2 %collective-permute-start.5 = (bf16[64,768]{1,0:T(8,128)(2,1)S(1)}, bf16[64,768]{1,0:T(8,128)(2,1)S(1)}, u32[]{:S(2)}, u32[]{:S(2)}) collective-permute-start(bf16[64,768]{1,0:T(8,128)(2,1)S(1)} %embed.1.refs_0_), channel_id=1, source_target_pairs={{0,1},{1,0},{2,3},{3,2},{4,5},{5,4},{6,7},{7,6},{8,9},{9,8},{10,11... | collective-permute-start | bytes 294920 | tf_op jit(solution)/shard_map/ppermute | solution.py:379
  36.7 6.1 %collective-permute-start.20 = (bf16[64,768]{1,0:T(8,128)(2,1)S(1)}, bf16[64,768]{1,0:T(8,128)(2,1)S(1)}, u32[]{:S(2)}, u32[]{:S(2)}) collective-permute-start(bf16[64,768]{1,0:T(8,128)(2,1)S(1)} %collective-permute-done.18.refs_0_), channel_id=1, source_target_pairs={{0,2},{1,3},{2,0},{3,1},{4,6},{5,7},{6,4},{7,5},{8,10},{9,11},{10,... | collective-permute-start | bytes 294920 | tf_op jit(solution)/shard_map/ppermute | solution.py:379
  40.5 2.3 %collective-permute-start.19 = (bf16[64,768]{1,0:T(8,128)(2,1)S(1)}, bf16[64,768]{1,0:T(8,128)(2,1)S(1)}, u32[]{:S(2)}, u32[]{:S(2)}) collective-permute-start(bf16[64,768]{1,0:T(8,128)(2,1)S(1)} %collective-permute-done.18.refs_0_), channel_id=1, source_target_pairs={{0,1},{1,0},{2,3},{3,2},{4,5},{5,4},{6,7},{7,6},{8,9},{9,8},{10,11... | collective-permute-start | bytes 294920 | tf_op jit(solution)/shard_map/ppermute | solution.py:379
  40.5 5.6 %collective-permute-start.15 = (bf16[64,768]{1,0:T(8,128)(2,1)S(1)}, bf16[64,768]{1,0:T(8,128)(2,1)S(1)}, u32[]{:S(2)}, u32[]{:S(2)}) collective-permute-start(bf16[64,768]{1,0:T(8,128)(2,1)S(1)} %collective-permute-done.13.refs_0_), channel_id=1, source_target_pairs={{0,2},{1,3},{2,0},{3,1},{4,6},{5,7},{6,4},{7,5},{8,10},{9,11},{10,... | collective-permute-start | bytes 294920 | tf_op jit(solution)/shard_map/ppermute | solution.py:379
  42.0 4.1 %collective-permute-start.14 = (bf16[64,768]{1,0:T(8,128)(2,1)S(1)}, bf16[64,768]{1,0:T(8,128)(2,1)S(1)}, u32[]{:S(2)}, u32[]{:S(2)}) collective-permute-start(bf16[64,768]{1,0:T(8,128)(2,1)S(1)} %collective-permute-done.13.refs_0_), channel_id=1, source_target_pairs={{0,1},{1,0},{2,3},{3,2},{4,5},{5,4},{6,7},{7,6},{8,9},{9,8},{10,11... | collective-permute-start | bytes 294920 | tf_op jit(solution)/shard_map/ppermute | solution.py:379
  42.2 5.6 %collective-permute-start.10 = (bf16[64,768]{1,0:T(8,128)(2,1)S(1)}, bf16[64,768]{1,0:T(8,128)(2,1)S(1)}, u32[]{:S(2)}, u32[]{:S(2)}) collective-permute-start(bf16[64,768]{1,0:T(8,128)(2,1)S(1)} %collective-permute-done.8.refs_0_), channel_id=1, source_target_pairs={{0,2},{1,3},{2,0},{3,1},{4,6},{5,7},{6,4},{7,5},{8,10},{9,11},{10,... | collective-permute-start | bytes 294920 | tf_op jit(solution)/shard_map/ppermute | solution.py:379
  42.8 10.7 %collective-permute-start.9 = (bf16[64,768]{1,0:T(8,128)(2,1)S(1)}, bf16[64,768]{1,0:T(8,128)(2,1)S(1)}, u32[]{:S(2)}, u32[]{:S(2)}) collective-permute-start(bf16[64,768]{1,0:T(8,128)(2,1)S(1)} %collective-permute-done.8.refs_0_), channel_id=1, source_target_pairs={{0,1},{1,0},{2,3},{3,2},{4,5},{5,4},{6,7},{7,6},{8,9},{9,8},{10,11... | collective-permute-start | bytes 294920 | tf_op jit(solution)/shard_map/ppermute | solution.py:379
  42.8 5.3 %collective-permute-start.7 = (bf16[64,768]{1,0:T(8,128)(2,1)S(1)}, bf16[64,768]{1,0:T(8,128)(2,1)S(1)}, u32[]{:S(2)}, u32[]{:S(2)}) collective-permute-start(bf16[64,768]{1,0:T(8,128)(2,1)S(1)} %collective-permute-done.6.refs_2_), channel_id=1, source_target_pairs={{0,1},{1,0},{2,3},{3,2},{4,5},{5,4},{6,7},{7,6},{8,9},{9,8},{10,11... | collective-permute-start | bytes 294920 | tf_op jit(solution)/shard_map/ppermute | solution.py:379
  46.1 2.5 %collective-permute-start.21 = (bf16[64,768]{1,0:T(8,128)(2,1)S(1)}, bf16[64,768]{1,0:T(8,128)(2,1)S(1)}, u32[]{:S(2)}, u32[]{:S(2)}) collective-permute-start(bf16[64,768]{1,0:T(8,128)(2,1)S(1)} %collective-permute-done.20.refs_2_), channel_id=1, source_target_pairs={{0,1},{1,0},{2,3},{3,2},{4,5},{5,4},{6,7},{7,6},{8,9},{9,8},{10,11... | collective-permute-start | bytes 294920 | tf_op jit(solution)/shard_map/ppermute | solution.py:379
  46.1 4.0 %collective-permute-start.16 = (bf16[64,768]{1,0:T(8,128)(2,1)S(1)}, bf16[64,768]{1,0:T(8,128)(2,1)S(1)}, u32[]{:S(2)}, u32[]{:S(2)}) collective-permute-start(bf16[64,768]{1,0:T(8,128)(2,1)S(1)} %collective-permute-done.15.refs_2_), channel_id=1, source_target_pairs={{0,1},{1,0},{2,3},{3,2},{4,5},{5,4},{6,7},{7,6},{8,9},{9,8},{10,11... | collective-permute-start | bytes 294920 | tf_op jit(solution)/shard_map/ppermute | solution.py:379
  47.8 5.6 %collective-permute-start.11 = (bf16[64,768]{1,0:T(8,128)(2,1)S(1)}, bf16[64,768]{1,0:T(8,128)(2,1)S(1)}, u32[]{:S(2)}, u32[]{:S(2)}) collective-permute-start(bf16[64,768]{1,0:T(8,128)(2,1)S(1)} %collective-permute-done.10.refs_2_), channel_id=1, source_target_pairs={{0,1},{1,0},{2,3},{3,2},{4,5},{5,4},{6,7},{7,6},{8,9},{9,8},{10,11... | collective-permute-start | bytes 294920 | tf_op jit(solution)/shard_map/ppermute | solution.py:379
  48.0 6.5 %collective-permute-start.23 = (bf16[192,192]{1,0:T(8,128)(2,1)S(1)}, bf16[192,192]{1,0:T(8,128)(2,1)S(1)}, u32[]{:S(2)}, u32[]{:S(2)}) collective-permute-start(bf16[192,192]{1,0:T(8,128)(2,1)S(1)} %get-tuple-element.61), channel_id=1, source_target_pairs={{0,1},{1,0},{2,3},{3,2},{4,5},{5,4},{6,7},{7,6},{8,9},{9,8},{10,11... | collective-permute-start | bytes 221192 | tf_op jit(solution)/shard_map/ppermute | solution.py:379
  48.6 6.0 %collective-permute-start.24 = (bf16[192,192]{1,0:T(8,128)(2,1)S(1)}, bf16[192,192]{1,0:T(8,128)(2,1)S(1)}, u32[]{:S(2)}, u32[]{:S(2)}) collective-permute-start(bf16[192,192]{1,0:T(8,128)(2,1)S(1)} %get-tuple-element.60), channel_id=1, source_target_pairs={{0,2},{1,3},{2,0},{3,1},{4,6},{5,7},{6,4},{7,5},{8,10},{9,11},{10,... | collective-permute-start | bytes 221192 | tf_op jit(solution)/shard_map/ppermute | solution.py:379
  50.1 5.1 %collective-permute-start.25 = (bf16[192,192]{1,0:T(8,128)(2,1)S(1)}, bf16[192,192]{1,0:T(8,128)(2,1)S(1)}, u32[]{:S(2)}, u32[]{:S(2)}) collective-permute-start(bf16[192,192]{1,0:T(8,128)(2,1)S(1)} %get-tuple-element.59), channel_id=1, source_target_pairs={{0,3},{1,2},{2,1},{3,0},{4,7},{5,6},{6,5},{7,4},{8,11},{9,10},{10,... | collective-permute-start | bytes 221192 | tf_op jit(solution)/shard_map/ppermute | solution.py:379
  58.6 7.0 %collective-permute-start.27 = (bf16[192,512]{1,0:T(8,128)(2,1)S(1)}, bf16[192,512]{1,0:T(8,128)(2,1)S(1)}, u32[]{:S(2)}, u32[]{:S(2)}) collective-permute-start(bf16[192,512]{1,0:T(8,128)(2,1)S(1)} %attend.1.a0), channel_id=1, source_target_pairs={{0,2},{1,3},{2,0},{3,1},{4,6},{5,7},{6,4},{7,5},{8,10},{9,11},{10,... | collective-permute-start | bytes 589832 | tf_op jit(solution)/shard_map/ppermute | solution.py:379
  59.6 6.0 %collective-permute-start.26 = (bf16[192,512]{1,0:T(8,128)(2,1)S(1)}, bf16[192,512]{1,0:T(8,128)(2,1)S(1)}, u32[]{:S(2)}, u32[]{:S(2)}) collective-permute-start(bf16[192,512]{1,0:T(8,128)(2,1)S(1)} %attend.1.a0), channel_id=1, source_target_pairs={{0,1},{1,0},{2,3},{3,2},{4,5},{5,4},{6,7},{7,6},{8,9},{9,8},{10,11... | collective-permute-start | bytes 589832 | tf_op jit(solution)/shard_map/ppermute | solution.py:379
  65.6 1.4 %collective-permute-start.28 = (bf16[192,512]{1,0:T(8,128)(2,1)S(1)}, bf16[192,512]{1,0:T(8,128)(2,1)S(1)}, u32[]{:S(2)}, u32[]{:S(2)}) collective-permute-start(bf16[192,512]{1,0:T(8,128)(2,1)S(1)} %collective-permute-done.27.a2), channel_id=1, source_target_pairs={{0,1},{1,0},{2,3},{3,2},{4,5},{5,4},{6,7},{7,6},{8,9},{9,8},{10,11... | collective-permute-start | bytes 589832 | tf_op jit(solution)/shard_map/ppermute | solution.py:379

commit v3 on v2

--- a/solution.py
+++ b/solution.py
@@ -52,61 +52,50 @@
     return ref[...].reshape(1, ref.shape[0])
 
 
-def ffn_kernel(steps, rows_ref, gain_ref, gate_ref, up_ref, down_ref, keep_ref, send_ref, normed, hidden):
-    step = pl.program_id(0)
+def ffn_kernel(
+    rows_ref, gain_ref, gate_ref, up_ref, down_ref, keep_ref, send_ref,
+    rows, gate, upward, down, normed, hidden, sems,
+):
     me = mdl_index()
-    share = rows_ref.shape[0] // 4
-    chunk = gate_ref.shape[1]
-
-    @pl.when(step == 0)
-    def _():
-        for place, other in enumerate((0, 2, 1, 3)):
-            start = pl.multiple_of((me ^ other) * share, share)
-            rows = rows_ref[pl.ds(start, share), :].astype(f32)
-            normed[place * share : (place + 1) * share, :] = layer_norm(rows, row(gain_ref)).astype(bf16)
-
-    for i in range(steps):
-
-        @pl.when(step == i)
-        def _(i=i):
-            gate = dot(normed[...], gate_ref[...])
-            upward = dot(normed[...], up_ref[...])
-            hidden[:, i * chunk : (i + 1) * chunk] = (gate * jax.nn.sigmoid(gate) * upward).astype(bf16)
-
-    @pl.when(step >= steps)
-    def _():
-        total = dot(hidden[...], down_ref[...])
-        keep_ref[...] = total[: 2 * share, :]
-        send_ref[...] = total[2 * share :, :].astype(bf16)
+    half = keep_ref.shape[0]
+    pairs = ((rows_ref, rows), (gate_ref, gate), (up_ref, upward), (down_ref, down))
+    copies = [pltpu.make_async_copy(source, target, sems.at[i]) for i, (source, target) in enumerate(pairs)]
+    for copy in copies:
+        copy.start()
+    copies[0].wait()
+    for place in range(2):
+        start = pl.multiple_of(((me & 1) ^ place) * half, half)
+        part = rows[pl.ds(start, half), :].astype(f32)
+        normed[place * half : (place + 1) * half, :] = layer_norm(part, row(gain_ref)).astype(bf16)
+    copies[1].wait()
+    opened = dot(normed[...], gate[...])
+    opened = opened * jax.nn.sigmoid(opened)
+    copies[2].wait()
+    hidden[...] = (opened * dot(normed[...], upward[...])).astype(bf16)
+    copies[3].wait()
+    send_ref[...] = dot(hidden[half:, :], down[...]).astype(bf16)
+    keep_ref[...] = dot(hidden[:half, :], down[...])
 
 
 def feed_forward(rows, gain, gate_weight, up_weight, down_weight):
     tiles, width = rows.shape
     hidden = gate_weight.shape[1]
-    steps, later = 4, 4
-    chunk = hidden // steps
-    part = width // later
     half = tiles // 2
-
-    def early(i):
-        return (0, jnp.minimum(i, steps - 1))
-
-    def late(i):
-        return (0, jnp.maximum(i - steps, 0))
-
+    far = pl.BlockSpec(memory_space=pltpu.HBM)
     return pl.pallas_call(
-        functools.partial(ffn_kernel, steps),
-        grid=(steps + later,),
-        in_specs=[
-            whole((tiles, width)),
-            whole((width,)),
-            pl.BlockSpec((width, chunk), early),
-            pl.BlockSpec((width, chunk), early),
-            pl.BlockSpec((hidden, part), late),
+        ffn_kernel,
+        in_specs=[far, VMEM, far, far, far],
+        out_specs=[VMEM, VMEM],
+        out_shape=[jax.ShapeDtypeStruct((half, width), f32), jax.ShapeDtypeStruct((half, width), bf16)],
+        scratch_shapes=[
+            pltpu.VMEM((tiles, width), bf16),
+            pltpu.VMEM((width, hidden), bf16),
+            pltpu.VMEM((width, hidden), bf16),
+            pltpu.VMEM((hidden, width), bf16),
+            pltpu.VMEM((tiles, width), bf16),
+            pltpu.VMEM((tiles, hidden), bf16),
+            pltpu.SemaphoreType.DMA((4,)),
         ],
-        out_specs=[pl.BlockSpec((half, part), late), pl.BlockSpec((half, part), late)],
-        out_shape=[jax.ShapeDtypeStruct((half, width), f32), jax.ShapeDtypeStruct((half, width), bf16)],
-        scratch_shapes=[pltpu.VMEM((tiles, width), bf16), pltpu.VMEM((tiles, hidden), bf16)],
         compiler_params=pltpu.CompilerParams(vmem_limit_bytes=60 * MIB),
         cost_estimate=pl.CostEstimate(
             flops=6 * tiles * width * hidden, bytes_accessed=6 * width * hidden, transcendentals=tiles * hidden
@@ -115,38 +104,34 @@
     )(rows, gain, gate_weight, up_weight, down_weight)
 
 
-def embed_kernel(rows_ref, keep_ref, near_ref, far_ref, scale_ref, gain_ref, p0, p1, p2, p3, out_ref, blocks):
-    me = mdl_index()
-    share = out_ref.shape[0]
-    start = pl.multiple_of(me * share, share)
-    rows = rows_ref[pl.ds(start, share), :].astype(f32)
-    feedfwd = keep_ref[...] + near_ref[...].astype(f32) + far_ref[...].astype(f32)
+def embed_kernel(rows_ref, here_ref, far_ref, scale_ref, gain_ref, own, near, out_ref, blocks):
+    core = mdl_index() & 1
+    half = here_ref.shape[0]
+    start = pl.multiple_of(core * half, half)
+    rows = rows_ref[pl.ds(start, half), :].astype(f32)
+    feedfwd = here_ref[...].astype(f32) + far_ref[...].astype(f32)
     stream = rows + row(scale_ref) * feedfwd
     final = layer_norm(stream, row(gain_ref)).astype(bf16)
-    for other, weight in enumerate((p0, p1, p2, p3)):
-        blocks[me ^ other] = dot_t(final, weight[...])
-    out_ref[...] = jnp.concatenate([blocks[k] for k in range(4)], axis=1).astype(bf16)
-
-
-def embed(rows, keep, near, far, scale, gain, pieces):
-    tiles, width = rows.shape
-    share = far.shape[0]
-    columns = pieces[0].shape[0]
-    first = pl.BlockSpec((share, width), lambda i: (0, 0))
+    blocks[core] = dot_t(final, own[...])
+    blocks[core ^ 1] = dot_t(final, near[...])
+    out_ref[...] = jnp.concatenate([blocks[0], blocks[1]], axis=1).astype(bf16)
+
+
+def embed(rows, here, far, scale, gain, own, near):
+    half, width = here.shape
+    columns = own.shape[0]
     return pl.pallas_call(
         embed_kernel,
-        grid=(1,),
-        in_specs=[whole((tiles, width)), first, first, whole((share, width)), whole((width,)), whole((width,))]
-        + [whole((columns, width))] * 4,
-        out_specs=whole((share, 4 * columns)),
-        out_shape=jax.ShapeDtypeStruct((share, 4 * columns), bf16),
-        scratch_shapes=[pltpu.VMEM((4, share, columns), f32)],
+        in_specs=[VMEM] * 7,
+        out_specs=VMEM,
+        out_shape=jax.ShapeDtypeStruct((half, 2 * columns), bf16),
+        scratch_shapes=[pltpu.VMEM((2, half, columns), f32)],
         compiler_params=pltpu.CompilerParams(vmem_limit_bytes=16 * MIB),
         cost_estimate=pl.CostEstimate(
-            flops=8 * share * width * columns, bytes_accessed=8 * width * columns, transcendentals=0
+            flops=4 * half * width * columns, bytes_accessed=4 * width * columns, transcendentals=0
         ),
         name="embed",
-    )(rows, keep, near, far, scale, gain, *pieces)
+    )(rows, here, far, scale, gain, own, near)
 
 
 LANES = 256
@@ -160,10 +145,11 @@
     columns = wq.shape[0]
     cap = local_ref.shape[0]
     if loose > 1:
-        share = tiles // 4
+        half, side = tiles // 2, width // 2
         for km in range(4):
-            at = pl.multiple_of((me ^ km) * share, share)
-            block[pl.ds(at, share), :] = pieces[km][...]
+            at = pl.multiple_of(((me ^ km) & 1) * half, half)
+            over = pl.multiple_of(((me ^ km) >> 1) * side, side)
+            block[pl.ds(at, half), pl.ds(over, side)] = pieces[km][...]
         rows = block[...]
     else:
         rows = pieces[0][...]
@@ -370,7 +356,6 @@
     n = lax.axis_size("seq")
     me = lax.axis_index("mdl")
     columns = query_weight.shape[1]
-    share = tiles // 4
     slots = 2 * tiles
     cap = slots // n
     few = n <= 4
@@ -381,43 +366,56 @@
     def over_seq(value, k):
         return lax.ppermute(value, "seq", [(i, i ^ k) for i in range(n)])
 
+    def after(value, *earlier):
+        return lax.optimization_barrier((value, *earlier))[0]
+
     proj = proj_weight.T
-    proj_far = over_mdl(proj, 2)
-    proj_near = over_mdl(proj, 1)
-    proj_cross = over_mdl(proj_far, 1)
-
-    owner = destination.reshape(1, tiles)
+    keep, send = feed_forward(class_rows, norm1_gain, gate_weight, up_weight, down_weight)
+    near = over_mdl(send, 1)
+    summed = (keep + near.astype(f32)).astype(bf16)
+    far = over_mdl(summed, 2)
+    proj_near = over_mdl(after(proj, summed), 1)
+    owner = after(destination, summed).reshape(1, tiles)
     if few:
         owners = [owner] + [over_seq(owner, k) for k in range(1, n)]
     else:
         owners = [lax.all_gather(owner, "seq", axis=0)]
-
-    keep, send = feed_forward(class_rows, norm1_gain, gate_weight, up_weight, down_weight)
-    near = over_mdl(send, 1)
-    onward = (keep[share:] + near[share:].astype(f32)).astype(bf16)
-    far = over_mdl(onward, 2)
     embedded = embed(
-        class_rows, keep, near, far, layer_scale, norm2_gain, (proj, proj_near, proj_far, proj_cross)
+        class_rows, summed, after(far, *owners), layer_scale, norm2_gain, proj, proj_near
     )
-
-    out_late, _ = lax.optimization_barrier((out_weight, embedded))
-
-    def out_block(k):
-        return lax.dynamic_slice_in_dim(out_late, (me ^ k) * columns, columns, axis=1)
-
-    out_blocks = [out_block(0)] + [over_mdl(out_block(k), k) for k in (1, 2, 3)]
 
     weights = (query_weight.T, key_weight.T, value_weight.T)
     if few:
-        ready = []
+        ready, acrosses = [], []
         for k in range(n):
             own = over_seq(embedded, k) if k else embedded
+            if k == 2:
+                own = after(own, ready[0][0])
             across = over_mdl(own, 2)
+            if k == 3:
+                across = after(across, ready[1][0])
+            acrosses.append(across)
             pieces = [own, over_mdl(own, 1), across, over_mdl(across, 1)]
             ready.append(prepare(pieces, owners[k], norm3_gain, weights, cap))
-    else:
-        gathered = lax.all_gather(lax.all_gather(embedded, "mdl", axis=0, tiled=True), "seq", axis=0)
+        out_late = after(out_weight, acrosses[0])
+    else:
+        sides = lax.all_gather(embedded, "mdl", axis=0).reshape(2, 2, tiles // 2, -1)
+        block = sides.transpose(1, 2, 0, 3).reshape(tiles, -1)
+        gathered = lax.all_gather(block, "seq", axis=0)
         ready = [prepare([gathered], owners[0], norm3_gain, weights, cap)]
+        out_late = after(out_weight, embedded)
+
+    def columns_of(value, k):
+        return lax.dynamic_slice_in_dim(value, k * columns, columns, axis=1)
+
+    paired = lax.dynamic_slice_in_dim(out_late, (me ^ 2) // 2 * (2 * columns), 2 * columns, axis=1)
+    out_far = over_mdl(paired, 2)
+    out_blocks = [
+        columns_of(out_late, me),
+        over_mdl(columns_of(out_late, me ^ 1), 1),
+        columns_of(out_far, me % 2),
+        over_mdl(columns_of(out_far, (me ^ 1) % 2), 1),
+    ]
     local, every, classes, residual = (list(items) for items in zip(*ready))
     local, out_blocks = lax.optimization_barrier((local, out_blocks))
     attended = attend(local, every, classes, n, slots, columns)

time: 68.5 us -> 60.5 us (0.88)
  starting transfers between devices: 25 us -> 20.1 us
  Pallas kernels: 20.1 us -> 16.6 us
  waiting for transfers between devices: 20.5 us -> 21.6 us
  local copies, waits for them, and re-layouts: 1.36 us -> 0.32 us
    ppermute x6, waiting for transfers between devices: 3.94 us -> 7.65 us  [over_seq(): return lax.ppermute(value, 'seq', [(i, i ^ k) for i in range(n)])]
    ppermute x23 -> x21, starting transfers between devices: 15.1 us -> 11.5 us  [over_mdl(): return lax.ppermute(value, 'mdl', [(i, i ^ k) for i in range(4)])]
    pallas_call x2, Pallas kernels: 11.2 us -> 7.73 us  [the longest x1 6.84 us: feed_forward(): pl.pallas_call(ffn_kernel, in_specs=[far, VMEM, far, far, far], out_specs...]
    ppermute x23 -> x21, waiting for transfers between devices: 16.5 us -> 13.9 us  [over_mdl(): return lax.ppermute(value, 'mdl', [(i, i ^ k) for i in range(4)])]
    ppermute x6, starting transfers between devices: 9.88 us -> 8.56 us  [over_seq(): return lax.ppermute(value, 'seq', [(i, i ^ k) for i in range(n)])]
    unnamed x22 -> x20, local copies, waits for them, and re-layouts: 1.17 us -> 0.05 us
  transfers between devices with their start and end apart: 29 -> 27, of which waited for: 9 -> 10; matrix products, arithmetic and copies ran while one was open for 2% -> 0% of each run, Pallas kernels for 23% -> 7%
where the time goes in v3:
time: 60.5 us; the launch traced here: 60 us
  waiting for transfers between devices  21.6 us (36%)
  starting transfers between devices  20.1 us (33%)
  Pallas kernels  16.6 us (27%)
  other arithmetic  1.2 us (2%)
    ppermute x21, waiting for transfers between devices, over_mdl(): return lax.ppermute(value, 'mdl', [(i, i ^ k) for i in range(4)])  13.9 us
    ppermute x21, starting transfers between devices, over_mdl(): return lax.ppermute(value, 'mdl', [(i, i ^ k) for i in range(4)])  11.5 us
    ppermute x6, starting transfers between devices, over_seq(): return lax.ppermute(value, 'seq', [(i, i ^ k) for i in range(n)])  8.56 us
    ppermute x6, waiting for transfers between devices, over_seq(): return lax.ppermute(value, 'seq', [(i, i ^ k) for i in range(n)])  7.65 us
    pallas_call x1, Pallas kernels, feed_forward(): pl.pallas_call(ffn_kernel, in_specs=[far, VMEM, far, far, far], out_specs...  6.84 us
    pallas_call x4, Pallas kernels, prepare(): pl.pallas_call(functools.partial(prepare_kernel, loose), grid=(count,), i...  4.4 us
    pallas_call x1, Pallas kernels, attend(): pl.pallas_call(functools.partial(attend_kernel, n, groups, columns), in_s...  3.4 us
  transfers between devices with their start and end apart: 27, of which 10 were waited for; matrix products, arithmetic and copies ran while one was open for 0% of the time, Pallas kernels for 7%

profile of v3, /device:TPU:0, one launch (start us, length us, event | category | flops | bytes accessed | tf_op | source)
XLA Modules:
  0.0 60.0 jit_solution(13002537150530613532)
XLA Ops:
  0.0 6.8 %feed_forward.1 = (f32[128,1536]{1,0:T(8,128)}, bf16[128,1536]{1,0:T(8,128)(2,1)}) custom-call(bf16[256,1536]{1,0:T(8,128)(2,1)} %rows_ref.3, f32[1536]{0:T(1024)} %gain_ref.2, bf16[1536,1024]{1,0:T(8,128)(2,1)} %gate_ref.1, bf16[1536,1024]{1,0:T(8,128)(2,1)} %up_ref.1, bf16[1024,1536]{1,0:T(8,128)(2,1)} %down_ref.1), custom_call_target="tpu_custom_call" | custom-call | flops 2415919104 | bytes 9437184 | tf_op jit(solution)/shard_map/feed_forward/pallas_call | solution.py:85
  6.9 0.0 copy-start.9
  6.9 0.0 copy-start
  6.9 0.0 copy-start.1
  6.9 0.0 copy-start.2
  6.9 0.0 copy-start.5
  6.9 0.5 collective-permute-start
  7.5 1.6 %collective-permute-done = bf16[128,1536]{1,0:T(8,128)(2,1)S(1)} collective-permute-done((bf16[128,1536]{1,0:T(8,128)(2,1)}, bf16[128,1536]{1,0:T(8,128)(2,1)S(1)}, u32[]{:S(2)}, u32[]{:S(2)}) %collective-permute-start) | collective-permute-done | bytes 393248 | tf_op jit(solution)/shard_map/ppermute | solution.py:364
  9.0 1.2 %add_convert_fusion.here_ref = bf16[128,1536]{1,0:T(8,128)(2,1)S(1)} fusion(f32[128,1536]{1,0:T(8,128)} %get-tuple-element.37, bf16[128,1536]{1,0:T(8,128)(2,1)S(1)} %collective-permute-done), kind=kLoop, calls=%fused_computation | loop fusion | flops 589824 | bytes 1572864 | tf_op jit(solution)/shard_map/convert_element_type | solution.py:375
  10.2 0.4 collective-permute-start.5
  10.7 2.6 %collective-permute-start.1 = (bf16[128,1536]{1,0:T(8,128)(2,1)S(1)}, bf16[128,1536]{1,0:T(8,128)(2,1)S(1)}, u32[]{:S(2)}, u32[]{:S(2)}) collective-permute-start(bf16[128,1536]{1,0:T(8,128)(2,1)S(1)} %add_convert_fusion.here_ref), channel_id=1, source_target_pairs={{0,2},{1,3},{2,0},{3,1},{4,6},{5,7},{6,4},{7,5},{8,10},{9,11},{10,... | collective-permute-start | bytes 1179656 | tf_op jit(solution)/shard_map/ppermute | solution.py:364
  13.3 3.6 %collective-permute-start.4 = (s32[1,256]{1,0:T(1,128)S(1)}, s32[1,256]{1,0:T(1,128)S(1)}, u32[]{:S(2)}, u32[]{:S(2)}) collective-permute-start(s32[1,256]{1,0:T(1,128)S(1)} %bitcast.20), channel_id=1, source_target_pairs={{0,12},{4,8},{8,4},{12,0},{1,13},{5,9},{9,5},{13,1},{2,14},{6,10},... | collective-permute-start | bytes 3080 | tf_op jit(solution)/shard_map/ppermute | solution.py:367
  16.9 0.0 collective-permute-start.3
  16.9 0.8 %collective-permute-start.2 = (s32[1,256]{1,0:T(1,128)S(1)}, s32[1,256]{1,0:T(1,128)S(1)}, u32[]{:S(2)}, u32[]{:S(2)}) collective-permute-start(s32[1,256]{1,0:T(1,128)S(1)} %bitcast.22), channel_id=1, source_target_pairs={{0,4},{4,0},{8,12},{12,8},{1,5},{5,1},{9,13},{13,9},{2,6},{6,2},{1... | collective-permute-start | bytes 3080 | tf_op jit(solution)/shard_map/ppermute | solution.py:367
  17.7 1.0 %collective-permute-done.4.refs_4_ = s32[1,256]{1,0:T(1,128)S(1)} collective-permute-done((s32[1,256]{1,0:T(1,128)S(1)}, s32[1,256]{1,0:T(1,128)S(1)}, u32[]{:S(2)}, u32[]{:S(2)}) %collective-permute-start.4) | collective-permute-done | bytes 1056 | tf_op jit(solution)/shard_map/ppermute | solution.py:367
  18.7 2.7 %collective-permute-done.3.refs_4_ = s32[1,256]{1,0:T(1,128)S(1)} collective-permute-done((s32[1,256]{1,0:T(1,128)S(1)}, s32[1,256]{1,0:T(1,128)S(1)}, u32[]{:S(2)}, u32[]{:S(2)}) %collective-permute-start.3) | collective-permute-done | bytes 1056 | tf_op jit(solution)/shard_map/ppermute | solution.py:367
  21.4 0.0 collective-permute-done.2.refs_4_
  21.4 1.6 %collective-permute-done.1.far_ref = bf16[128,1536]{1,0:T(8,128)(2,1)S(1)} collective-permute-done((bf16[128,1536]{1,0:T(8,128)(2,1)S(1)}, bf16[128,1536]{1,0:T(8,128)(2,1)S(1)}, u32[]{:S(2)}, u32[]{:S(2)}) %collective-permute-start.1) | collective-permute-done | bytes 393248 | tf_op jit(solution)/shard_map/ppermute | solution.py:364
  22.9 0.0 collective-permute-done.5.near
  23.0 0.9 %embed.1.refs_0_ = bf16[128,384]{1,0:T(8,128)(2,1)S(1)} custom-call(bf16[256,1536]{1,0:T(8,128)(2,1)S(1)} %copy-done.3, bf16[128,1536]{1,0:T(8,128)(2,1)S(1)} %add_convert_fusion.here_ref, bf16[128,1536]{1,0:T(8,128)(2,1)S(1)} %collective-permute-done.1.far_ref, f32[1536]{0:T(1024)S(1)} %copy-done.6, f32[1536]{0:T(1024)S(1)} %copy-done.7, ...), custom_call_target="tpu_custom_call" | custom-call | flops 150994944 | bytes 1179648 | tf_op jit(solution)/shard_map/embed/pallas_call | solution.py:123
  23.9 1.8 %collective-permute-start.7 = (bf16[128,384]{1,0:T(8,128)(2,1)S(1)}, bf16[128,384]{1,0:T(8,128)(2,1)S(1)}, u32[]{:S(2)}, u32[]{:S(2)}) collective-permute-start(bf16[128,384]{1,0:T(8,128)(2,1)S(1)} %embed.1.refs_0_), channel_id=1, source_target_pairs={{0,2},{1,3},{2,0},{3,1},{4,6},{5,7},{6,4},{7,5},{8,10},{9,11},{10,... | collective-permute-start | bytes 294920 | tf_op jit(solution)/shard_map/ppermute | solution.py:364
  25.7 1.6 %collective-permute-start.9 = (bf16[128,384]{1,0:T(8,128)(2,1)S(1)}, bf16[128,384]{1,0:T(8,128)(2,1)S(1)}, u32[]{:S(2)}, u32[]{:S(2)}) collective-permute-start(bf16[128,384]{1,0:T(8,128)(2,1)S(1)} %embed.1.refs_0_), channel_id=1, source_target_pairs={{0,4},{4,0},{8,12},{12,8},{1,5},{5,1},{9,13},{13,9},{2,6},{6,2},{1... | collective-permute-start | bytes 294920 | tf_op jit(solution)/shard_map/ppermute | solution.py:367
  27.3 2.5 %collective-permute-start.17 = (bf16[128,384]{1,0:T(8,128)(2,1)S(1)}, bf16[128,384]{1,0:T(8,128)(2,1)S(1)}, u32[]{:S(2)}, u32[]{:S(2)}) collective-permute-start(bf16[128,384]{1,0:T(8,128)(2,1)S(1)} %embed.1.refs_0_), channel_id=1, source_target_pairs={{0,12},{4,8},{8,4},{12,0},{1,13},{5,9},{9,5},{13,1},{2,14},{6,10},... | collective-permute-start | bytes 294920 | tf_op jit(solution)/shard_map/ppermute | solution.py:367
  29.7 0.1 collective-permute-start.13
  29.8 0.0 collective-permute-start.6
  29.8 0.0 collective-permute-done.7.refs_2_
  29.9 0.5 collective-permute-start.8
  30.4 0.0 collective-permute-done.9.refs_0_
  30.4 0.5 collective-permute-start.11
  30.9 3.9 %collective-permute-done.17.refs_0_ = bf16[128,384]{1,0:T(8,128)(2,1)S(1)} collective-permute-done((bf16[128,384]{1,0:T(8,128)(2,1)S(1)}, bf16[128,384]{1,0:T(8,128)(2,1)S(1)}, u32[]{:S(2)}, u32[]{:S(2)}) %collective-permute-start.17) | collective-permute-done | bytes 98336 | tf_op jit(solution)/shard_map/ppermute | solution.py:367
  34.9 0.5 collective-permute-start.22
  35.4 0.0 collective-permute-done.6.refs_1_
  35.4 0.0 collective-permute-start.10
  35.4 0.0 collective-permute-done.8.refs_3_
  35.4 1.6 %collective-permute-start.19 = (bf16[128,384]{1,0:T(8,128)(2,1)S(1)}, bf16[128,384]{1,0:T(8,128)(2,1)S(1)}, u32[]{:S(2)}, u32[]{:S(2)}) collective-permute-start(bf16[128,384]{1,0:T(8,128)(2,1)S(1)} %collective-permute-done.17.refs_0_), channel_id=1, source_target_pairs={{0,2},{1,3},{2,0},{3,1},{4,6},{5,7},{6,4},{7,5},{8,10},{9,11},{10,... | collective-permute-start | bytes 294920 | tf_op jit(solution)/shard_map/ppermute | solution.py:364
  37.0 1.1 %prepare.4 = (bf16[128,768]{1,0:T(8,128)(2,1)S(1)}, bf16[256,512]{1,0:T(8,128)(2,1)S(1)}, s32[1,256]{1,0:T(1,128)S(1)}, bf16[192,128]{1,0:T(8,128)(2,1)S(1)}) custom-call(bf16[128,384]{1,0:T(8,128)(2,1)S(1)} %embed.1.refs_0_, bf16[128,384]{1,0:T(8,128)(2,1)S(1)} %collective-permute-done.6.refs_1_, bf16[128,384]{1,0:T(8,128)(2,1)S(1)} %collective-permute-done.7.refs_2_, ...), custom_call_target="tpu_custom_call" | custom-call | flops 226492416 | bytes 884736 | tf_op jit(solution)/shard_map/prepare/pallas_call | solution.py:203
  38.1 0.0 collective-permute-done.13.refs_0_
  38.1 0.6 collective-permute-start.15
  38.7 0.1 constant_dynamic-slice_fusion.3
  38.8 0.0 collective-permute-done.10.refs_1_
  38.8 0.6 collective-permute-start.21
  39.4 0.6 collective-permute-done.12.refs_3_
  40.0 0.2 collective-permute-start.18
  40.1 1.1 %prepare.5 = (bf16[128,768]{1,0:T(8,128)(2,1)S(1)}, bf16[256,512]{1,0:T(8,128)(2,1)S(1)}, s32[1,256]{1,0:T(1,128)S(1)}, bf16[192,128]{1,0:T(8,128)(2,1)S(1)}) custom-call(bf16[128,384]{1,0:T(8,128)(2,1)S(1)} %collective-permute-done.9.refs_0_, bf16[128,384]{1,0:T(8,128)(2,1)S(1)} %collective-permute-done.10.refs_1_, ...), custom_call_target="tpu_custom_call" | custom-call | flops 226492416 | bytes 884736 | tf_op jit(solution)/shard_map/prepare/pallas_call | solution.py:203
  41.3 1.9 %collective-permute-done.19.refs_2_ = bf16[128,384]{1,0:T(8,128)(2,1)S(1)} collective-permute-done((bf16[128,384]{1,0:T(8,128)(2,1)S(1)}, bf16[128,384]{1,0:T(8,128)(2,1)S(1)}, u32[]{:S(2)}, u32[]{:S(2)}) %collective-permute-start.19) | collective-permute-done | bytes 98336 | tf_op jit(solution)/shard_map/ppermute | solution.py:364
  43.2 0.5 collective-permute-start.20
  43.7 0.5 collective-permute-done.15.refs_2_
  44.2 0.0 collective-permute-start.16
  44.2 0.1 constant_dynamic-slice_fusion
  44.3 0.0 collective-permute-done.18.refs_1_
  44.4 0.6 collective-permute-start.23
  44.9 1.1 %prepare.7 = (bf16[128,768]{1,0:T(8,128)(2,1)S(1)}, bf16[256,512]{1,0:T(8,128)(2,1)S(1)}, s32[1,256]{1,0:T(1,128)S(1)}, bf16[192,128]{1,0:T(8,128)(2,1)S(1)}) custom-call(bf16[128,384]{1,0:T(8,128)(2,1)S(1)} %collective-permute-done.17.refs_0_, bf16[128,384]{1,0:T(8,128)(2,1)S(1)} %collective-permute-done.18.refs_1_, ...), custom_call_target="tpu_custom_call" | custom-call | flops 226492416 | bytes 884736 | tf_op jit(solution)/shard_map/prepare/pallas_call | solution.py:203
  46.1 0.0 collective-permute-done.16.refs_3_
  46.1 1.1 %prepare.6 = (bf16[128,768]{1,0:T(8,128)(2,1)S(1)}, bf16[256,512]{1,0:T(8,128)(2,1)S(1)}, s32[1,256]{1,0:T(1,128)S(1)}, bf16[192,128]{1,0:T(8,128)(2,1)S(1)}) custom-call(bf16[128,384]{1,0:T(8,128)(2,1)S(1)} %collective-permute-done.13.refs_0_, bf16[128,384]{1,0:T(8,128)(2,1)S(1)} %collective-permute-done.14.refs_1_, ...), custom_call_target="tpu_custom_call" | custom-call | flops 226492416 | bytes 884736 | tf_op jit(solution)/shard_map/prepare/pallas_call | solution.py:203
  47.2 0.0 collective-permute-done.21.w1
  47.2 0.0 collective-permute-done.23.w3
  47.2 3.4 %attend.1.a0 = bf16[192,512]{1,0:T(8,128)(2,1)S(1)} custom-call(bf16[128,768]{1,0:T(8,128)(2,1)S(1)} %get-tuple-element.49.refs_0_, bf16[128,768]{1,0:T(8,128)(2,1)S(1)} %get-tuple-element.50.refs_1_, bf16[128,768]{1,0:T(8,128)(2,1)S(1)} %get-tuple-element.51.refs_2_, bf16[128,768]{1,0:T(8,128)(2,1)S(1)} %get-tuple-element.52.refs_3_, ...), custom_call_target="tpu_custom_call" | custom-call | flops 1207959552 | bytes 393216 | tf_op jit(solution)/shard_map/attend/pallas_call | solution.py:295
  50.6 0.6 collective-permute-start.25
  51.2 0.0 collective-permute-start.24
  51.2 6.3 %collective-permute-done.25.a2 = bf16[192,512]{1,0:T(8,128)(2,1)S(1)} collective-permute-done((bf16[192,512]{1,0:T(8,128)(2,1)S(1)}, bf16[192,512]{1,0:T(8,128)(2,1)S(1)}, u32[]{:S(2)}, u32[]{:S(2)}) %collective-permute-start.25) | collective-permute-done | bytes 196640 | tf_op jit(solution)/shard_map/ppermute | solution.py:364
  57.5 0.0 collective-permute-start.26
  57.5 0.0 collective-permute-done.24.a1
  57.5 1.4 %collective-permute-done.26.a3 = bf16[192,512]{1,0:T(8,128)(2,1)S(1)} collective-permute-done((bf16[192,512]{1,0:T(8,128)(2,1)S(1)}, bf16[192,512]{1,0:T(8,128)(2,1)S(1)}, u32[]{:S(2)}, u32[]{:S(2)}) %collective-permute-start.26) | collective-permute-done | bytes 196640 | tf_op jit(solution)/shard_map/ppermute | solution.py:364
  59.0 1.1 %project_out.1 = bf16[192,512]{1,0:T(8,128)(2,1)} custom-call(bf16[192,512]{1,0:T(8,128)(2,1)S(1)} %attend.1.a0, bf16[192,512]{1,0:T(8,128)(2,1)S(1)} %collective-permute-done.24.a1, bf16[192,512]{1,0:T(8,128)(2,1)S(1)} %collective-permute-done.25.a2, bf16[192,512]{1,0:T(8,128)(2,1)S(1)} %collective-permute-done.26.a3, ...), custom_call_target="tpu_custom_call" | custom-call | tf_op jit(solution)/shard_map/project_out/pallas_call | solution.py:329
  (22 shorter events, 0.1 us)
Async XLA Ops:
  0.0 22.9 %copy-start.3 = (bf16[256,1536]{1,0:T(8,128)(2,1)S(1)}, bf16[256,1536]{1,0:T(8,128)(2,1)}, u32[]{:S(2)}) copy-start(bf16[256,1536]{1,0:T(8,128)(2,1)} %rows_ref.3) | copy-start | bytes 2359300
  0.0 10.2 %copy-start.4 = (bf16[1536,192]{0,1:T(8,128)(2,1)S(1)}, bf16[1536,192]{0,1:T(8,128)(2,1)}, u32[]{:S(2)}) copy-start(bf16[1536,192]{0,1:T(8,128)(2,1)} %param.22) | copy-start | bytes 1769476
  0.0 13.3 %copy-start.8 = (s32[256,1]{0,1:T(1,128)S(1)}, s32[256,1]{0,1:T(1,128)}, u32[]{:S(2)}) copy-start(s32[256,1]{0,1:T(1,128)} %param.15) | copy-start | bytes 3076
  0.0 22.9 %copy-start.7 = (f32[1536]{0:T(1024)S(1)}, f32[1536]{0:T(1024)}, u32[]{:S(2)}) copy-start(f32[1536]{0:T(1024)} %gain_ref.3) | copy-start | bytes 18436
  0.0 22.9 %copy-start.6 = (f32[1536]{0:T(1024)S(1)}, f32[1536]{0:T(1024)}, u32[]{:S(2)}) copy-start(f32[1536]{0:T(1024)} %scale_ref.1) | copy-start | bytes 18436
  6.9 24.0 %copy-start.9 = (bf16[192,768]{1,0:T(8,128)(2,1)S(1)}, bf16[192,768]{1,0:T(8,128)(2,1)}, u32[]{:S(2)}) copy-start(bf16[192,768]{1,0:T(8,128)(2,1)} %param.27) | copy-start | bytes 884740
  6.9 30.1 %copy-start = (bf16[768,192]{0,1:T(8,128)(2,1)S(1)}, bf16[768,192]{0,1:T(8,128)(2,1)}, u32[]{:S(2)}) copy-start(bf16[768,192]{0,1:T(8,128)(2,1)} %param.24) | copy-start | bytes 884740
  6.9 30.1 %copy-start.1 = (bf16[768,192]{0,1:T(8,128)(2,1)S(1)}, bf16[768,192]{0,1:T(8,128)(2,1)}, u32[]{:S(2)}) copy-start(bf16[768,192]{0,1:T(8,128)(2,1)} %param.25) | copy-start | bytes 884740
  6.9 30.1 %copy-start.2 = (bf16[768,192]{0,1:T(8,128)(2,1)S(1)}, bf16[768,192]{0,1:T(8,128)(2,1)}, u32[]{:S(2)}) copy-start(bf16[768,192]{0,1:T(8,128)(2,1)} %param.26) | copy-start | bytes 884740
  6.9 30.1 %copy-start.5 = (f32[768]{0:T(1024)S(1)}, f32[768]{0:T(1024)}, u32[]{:S(2)}) copy-start(f32[768]{0:T(1024)} %refs_5_.7) | copy-start | bytes 9220
  6.9 2.1 %collective-permute-start = (bf16[128,1536]{1,0:T(8,128)(2,1)}, bf16[128,1536]{1,0:T(8,128)(2,1)S(1)}, u32[]{:S(2)}, u32[]{:S(2)}) collective-permute-start(bf16[128,1536]{1,0:T(8,128)(2,1)} %get-tuple-element.38), channel_id=1, source_target_pairs={{0,1},{1,0},{2,3},{3,2},{4,5},{5,4},{6,7},{7,6},{8,9},{9,8},{10,11... | collective-permute-start | bytes 1179656 | tf_op jit(solution)/shard_map/ppermute | solution.py:364
  10.2 12.7 %collective-permute-start.5 = (bf16[192,1536]{1,0:T(8,128)(2,1)S(1)}, bf16[192,1536]{1,0:T(8,128)(2,1)S(1)}, u32[]{:S(2)}, u32[]{:S(2)}) collective-permute-start(bf16[192,1536]{1,0:T(8,128)(2,1)S(1)} %bitcast.18), channel_id=1, source_target_pairs={{0,1},{1,0},{2,3},{3,2},{4,5},{5,4},{6,7},{7,6},{8,9},{9,8},{10,11... | collective-permute-start | bytes 1769480 | tf_op jit(solution)/shard_map/ppermute | solution.py:364
  10.7 12.3 %collective-permute-start.1 = (bf16[128,1536]{1,0:T(8,128)(2,1)S(1)}, bf16[128,1536]{1,0:T(8,128)(2,1)S(1)}, u32[]{:S(2)}, u32[]{:S(2)}) collective-permute-start(bf16[128,1536]{1,0:T(8,128)(2,1)S(1)} %add_convert_fusion.here_ref), channel_id=1, source_target_pairs={{0,2},{1,3},{2,0},{3,1},{4,6},{5,7},{6,4},{7,5},{8,10},{9,11},{10,... | collective-permute-start | bytes 1179656 | tf_op jit(solution)/shard_map/ppermute | solution.py:364
  13.3 5.4 %collective-permute-start.4 = (s32[1,256]{1,0:T(1,128)S(1)}, s32[1,256]{1,0:T(1,128)S(1)}, u32[]{:S(2)}, u32[]{:S(2)}) collective-permute-start(s32[1,256]{1,0:T(1,128)S(1)} %bitcast.20), channel_id=1, source_target_pairs={{0,12},{4,8},{8,4},{12,0},{1,13},{5,9},{9,5},{13,1},{2,14},{6,10},... | collective-permute-start | bytes 3080 | tf_op jit(solution)/shard_map/ppermute | solution.py:367
  16.9 4.5 %collective-permute-start.3 = (s32[1,256]{1,0:T(1,128)S(1)}, s32[1,256]{1,0:T(1,128)S(1)}, u32[]{:S(2)}, u32[]{:S(2)}) collective-permute-start(s32[1,256]{1,0:T(1,128)S(1)} %bitcast.21), channel_id=1, source_target_pairs={{0,8},{4,12},{8,0},{12,4},{1,9},{5,13},{9,1},{13,5},{2,10},{6,14},... | collective-permute-start | bytes 3080 | tf_op jit(solution)/shard_map/ppermute | solution.py:367
  16.9 4.5 %collective-permute-start.2 = (s32[1,256]{1,0:T(1,128)S(1)}, s32[1,256]{1,0:T(1,128)S(1)}, u32[]{:S(2)}, u32[]{:S(2)}) collective-permute-start(s32[1,256]{1,0:T(1,128)S(1)} %bitcast.22), channel_id=1, source_target_pairs={{0,4},{4,0},{8,12},{12,8},{1,5},{5,1},{9,13},{13,9},{2,6},{6,2},{1... | collective-permute-start | bytes 3080 | tf_op jit(solution)/shard_map/ppermute | solution.py:367
  23.9 6.0 %collective-permute-start.7 = (bf16[128,384]{1,0:T(8,128)(2,1)S(1)}, bf16[128,384]{1,0:T(8,128)(2,1)S(1)}, u32[]{:S(2)}, u32[]{:S(2)}) collective-permute-start(bf16[128,384]{1,0:T(8,128)(2,1)S(1)} %embed.1.refs_0_), channel_id=1, source_target_pairs={{0,2},{1,3},{2,0},{3,1},{4,6},{5,7},{6,4},{7,5},{8,10},{9,11},{10,... | collective-permute-start | bytes 294920 | tf_op jit(solution)/shard_map/ppermute | solution.py:364
  25.7 4.7 %collective-permute-start.9 = (bf16[128,384]{1,0:T(8,128)(2,1)S(1)}, bf16[128,384]{1,0:T(8,128)(2,1)S(1)}, u32[]{:S(2)}, u32[]{:S(2)}) collective-permute-start(bf16[128,384]{1,0:T(8,128)(2,1)S(1)} %embed.1.refs_0_), channel_id=1, source_target_pairs={{0,4},{4,0},{8,12},{12,8},{1,5},{5,1},{9,13},{13,9},{2,6},{6,2},{1... | collective-permute-start | bytes 294920 | tf_op jit(solution)/shard_map/ppermute | solution.py:367
  27.3 7.6 %collective-permute-start.17 = (bf16[128,384]{1,0:T(8,128)(2,1)S(1)}, bf16[128,384]{1,0:T(8,128)(2,1)S(1)}, u32[]{:S(2)}, u32[]{:S(2)}) collective-permute-start(bf16[128,384]{1,0:T(8,128)(2,1)S(1)} %embed.1.refs_0_), channel_id=1, source_target_pairs={{0,12},{4,8},{8,4},{12,0},{1,13},{5,9},{9,5},{13,1},{2,14},{6,10},... | collective-permute-start | bytes 294920 | tf_op jit(solution)/shard_map/ppermute | solution.py:367
  29.7 8.4 %collective-permute-start.13 = (bf16[128,384]{1,0:T(8,128)(2,1)S(1)}, bf16[128,384]{1,0:T(8,128)(2,1)S(1)}, u32[]{:S(2)}, u32[]{:S(2)}) collective-permute-start(bf16[128,384]{1,0:T(8,128)(2,1)S(1)} %embed.1.refs_0_), channel_id=1, source_target_pairs={{0,8},{4,12},{8,0},{12,4},{1,9},{5,13},{9,1},{13,5},{2,10},{6,14},... | collective-permute-start | bytes 294920 | tf_op jit(solution)/shard_map/ppermute | solution.py:367
  29.8 5.5 %collective-permute-start.6 = (bf16[128,384]{1,0:T(8,128)(2,1)S(1)}, bf16[128,384]{1,0:T(8,128)(2,1)S(1)}, u32[]{:S(2)}, u32[]{:S(2)}) collective-permute-start(bf16[128,384]{1,0:T(8,128)(2,1)S(1)} %embed.1.refs_0_), channel_id=1, source_target_pairs={{0,1},{1,0},{2,3},{3,2},{4,5},{5,4},{6,7},{7,6},{8,9},{9,8},{10,11... | collective-permute-start | bytes 294920 | tf_op jit(solution)/shard_map/ppermute | solution.py:364
  29.9 5.5 %collective-permute-start.8 = (bf16[128,384]{1,0:T(8,128)(2,1)S(1)}, bf16[128,384]{1,0:T(8,128)(2,1)S(1)}, u32[]{:S(2)}, u32[]{:S(2)}) collective-permute-start(bf16[128,384]{1,0:T(8,128)(2,1)S(1)} %collective-permute-done.7.refs_2_), channel_id=1, source_target_pairs={{0,1},{1,0},{2,3},{3,2},{4,5},{5,4},{6,7},{7,6},{8,9},{9,8},{10,11... | collective-permute-start | bytes 294920 | tf_op jit(solution)/shard_map/ppermute | solution.py:364
  30.4 8.3 %collective-permute-start.11 = (bf16[128,384]{1,0:T(8,128)(2,1)S(1)}, bf16[128,384]{1,0:T(8,128)(2,1)S(1)}, u32[]{:S(2)}, u32[]{:S(2)}) collective-permute-start(bf16[128,384]{1,0:T(8,128)(2,1)S(1)} %collective-permute-done.9.refs_0_), channel_id=1, source_target_pairs={{0,2},{1,3},{2,0},{3,1},{4,6},{5,7},{6,4},{7,5},{8,10},{9,11},{10,... | collective-permute-start | bytes 294920 | tf_op jit(solution)/shard_map/ppermute | solution.py:364
  34.9 8.3 %collective-permute-start.22 = (bf16[192,384]{1,0:T(8,128)(2,1)S(1)}, bf16[192,384]{1,0:T(8,128)(2,1)S(1)}, u32[]{:S(2)}, u32[]{:S(2)}) collective-permute-start(bf16[192,384]{1,0:T(8,128)(2,1)S(1)} %constant_dynamic-slice_fusion.2), channel_id=1, source_target_pairs={{0,2},{1,3},{2,0},{3,1},{4,6},{5,7},{6,4},{7,5},{8,10},{9,11},{10,... | collective-permute-start | bytes 442376 | tf_op jit(solution)/shard_map/ppermute | solution.py:364
  35.4 3.4 %collective-permute-start.10 = (bf16[128,384]{1,0:T(8,128)(2,1)S(1)}, bf16[128,384]{1,0:T(8,128)(2,1)S(1)}, u32[]{:S(2)}, u32[]{:S(2)}) collective-permute-start(bf16[128,384]{1,0:T(8,128)(2,1)S(1)} %collective-permute-done.9.refs_0_), channel_id=1, source_target_pairs={{0,1},{1,0},{2,3},{3,2},{4,5},{5,4},{6,7},{7,6},{8,9},{9,8},{10,11... | collective-permute-start | bytes 294920 | tf_op jit(solution)/shard_map/ppermute | solution.py:364
  35.4 7.8 %collective-permute-start.19 = (bf16[128,384]{1,0:T(8,128)(2,1)S(1)}, bf16[128,384]{1,0:T(8,128)(2,1)S(1)}, u32[]{:S(2)}, u32[]{:S(2)}) collective-permute-start(bf16[128,384]{1,0:T(8,128)(2,1)S(1)} %collective-permute-done.17.refs_0_), channel_id=1, source_target_pairs={{0,2},{1,3},{2,0},{3,1},{4,6},{5,7},{6,4},{7,5},{8,10},{9,11},{10,... | collective-permute-start | bytes 294920 | tf_op jit(solution)/shard_map/ppermute | solution.py:364
  38.1 6.1 %collective-permute-start.15 = (bf16[128,384]{1,0:T(8,128)(2,1)S(1)}, bf16[128,384]{1,0:T(8,128)(2,1)S(1)}, u32[]{:S(2)}, u32[]{:S(2)}) collective-permute-start(bf16[128,384]{1,0:T(8,128)(2,1)S(1)} %collective-permute-done.13.refs_0_), channel_id=1, source_target_pairs={{0,2},{1,3},{2,0},{3,1},{4,6},{5,7},{6,4},{7,5},{8,10},{9,11},{10,... | collective-permute-start | bytes 294920 | tf_op jit(solution)/shard_map/ppermute | solution.py:364
  38.7 1.3 %collective-permute-start.12 = (bf16[128,384]{1,0:T(8,128)(2,1)S(1)}, bf16[128,384]{1,0:T(8,128)(2,1)S(1)}, u32[]{:S(2)}, u32[]{:S(2)}) collective-permute-start(bf16[128,384]{1,0:T(8,128)(2,1)S(1)} %collective-permute-done.11.refs_2_), channel_id=1, source_target_pairs={{0,1},{1,0},{2,3},{3,2},{4,5},{5,4},{6,7},{7,6},{8,9},{9,8},{10,11... | collective-permute-start | bytes 294920 | tf_op jit(solution)/shard_map/ppermute | solution.py:364
  38.8 8.3 %collective-permute-start.21 = (bf16[192,192]{1,0:T(8,128)(2,1)S(1)}, bf16[192,192]{1,0:T(8,128)(2,1)S(1)}, u32[]{:S(2)}, u32[]{:S(2)}) collective-permute-start(bf16[192,192]{1,0:T(8,128)(2,1)S(1)} %get-tuple-element.69), channel_id=1, source_target_pairs={{0,1},{1,0},{2,3},{3,2},{4,5},{5,4},{6,7},{7,6},{8,9},{9,8},{10,11... | collective-permute-start | bytes 221192 | tf_op jit(solution)/shard_map/ppermute | solution.py:364
  40.0 4.4 %collective-permute-start.18 = (bf16[128,384]{1,0:T(8,128)(2,1)S(1)}, bf16[128,384]{1,0:T(8,128)(2,1)S(1)}, u32[]{:S(2)}, u32[]{:S(2)}) collective-permute-start(bf16[128,384]{1,0:T(8,128)(2,1)S(1)} %collective-permute-done.17.refs_0_), channel_id=1, source_target_pairs={{0,1},{1,0},{2,3},{3,2},{4,5},{5,4},{6,7},{7,6},{8,9},{9,8},{10,11... | collective-permute-start | bytes 294920 | tf_op jit(solution)/shard_map/ppermute | solution.py:364
  43.2 2.9 %collective-permute-start.14 = (bf16[128,384]{1,0:T(8,128)(2,1)S(1)}, bf16[128,384]{1,0:T(8,128)(2,1)S(1)}, u32[]{:S(2)}, u32[]{:S(2)}) collective-permute-start(bf16[128,384]{1,0:T(8,128)(2,1)S(1)} %collective-permute-done.13.refs_0_), channel_id=1, source_target_pairs={{0,1},{1,0},{2,3},{3,2},{4,5},{5,4},{6,7},{7,6},{8,9},{9,8},{10,11... | collective-permute-start | bytes 294920 | tf_op jit(solution)/shard_map/ppermute | solution.py:364
  43.2 1.8 %collective-permute-start.20 = (bf16[128,384]{1,0:T(8,128)(2,1)S(1)}, bf16[128,384]{1,0:T(8,128)(2,1)S(1)}, u32[]{:S(2)}, u32[]{:S(2)}) collective-permute-start(bf16[128,384]{1,0:T(8,128)(2,1)S(1)} %collective-permute-done.19.refs_2_), channel_id=1, source_target_pairs={{0,1},{1,0},{2,3},{3,2},{4,5},{5,4},{6,7},{7,6},{8,9},{9,8},{10,11... | collective-permute-start | bytes 294920 | tf_op jit(solution)/shard_map/ppermute | solution.py:364
  44.2 1.8 %collective-permute-start.16 = (bf16[128,384]{1,0:T(8,128)(2,1)S(1)}, bf16[128,384]{1,0:T(8,128)(2,1)S(1)}, u32[]{:S(2)}, u32[]{:S(2)}) collective-permute-start(bf16[128,384]{1,0:T(8,128)(2,1)S(1)} %collective-permute-done.15.refs_2_), channel_id=1, source_target_pairs={{0,1},{1,0},{2,3},{3,2},{4,5},{5,4},{6,7},{7,6},{8,9},{9,8},{10,11... | collective-permute-start | bytes 294920 | tf_op jit(solution)/shard_map/ppermute | solution.py:364
  44.4 2.8 %collective-permute-start.23 = (bf16[192,192]{1,0:T(8,128)(2,1)S(1)}, bf16[192,192]{1,0:T(8,128)(2,1)S(1)}, u32[]{:S(2)}, u32[]{:S(2)}) collective-permute-start(bf16[192,192]{1,0:T(8,128)(2,1)S(1)} %get-tuple-element.71), channel_id=1, source_target_pairs={{0,1},{1,0},{2,3},{3,2},{4,5},{5,4},{6,7},{7,6},{8,9},{9,8},{10,11... | collective-permute-start | bytes 221192 | tf_op jit(solution)/shard_map/ppermute | solution.py:364
  50.6 6.9 %collective-permute-start.25 = (bf16[192,512]{1,0:T(8,128)(2,1)S(1)}, bf16[192,512]{1,0:T(8,128)(2,1)S(1)}, u32[]{:S(2)}, u32[]{:S(2)}) collective-permute-start(bf16[192,512]{1,0:T(8,128)(2,1)S(1)} %attend.1.a0), channel_id=1, source_target_pairs={{0,2},{1,3},{2,0},{3,1},{4,6},{5,7},{6,4},{7,5},{8,10},{9,11},{10,... | collective-permute-start | bytes 589832 | tf_op jit(solution)/shard_map/ppermute | solution.py:364
  51.2 6.3 %collective-permute-start.24 = (bf16[192,512]{1,0:T(8,128)(2,1)S(1)}, bf16[192,512]{1,0:T(8,128)(2,1)S(1)}, u32[]{:S(2)}, u32[]{:S(2)}) collective-permute-start(bf16[192,512]{1,0:T(8,128)(2,1)S(1)} %attend.1.a0), channel_id=1, source_target_pairs={{0,1},{1,0},{2,3},{3,2},{4,5},{5,4},{6,7},{7,6},{8,9},{9,8},{10,11... | collective-permute-start | bytes 589832 | tf_op jit(solution)/shard_map/ppermute | solution.py:364
  57.5 1.4 %collective-permute-start.26 = (bf16[192,512]{1,0:T(8,128)(2,1)S(1)}, bf16[192,512]{1,0:T(8,128)(2,1)S(1)}, u32[]{:S(2)}, u32[]{:S(2)}) collective-permute-start(bf16[192,512]{1,0:T(8,128)(2,1)S(1)} %collective-permute-done.25.a2), channel_id=1, source_target_pairs={{0,1},{1,0},{2,3},{3,2},{4,5},{5,4},{6,7},{7,6},{8,9},{9,8},{10,11... | collective-permute-start | bytes 589832 | tf_op jit(solution)/shard_map/ppermute | solution.py:364

commit v4 on v3

v4 whole, which is shorter than its diff:
```python
import functools

import jax
import jax.numpy as jnp
from jax import lax
from jax.experimental import pallas as pl
from jax.experimental.pallas import tpu as pltpu
from jax.sharding import PartitionSpec as P

HD = 48
RATE = 4
EPSILON = 1e-06
MASKED = -1e30
MIB = 1024 * 1024
LOG2E = 1.4426950408889634

f32 = jnp.float32
bf16 = jnp.bfloat16


def layer_norm(features, norm_gain):
    middle = jnp.mean(features, axis=-1, keepdims=True)
    centred = features - middle
    spread = jnp.mean(centred * centred, axis=-1, keepdims=True)
    return centred * lax.rsqrt(spread + EPSILON) * norm_gain


def dot(a, b):
    return jnp.dot(a, b, preferred_element_type=f32)


def dot_t(a, b):
    return lax.dot_general(a, b, (((1,), (1,)), ((), ())), preferred_element_type=f32)


def whole(shape):
    return pl.BlockSpec(shape, lambda *_: (0,) * len(shape))


VMEM = pl.BlockSpec(memory_space=pltpu.VMEM)


def mdl_index():
    return lax.axis_index("mdl")


def seq_index():
    return lax.axis_index("seq")


def row(ref):
    return ref[...].reshape(1, ref.shape[0])


def ffn_kernel(
    rows_ref, gain_ref, gate_ref, up_ref, down_ref, keep_ref, send_ref,
    rows, gate, upward, down, normed, sems,
):
    me = mdl_index()
    half = keep_ref.shape[0]
    pairs = ((rows_ref, rows), (gate_ref, gate), (up_ref, upward), (down_ref, down))
    copies = [pltpu.make_async_copy(source, target, sems.at[i]) for i, (source, target) in enumerate(pairs)]
    for copy in copies:
        copy.start()
    copies[0].wait()
    for place in range(2):
        start = pl.multiple_of(((me & 1) ^ place) * half, half)
        part = rows[pl.ds(start, half), :].astype(f32)
        normed[place * half : (place + 1) * half, :] = layer_norm(part, row(gain_ref)).astype(bf16)
    copies[1].wait()
    opened = dot(normed[...], gate[...])
    opened = opened * jax.nn.sigmoid(opened)
    copies[2].wait()
    hidden = (opened * dot(normed[...], upward[...])).astype(bf16)
    keep_ref[...] = hidden[:half, :]
    copies[3].wait()
    send_ref[...] = dot(hidden[half:, :], down[...]).astype(bf16)


def feed_forward(rows, gain, gate_weight, up_weight, down_weight):
    tiles, width = rows.shape
    hidden = gate_weight.shape[1]
    half = tiles // 2
    far = pl.BlockSpec(memory_space=pltpu.HBM)
    return pl.pallas_call(
        ffn_kernel,
        in_specs=[far, VMEM, far, far, far],
        out_specs=[VMEM, VMEM],
        out_shape=[jax.ShapeDtypeStruct((half, hidden), bf16), jax.ShapeDtypeStruct((half, width), bf16)],
        scratch_shapes=[
            pltpu.VMEM((tiles, width), bf16),
            pltpu.VMEM((width, hidden), bf16),
            pltpu.VMEM((width, hidden), bf16),
            pltpu.VMEM((hidden, width), bf16),
            pltpu.VMEM((tiles, width), bf16),
            pltpu.SemaphoreType.DMA((4,)),
        ],
        compiler_params=pltpu.CompilerParams(vmem_limit_bytes=60 * MIB),
        cost_estimate=pl.CostEstimate(
            flops=6 * tiles * width * hidden, bytes_accessed=6 * width * hidden, transcendentals=tiles * hidden
        ),
        name="feed_forward",
    )(rows, gain, gate_weight, up_weight, down_weight)


def gather_kernel(hidden_ref, down_ref, near_ref, out_ref):
    out_ref[...] = (dot(hidden_ref[...], down_ref[...]) + near_ref[...].astype(f32)).astype(bf16)


def gather_sums(hidden, down_weight, near):
    return pl.pallas_call(
        gather_kernel,
        in_specs=[VMEM] * 3,
        out_specs=VMEM,
        out_shape=jax.ShapeDtypeStruct(near.shape, bf16),
        compiler_params=pltpu.CompilerParams(vmem_limit_bytes=16 * MIB),
        name="gather_sums",
    )(hidden, down_weight, near)


def embed_kernel(rows_ref, here_ref, far_ref, scale_ref, gain_ref, own, near, out_ref, blocks):
    core = mdl_index() & 1
    half = here_ref.shape[0]
    start = pl.multiple_of(core * half, half)
    rows = rows_ref[pl.ds(start, half), :].astype(f32)
    feedfwd = here_ref[...].astype(f32) + far_ref[...].astype(f32)
    stream = rows + row(scale_ref) * feedfwd
    final = layer_norm(stream, row(gain_ref)).astype(bf16)
    blocks[core] = dot_t(final, own[...])
    blocks[core ^ 1] = dot_t(final, near[...])
    out_ref[...] = jnp.concatenate([blocks[0], blocks[1]], axis=1).astype(bf16)


def embed(rows, here, far, scale, gain, own, near):
    half, width = here.shape
    columns = own.shape[0]
    return pl.pallas_call(
        embed_kernel,
        in_specs=[VMEM] * 7,
        out_specs=VMEM,
        out_shape=jax.ShapeDtypeStruct((half, 2 * columns), bf16),
        scratch_shapes=[pltpu.VMEM((2, half, columns), f32)],
        compiler_params=pltpu.CompilerParams(vmem_limit_bytes=16 * MIB),
        cost_estimate=pl.CostEstimate(
            flops=4 * half * width * columns, bytes_accessed=4 * width * columns, transcendentals=0
        ),
        name="embed",
    )(rows, here, far, scale, gain, own, near)


LANES = 256


def plan_kernel(groups, n, *refs):
    here = seq_index()
    for owner_ref, chosen_ref, bias_ref in zip(refs[:groups], refs[groups : 2 * groups], refs[2 * groups :]):
        owner = owner_ref[...]
        cap, tiles = chosen_ref.shape
        rows = lax.broadcasted_iota(jnp.int32, (tiles, tiles), 0)
        lanes = lax.broadcasted_iota(jnp.int32, (tiles, tiles), 1)
        named = lax.broadcasted_iota(jnp.int32, (max(n, 8), tiles), 0) == owner
        onehot = jnp.where(named, 1.0, 0.0)
        earlier = dot(onehot.astype(bf16), jnp.where(rows < lanes, 1.0, 0.0).astype(bf16))
        arrival = jnp.sum(onehot * earlier, axis=0, keepdims=True)
        slot = lax.broadcasted_iota(jnp.int32, (cap, tiles), 0)
        taken = (slot == arrival.astype(jnp.int32)) & (owner == here)
        chosen_ref[...] = jnp.where(taken, 1.0, 0.0).astype(bf16)
        column = jnp.sum(jnp.where(rows == lanes, arrival, 0.0), axis=1, keepdims=True).astype(jnp.int32)
        kept = lax.broadcasted_iota(jnp.int32, bias_ref.shape, 1) == (column & (RATE - 1))
        bias_ref[...] = jnp.where(kept, 0.0, MASKED).astype(bf16)


def plan(owners, n, cap, spare):
    groups = len(owners)
    tiles = owners[0].shape[-1]
    if groups > 1 or n == 1:
        count, lead, block = 1, (), whole
    else:
        count, lead = n, (n,)

        def block(shape):
            return pl.BlockSpec((None, *shape), lambda b: (b, 0, 0))

    shapes = [(cap, tiles)] * groups + [(tiles, spare)] * groups
    outs = pl.pallas_call(
        functools.partial(plan_kernel, groups, n),
        grid=(count,),
        in_specs=[block((1, tiles))] * groups,
        out_specs=[block(shape) for shape in shapes],
        out_shape=[jax.ShapeDtypeStruct(lead + shape, bf16) for shape in shapes],
        compiler_params=pltpu.CompilerParams(vmem_limit_bytes=16 * MIB),
        name="plan",
    )(*owners)
    return list(zip(outs[:groups], outs[groups:]))


def prepare_kernel(loose, *refs):
    pieces = refs[:loose]
    chosen_ref, bias_ref, gain_ref, wq, wk, wv, local_ref, all_ref, residual_ref, block = refs[loose:]
    me = mdl_index()
    tiles, width = block.shape
    columns = wq.shape[0]
    if loose > 1:
        half, side = tiles // 2, width // 2
        for km in range(4):
            at = pl.multiple_of(((me ^ km) & 1) * half, half)
            over = pl.multiple_of(((me ^ km) >> 1) * side, side)
            block[pl.ds(at, half), pl.ds(over, side)] = pieces[km][...]
        rows = block[...]
    else:
        rows = pieces[0][...]
    chosen = chosen_ref[...]
    cap = chosen.shape[0]
    mine = (
        lax.broadcasted_iota(jnp.int32, (columns, width), 1)
        == lax.broadcasted_iota(jnp.int32, (columns, width), 0) + me * columns
    )
    picked = jnp.where(mine, 1.0, 0.0).astype(bf16)
    residual_ref[...] = dot_t(dot_t(picked, rows).astype(bf16), chosen).astype(bf16)
    normed = layer_norm(rows.astype(f32), row(gain_ref)).astype(bf16)
    queries = dot_t(normed, wq[...]).astype(bf16)
    keys = dot_t(normed, wk[...]).astype(bf16)
    values = dot_t(normed, wv[...]).astype(bf16)
    occupied = jnp.sum(chosen.astype(f32), axis=1, keepdims=True)
    all_ref[:, :columns] = keys
    all_ref[:, columns:LANES] = bias_ref[...]
    all_ref[:, LANES : LANES + columns] = values
    local_ref[:, :columns] = dot(chosen, queries).astype(bf16)
    local_ref[:, columns:LANES] = jnp.zeros((cap, LANES - columns), bf16)
    local_ref[:, LANES : LANES + columns] = dot(chosen, keys).astype(bf16)
    local_ref[:, LANES + columns : 2 * LANES] = jnp.broadcast_to(
        jnp.where(occupied > 0.5, 0.0, MASKED), (cap, LANES - columns)
    ).astype(bf16)
    local_ref[:, 2 * LANES : 2 * LANES + columns] = dot(chosen, values).astype(bf16)


def prepare(pieces, planned, gain, weights):
    columns, width = weights[0].shape
    loose = len(pieces)
    chosen, bias = planned
    cap, tiles = chosen.shape[-2:]
    if loose > 1:
        count, lead, block = 1, (), whole
    else:
        count, lead = chosen.shape[0], (chosen.shape[0],)

        def block(shape):
            return pl.BlockSpec((None, *shape), lambda b: (b, 0, 0))

    first = [block(piece.shape[-2:]) for piece in pieces] + [block((cap, tiles)), block(bias.shape[-2:])]
    outs = [((cap, 3 * LANES), bf16), ((tiles, 2 * LANES), bf16), ((columns, cap), bf16)]
    return pl.pallas_call(
        functools.partial(prepare_kernel, loose),
        grid=(count,),
        in_specs=first + [whole((width,))] + [whole((columns, width))] * 3,
        out_specs=[block(shape) for shape, _ in outs],
        out_shape=[jax.ShapeDtypeStruct(lead + shape, kind) for shape, kind in outs],
        scratch_shapes=[pltpu.VMEM((tiles, width), bf16)],
        compiler_params=pltpu.CompilerParams(vmem_limit_bytes=16 * MIB),
        cost_estimate=pl.CostEstimate(
            flops=6 * count * tiles * width * columns, bytes_accessed=6 * width * columns, transcendentals=0
        ),
        name="prepare",
    )(*pieces, chosen, bias, gain, *weights)


def attend_kernel(n, groups, columns, *refs):
    local = refs[:groups]
    every = refs[groups : 2 * groups]
    residual = refs[2 * groups : 3 * groups]
    out_weight, mine_ref, pass_ref, send_ref, scores_sc, blocks = refs[3 * groups :]
    heads = columns // HD
    slots = mine_ref.shape[1]
    me, here = mdl_index(), seq_index()
    factor = HD ** (-0.5) * LOG2E
    zero, one = jnp.zeros((), bf16), jnp.ones((), bf16)

    def taken(sources, start, size):
        parts = [ref[..., start : start + size].reshape(-1, size) for ref in sources]
        return parts[0] if groups == 1 else jnp.concatenate(parts, axis=0)

    q = taken(local, 0, LANES)
    key_local = taken(local, LANES, LANES)
    value_local = taken(local, 2 * LANES, columns)
    lane = lax.broadcasted_iota(jnp.int32, (slots, LANES), 1)
    head_lane = lane // HD
    head_of = head_lane[:, :columns]
    row_class = lax.broadcasted_iota(jnp.int32, (slots, 1), 0) & (RATE - 1)
    inside = lane < columns
    class_lane = jnp.where(inside, head_lane & (RATE - 1), lane - columns)
    picked = jnp.where(class_lane == row_class, jnp.where(inside, q, one), zero)
    stored = groups == 1 and n > 1
    if not stored:
        scores_sparse = dot_t(picked, taken(every, 0, LANES)) * factor
        peak_sparse = jnp.max(scores_sparse, axis=1, keepdims=True)
    else:

        def first(b, peak):
            scores_sc[b] = dot_t(picked, every[0][b, :, :LANES]) * factor
            return jnp.maximum(peak, jnp.max(scores_sc[b], axis=1, keepdims=True))

        peak_sparse = lax.fori_loop(0, n, first, jnp.full((slots, 1), MASKED, f32))

    ones = jnp.where(lane == columns, one, zero)
    numerator = jnp.zeros((slots, columns), f32)
    denominator = jnp.zeros((slots, columns), f32)
    peak_shared = peak_sparse
    for h in range(heads):
        query = jnp.where(head_lane == h, q, ones)
        scores = dot_t(query, key_local) * factor
        peak = jnp.max(scores, axis=1, keepdims=True)
        has = row_class == (h & (RATE - 1))
        peak = jnp.where(has, jnp.maximum(peak, peak_sparse), peak)
        peak_shared = jnp.where(has, peak, peak_shared)
        weights = jnp.exp2(scores - peak)
        total = jnp.sum(weights, axis=1, keepdims=True)
        numerator = jnp.where(head_of == h, dot(weights.astype(bf16), value_local), numerator)
        denominator = jnp.where(head_of == h, total, denominator)
    if not stored:
        weights = jnp.exp2(scores_sparse - peak_shared)
        total = jnp.sum(weights, axis=1, keepdims=True)
        summed = dot(weights.astype(bf16), taken(every, LANES, columns))
    else:

        def second(b, carry):
            weights = jnp.exp2(scores_sc[b] - peak_shared)
            values = every[0][b, :, LANES : LANES + columns]
            return carry[0] + jnp.sum(weights, axis=1, keepdims=True), carry[1] + dot(weights.astype(bf16), values)

        total, summed = lax.fori_loop(
            0, n, second, (jnp.zeros((slots, 1), f32), jnp.zeros((slots, columns), f32))
        )
    own_class = (head_of & (RATE - 1)) == row_class
    numerator = numerator + jnp.where(own_class, summed, 0.0)
    denominator = denominator + jnp.where(own_class, total, 0.0)
    occupied = key_local[:, columns : columns + 1].astype(f32) > -1.0
    attended = jnp.where(occupied, numerator / denominator, 0.0).T.astype(bf16)
    partial = lax.dot_general(out_weight[...], attended, (((0,), (0,)), ((), ())), preferred_element_type=f32)
    for k in range(4):
        blocks[k] = partial[k * columns : (k + 1) * columns, :]
    if groups == 1:
        mine_ref[...] = blocks[me] + residual[0][...].astype(f32)
        pass_ref[...] = blocks[me ^ 2]
        send_ref[:columns, :] = blocks[me ^ 1].astype(bf16)
        send_ref[columns:, :] = blocks[me ^ 3].astype(bf16)
    else:
        cap = slots // groups
        for k in range(groups):
            there = pl.ds(pl.multiple_of((here ^ k) * cap, cap), cap)
            part = slice(k * cap, (k + 1) * cap)
            mine_ref[:, there] = blocks[me, :, part] + residual[k][...].astype(f32)
            pass_ref[:, there] = blocks[me ^ 2, :, part]
            send_ref[:columns, there] = blocks[me ^ 1, :, part].astype(bf16)
            send_ref[columns:, there] = blocks[me ^ 3, :, part].astype(bf16)


def attend(local, every, residual, out_weight, n, slots, columns):
    groups = len(local)
    tiles = every[0].shape[-2]
    stored = (n, slots, tiles) if groups == 1 and n > 1 else (1, 8, 128)
    return pl.pallas_call(
        functools.partial(attend_kernel, n, groups, columns),
        in_specs=[VMEM] * (3 * groups + 1),
        out_specs=[VMEM] * 3,
        out_shape=[
            jax.ShapeDtypeStruct((columns, slots), f32),
            jax.ShapeDtypeStruct((columns, slots), f32),
            jax.ShapeDtypeStruct((2 * columns, slots), bf16),
        ],
        scratch_shapes=[pltpu.VMEM(stored, f32), pltpu.VMEM((4, columns, slots), f32)],
        compiler_params=pltpu.CompilerParams(vmem_limit_bytes=(24 if n <= 4 else 48) * MIB),
        cost_estimate=pl.CostEstimate(
            flops=4 * slots * columns * (4 * slots + n * tiles),
            bytes_accessed=2 * n * tiles * columns,
            transcendentals=slots * (4 * slots + n * tiles),
        ),
        name="attend",
    )(*local, *every, *residual, out_weight)


def per_device(
    class_rows,
    destination,
    norm1_gain,
    gate_weight,
    up_weight,
    down_weight,
    layer_scale,
    norm2_gain,
    proj_weight,
    norm3_gain,
    query_weight,
    key_weight,
    value_weight,
    out_weight,
):
    tiles = class_rows.shape[0]
    n = lax.axis_size("seq")
    me = lax.axis_index("mdl")
    columns = query_weight.shape[1]
    slots = 2 * tiles
    cap = slots // n
    few = n <= 4

    def over_mdl(value, k):
        return lax.ppermute(value, "mdl", [(i, i ^ k) for i in range(4)])

    def over_seq(value, k):
        return lax.ppermute(value, "seq", [(i, i ^ k) for i in range(n)])

    def after(value, *earlier):
        return lax.optimization_barrier((value, *earlier))[0]

    proj = proj_weight.T
    keep, send = feed_forward(class_rows, norm1_gain, gate_weight, up_weight, down_weight)
    near = over_mdl(send, 1)
    summed = gather_sums(keep, down_weight, near)
    far = over_mdl(summed, 2)
    proj_near = over_mdl(after(proj, summed), 1)
    owner = after(destination, summed).reshape(1, tiles)
    if few:
        owners = [owner] + [over_seq(owner, k) for k in range(1, n)]
    else:
        owners = [lax.all_gather(owner, "seq", axis=0)]
    planned = plan(owners, n, cap, LANES - columns)
    embedded = embed(
        class_rows, summed, after(far, *owners, *planned[0]), layer_scale, norm2_gain, proj, proj_near
    )

    weights = (query_weight.T, key_weight.T, value_weight.T)
    if few:
        spare = after(embedded, embedded[:8, :128] + embedded[8:16, :128])
        owns = [spare] + [over_seq(spare if k == 1 else embedded, k) for k in range(1, n)]
        ready = []
        for k in range(n):
            own = owns[k]
            across = over_mdl(own, 2)
            if k == 3:
                across = after(across, ready[1][0])
            if k == 2:
                across = after(across, ready[0][0])
            pieces = [own, over_mdl(own, 1), across, over_mdl(across, 1)]
            ready.append(prepare(pieces, planned[k], norm3_gain, weights))
    else:
        sides = lax.all_gather(embedded, "mdl", axis=0).reshape(2, 2, tiles // 2, -1)
        block = sides.transpose(1, 2, 0, 3).reshape(tiles, -1)
        gathered = lax.all_gather(block, "seq", axis=0)
        ready = [prepare([gathered], planned[0], norm3_gain, weights)]

    local, every, residual = (list(items) for items in zip(*ready))
    if not few:
        residual = [residual[0].transpose(1, 0, 2).reshape(columns, slots)]
    mine, passing, others = attend(local, every, residual, out_weight, n, slots, columns)
    nearer = over_mdl(others, 1)
    farther = over_mdl((passing + nearer[columns:].astype(f32)).astype(bf16), 2)
    total = mine + nearer[:columns].astype(f32) + farther.astype(f32)
    return total.astype(bf16).T


def solution(mesh):
    return jax.shard_map(
        per_device,
        mesh=mesh,
        in_specs=(
            P(("grp", "seq"), None),
            P(("grp", "seq"), None),
            P(),
            P(None, "mdl"),
            P(None, "mdl"),
            P("mdl", None),
            P(),
            P(),
            P(None, "mdl"),
            P(),
            P(None, "mdl"),
            P(None, "mdl"),
            P(None, "mdl"),
            P("mdl", None),
        ),
        out_specs=P(("grp", "seq"), "mdl"),
        check_vma=False,
    )
```

time: 60.5 us -> 58.4 us (0.965)
  waiting for transfers between devices: 21.6 us -> 16.2 us
  starting transfers between devices: 20.1 us -> 23.5 us
  local copies, waits for them, and re-layouts: 0.32 us -> 1 us
    ppermute x6, starting transfers between devices: 8.56 us -> 13.4 us  [over_seq(): return lax.ppermute(value, 'seq', [(i, i ^ k) for i in range(n)])]
    ppermute x21 -> x17, waiting for transfers between devices: 13.9 us -> 11 us  [over_mdl(): return lax.ppermute(value, 'mdl', [(i, i ^ k) for i in range(4)])]
    ppermute x6, waiting for transfers between devices: 7.65 us -> 5.14 us  [over_seq(): return lax.ppermute(value, 'seq', [(i, i ^ k) for i in range(n)])]
    ppermute x21 -> x17, starting transfers between devices: 11.5 us -> 10.1 us  [over_mdl(): return lax.ppermute(value, 'mdl', [(i, i ^ k) for i in range(4)])]
    convert_element_type x1, other arithmetic: 1.2 us -> 0.05 us  [per_device(): farther = over_mdl((passing + nearer[columns:].astype(f32)).astype(bf16), 2)]
    unnamed x20 -> x24, local copies, waits for them, and re-layouts: 0.05 us -> 1 us
    transpose x0 -> x1, other arithmetic: none -> 0.76 us  [per_device(): return total.astype(bf16).T]
  transfers between devices with their start and end apart: 27 -> 23, of which waited for: 10 -> 9; matrix products, arithmetic and copies ran while one was open for 0% -> 0% of each run, Pallas kernels for 7% -> 6%
where the time goes in v4:
time: 58.4 us; the launch traced here: 58.2 us
  starting transfers between devices  23.5 us (40%)
  Pallas kernels  16.5 us (28%)
  waiting for transfers between devices  16.2 us (28%)
  local copies, waits for them, and re-layouts  1 us (2%)
  other arithmetic  0.81 us (1%)
    ppermute x6, starting transfers between devices, over_seq(): return lax.ppermute(value, 'seq', [(i, i ^ k) for i in range(n)])  13.4 us
    ppermute x17, waiting for transfers between devices, over_mdl(): return lax.ppermute(value, 'mdl', [(i, i ^ k) for i in range(4)])  11 us
    ppermute x17, starting transfers between devices, over_mdl(): return lax.ppermute(value, 'mdl', [(i, i ^ k) for i in range(4)])  10.1 us
    pallas_call x1, Pallas kernels, feed_forward(): pl.pallas_call(ffn_kernel, in_specs=[far, VMEM, far, far, far], out_specs...  6.46 us
    ppermute x6, waiting for transfers between devices, over_seq(): return lax.ppermute(value, 'seq', [(i, i ^ k) for i in range(n)])  5.14 us
    pallas_call x4, Pallas kernels, prepare(): pl.pallas_call(functools.partial(prepare_kernel, loose), grid=(count,), i...  4.45 us
    pallas_call x1, Pallas kernels, attend(): pl.pallas_call(functools.partial(attend_kernel, n, groups, columns), in_s...  3.73 us
  transfers between devices with their start and end apart: 23, of which 9 were waited for; matrix products, arithmetic and copies ran while one was open for 0% of the time, Pallas kernels for 6%

profile of v4, /device:TPU:0, one launch (start us, length us, event | category | flops | bytes accessed | tf_op | source)
XLA Modules:
  0.0 58.2 jit_solution(968060061393483969)
XLA Ops:
  0.0 6.5 %feed_forward.1 = (bf16[128,1024]{1,0:T(8,128)(2,1)}, bf16[128,1536]{1,0:T(8,128)(2,1)}) custom-call(bf16[256,1536]{1,0:T(8,128)(2,1)} %rows_ref.3, f32[1536]{0:T(1024)} %gain_ref.2, bf16[1536,1024]{1,0:T(8,128)(2,1)} %gate_ref.1, bf16[1536,1024]{1,0:T(8,128)(2,1)} %up_ref.1, bf16[1024,1536]{1,0:T(8,128)(2,1)} %down_ref.3), custom_call_target="tpu_custom_call" | custom-call | flops 2415919104 | bytes 9437184 | tf_op jit(solution)/shard_map/feed_forward/pallas_call | solution.py:85
  6.5 0.0 copy-start.5
  6.5 0.0 copy-start.4
  6.5 0.5 collective-permute-start
  7.0 1.6 %collective-permute-done.near_ref = bf16[128,1536]{1,0:T(8,128)(2,1)S(1)} collective-permute-done((bf16[128,1536]{1,0:T(8,128)(2,1)}, bf16[128,1536]{1,0:T(8,128)(2,1)S(1)}, u32[]{:S(2)}, u32[]{:S(2)}) %collective-permute-start) | collective-permute-done | bytes 393248 | tf_op jit(solution)/shard_map/ppermute | solution.py:406
  8.6 0.9 %copy-done.6 = bf16[128,1024]{1,0:T(8,128)(2,1)S(1)} copy-done((bf16[128,1024]{1,0:T(8,128)(2,1)S(1)}, bf16[128,1024]{1,0:T(8,128)(2,1)}, u32[]{:S(2)}) %copy-start.6) | copy-done | bytes 262168
  9.6 0.6 %gather_sums.1.here_ref = bf16[128,1536]{1,0:T(8,128)(2,1)S(1)} custom-call(bf16[128,1024]{1,0:T(8,128)(2,1)S(1)} %copy-done.6, bf16[1024,1536]{1,0:T(8,128)(2,1)S(1)} %copy-done, bf16[128,1536]{1,0:T(8,128)(2,1)S(1)} %collective-permute-done.near_ref), custom_call_target="tpu_custom_call" | custom-call | tf_op jit(solution)/shard_map/gather_sums/pallas_call | solution.py:111
  10.2 0.4 collective-permute-start.5
  10.6 2.6 %collective-permute-start.1 = (bf16[128,1536]{1,0:T(8,128)(2,1)S(1)}, bf16[128,1536]{1,0:T(8,128)(2,1)S(1)}, u32[]{:S(2)}, u32[]{:S(2)}) collective-permute-start(bf16[128,1536]{1,0:T(8,128)(2,1)S(1)} %gather_sums.1.here_ref), channel_id=1, source_target_pairs={{0,2},{1,3},{2,0},{3,1},{4,6},{5,7},{6,4},{7,5},{8,10},{9,11},{10,... | collective-permute-start | bytes 1179656 | tf_op jit(solution)/shard_map/ppermute | solution.py:406
  13.2 3.6 %collective-permute-start.4 = (s32[1,256]{1,0:T(1,128)S(1)}, s32[1,256]{1,0:T(1,128)S(1)}, u32[]{:S(2)}, u32[]{:S(2)}) collective-permute-start(s32[1,256]{1,0:T(1,128)S(1)} %bitcast.21), channel_id=1, source_target_pairs={{0,12},{4,8},{8,4},{12,0},{1,13},{5,9},{9,5},{13,1},{2,14},{6,10},... | collective-permute-start | bytes 3080 | tf_op jit(solution)/shard_map/ppermute | solution.py:409
  16.8 0.0 collective-permute-start.3
  16.8 0.8 %collective-permute-start.2 = (s32[1,256]{1,0:T(1,128)S(1)}, s32[1,256]{1,0:T(1,128)S(1)}, u32[]{:S(2)}, u32[]{:S(2)}) collective-permute-start(s32[1,256]{1,0:T(1,128)S(1)} %bitcast.23), channel_id=1, source_target_pairs={{0,4},{4,0},{8,12},{12,8},{1,5},{5,1},{9,13},{13,9},{2,6},{6,2},{1... | collective-permute-start | bytes 3080 | tf_op jit(solution)/shard_map/ppermute | solution.py:409
  17.6 1.0 %collective-permute-done.4.refs_3_ = s32[1,256]{1,0:T(1,128)S(1)} collective-permute-done((s32[1,256]{1,0:T(1,128)S(1)}, s32[1,256]{1,0:T(1,128)S(1)}, u32[]{:S(2)}, u32[]{:S(2)}) %collective-permute-start.4) | collective-permute-done | bytes 1056 | tf_op jit(solution)/shard_map/ppermute | solution.py:409
  18.6 2.7 %collective-permute-done.3.refs_2_ = s32[1,256]{1,0:T(1,128)S(1)} collective-permute-done((s32[1,256]{1,0:T(1,128)S(1)}, s32[1,256]{1,0:T(1,128)S(1)}, u32[]{:S(2)}, u32[]{:S(2)}) %collective-permute-start.3) | collective-permute-done | bytes 1056 | tf_op jit(solution)/shard_map/ppermute | solution.py:409
  21.3 0.0 collective-permute-done.2.refs_1_
  21.3 0.4 plan.1
  21.7 1.1 %collective-permute-done.1.far_ref = bf16[128,1536]{1,0:T(8,128)(2,1)S(1)} collective-permute-done((bf16[128,1536]{1,0:T(8,128)(2,1)S(1)}, bf16[128,1536]{1,0:T(8,128)(2,1)S(1)}, u32[]{:S(2)}, u32[]{:S(2)}) %collective-permute-start.1) | collective-permute-done | bytes 393248 | tf_op jit(solution)/shard_map/ppermute | solution.py:406
  22.9 0.0 collective-permute-done.5.near
  22.9 0.9 %embed.1.refs_0_ = bf16[128,384]{1,0:T(8,128)(2,1)S(1)} custom-call(bf16[256,1536]{1,0:T(8,128)(2,1)S(1)} %copy-done.4, bf16[128,1536]{1,0:T(8,128)(2,1)S(1)} %gather_sums.1.here_ref, bf16[128,1536]{1,0:T(8,128)(2,1)S(1)} %collective-permute-done.1.far_ref, f32[1536]{0:T(1024)S(1)} %copy-done.8, f32[1536]{0:T(1024)S(1)} %copy-done.9, ...), custom_call_target="tpu_custom_call" | custom-call | flops 150994944 | bytes 1179648 | tf_op jit(solution)/shard_map/embed/pallas_call | solution.py:137
  23.8 0.0 copy-start.11
  23.8 1.9 %collective-permute-start.9 = (bf16[128,384]{1,0:T(8,128)(2,1)S(1)}, bf16[128,384]{1,0:T(8,128)(2,1)S(1)}, u32[]{:S(2)}, u32[]{:S(2)}) collective-permute-start(bf16[128,384]{1,0:T(8,128)(2,1)S(1)} %embed.1.refs_0_), channel_id=1, source_target_pairs={{0,4},{4,0},{8,12},{12,8},{1,5},{5,1},{9,13},{13,9},{2,6},{6,2},{1... | collective-permute-start | bytes 294920 | tf_op jit(solution)/shard_map/ppermute | solution.py:409
  25.7 1.5 %collective-permute-start.7 = (bf16[128,384]{1,0:T(8,128)(2,1)S(1)}, bf16[128,384]{1,0:T(8,128)(2,1)S(1)}, u32[]{:S(2)}, u32[]{:S(2)}) collective-permute-start(bf16[128,384]{1,0:T(8,128)(2,1)S(1)} %embed.1.refs_0_), channel_id=1, source_target_pairs={{0,2},{1,3},{2,0},{3,1},{4,6},{5,7},{6,4},{7,5},{8,10},{9,11},{10,... | collective-permute-start | bytes 294920 | tf_op jit(solution)/shard_map/ppermute | solution.py:406
  27.2 2.6 %collective-permute-start.13 = (bf16[128,384]{1,0:T(8,128)(2,1)S(1)}, bf16[128,384]{1,0:T(8,128)(2,1)S(1)}, u32[]{:S(2)}, u32[]{:S(2)}) collective-permute-start(bf16[128,384]{1,0:T(8,128)(2,1)S(1)} %embed.1.refs_0_), channel_id=1, source_target_pairs={{0,8},{4,12},{8,0},{12,4},{1,9},{5,13},{9,1},{13,5},{2,10},{6,14},... | collective-permute-start | bytes 294920 | tf_op jit(solution)/shard_map/ppermute | solution.py:409
  29.8 0.0 collective-permute-start.6
  29.8 0.0 collective-permute-done.9.refs_0_
  29.8 0.5 collective-permute-start.11
  30.3 4.5 %collective-permute-start.17 = (bf16[128,384]{1,0:T(8,128)(2,1)S(1)}, bf16[128,384]{1,0:T(8,128)(2,1)S(1)}, u32[]{:S(2)}, u32[]{:S(2)}) collective-permute-start(bf16[128,384]{1,0:T(8,128)(2,1)S(1)} %embed.1.refs_0_), channel_id=1, source_target_pairs={{0,12},{4,8},{8,4},{12,0},{1,13},{5,9},{9,5},{13,1},{2,14},{6,10},... | collective-permute-start | bytes 294920 | tf_op jit(solution)/shard_map/ppermute | solution.py:409
  34.8 0.0 collective-permute-done.7.refs_2_
  34.8 0.0 collective-permute-start.8
  34.8 0.0 collective-permute-done.13.refs_0_
  34.8 0.7 %collective-permute-start.15 = (bf16[128,384]{1,0:T(8,128)(2,1)S(1)}, bf16[128,384]{1,0:T(8,128)(2,1)S(1)}, u32[]{:S(2)}, u32[]{:S(2)}) collective-permute-start(bf16[128,384]{1,0:T(8,128)(2,1)S(1)} %collective-permute-done.13.refs_0_), channel_id=1, source_target_pairs={{0,2},{1,3},{2,0},{3,1},{4,6},{5,7},{6,4},{7,5},{8,10},{9,11},{10,... | collective-permute-start | bytes 294920 | tf_op jit(solution)/shard_map/ppermute | solution.py:406
  35.5 0.0 collective-permute-done.6.refs_1_
  35.5 0.2 collective-permute-start.10
  35.7 0.0 collective-permute-done.11.refs_2_
  35.7 0.3 collective-permute-start.12
  36.0 1.4 %collective-permute-done.17.refs_0_ = bf16[128,384]{1,0:T(8,128)(2,1)S(1)} collective-permute-done((bf16[128,384]{1,0:T(8,128)(2,1)S(1)}, bf16[128,384]{1,0:T(8,128)(2,1)S(1)}, u32[]{:S(2)}, u32[]{:S(2)}) %collective-permute-start.17) | collective-permute-done | bytes 98336 | tf_op jit(solution)/shard_map/ppermute | solution.py:409
  37.5 1.2 %collective-permute-start.19 = (bf16[128,384]{1,0:T(8,128)(2,1)S(1)}, bf16[128,384]{1,0:T(8,128)(2,1)S(1)}, u32[]{:S(2)}, u32[]{:S(2)}) collective-permute-start(bf16[128,384]{1,0:T(8,128)(2,1)S(1)} %collective-permute-done.17.refs_0_), channel_id=1, source_target_pairs={{0,2},{1,3},{2,0},{3,1},{4,6},{5,7},{6,4},{7,5},{8,10},{9,11},{10,... | collective-permute-start | bytes 294920 | tf_op jit(solution)/shard_map/ppermute | solution.py:406
  38.6 0.0 collective-permute-done.8.refs_3_
  38.6 0.0 collective-permute-start.18
  38.7 0.0 copy-done.2
  38.7 0.0 copy-done.3
  38.7 0.0 copy-done.7
  38.7 1.1 %prepare.4 = (bf16[128,768]{1,0:T(8,128)(2,1)S(1)}, bf16[256,512]{1,0:T(8,128)(2,1)S(1)}, bf16[192,128]{1,0:T(8,128)(2,1)S(1)}) custom-call(bf16[128,384]{1,0:T(8,128)(2,1)S(1)} %embed.1.refs_0_, bf16[128,384]{1,0:T(8,128)(2,1)S(1)} %collective-permute-done.6.refs_1_, bf16[128,384]{1,0:T(8,128)(2,1)S(1)} %collective-permute-done.7.refs_2_, ...), custom_call_target="tpu_custom_call" | custom-call | flops 226492416 | bytes 884736 | tf_op jit(solution)/shard_map/prepare/pallas_call | solution.py:252
  39.8 0.7 %collective-permute-done.15.refs_2_ = bf16[128,384]{1,0:T(8,128)(2,1)S(1)} collective-permute-done((bf16[128,384]{1,0:T(8,128)(2,1)S(1)}, bf16[128,384]{1,0:T(8,128)(2,1)S(1)}, u32[]{:S(2)}, u32[]{:S(2)}) %collective-permute-start.15) | collective-permute-done | bytes 98336 | tf_op jit(solution)/shard_map/ppermute | solution.py:406
  40.5 0.0 collective-permute-start.14
  40.5 0.0 collective-permute-done.10.refs_1_
  40.5 0.5 collective-permute-start.16
  41.0 0.0 collective-permute-done.12.refs_3_
  41.0 1.1 %prepare.5 = (bf16[128,768]{1,0:T(8,128)(2,1)S(1)}, bf16[256,512]{1,0:T(8,128)(2,1)S(1)}, bf16[192,128]{1,0:T(8,128)(2,1)S(1)}) custom-call(bf16[128,384]{1,0:T(8,128)(2,1)S(1)} %collective-permute-done.9.refs_0_, bf16[128,384]{1,0:T(8,128)(2,1)S(1)} %collective-permute-done.10.refs_1_, bf16[128,384]{1,0:T(8,128)(2,1)S(1)} %collective-permute-done.11.refs_2_, ...), custom_call_target="tpu_custom_call" | custom-call | flops 226492416 | bytes 884736 | tf_op jit(solution)/shard_map/prepare/pallas_call | solution.py:252
  42.1 0.0 collective-permute-done.19.refs_2_
  42.1 0.1 collective-permute-start.20
  42.2 0.0 collective-permute-done.14.refs_1_
  42.2 0.0 collective-permute-done.16.refs_3_
  42.2 1.1 %prepare.6 = (bf16[128,768]{1,0:T(8,128)(2,1)S(1)}, bf16[256,512]{1,0:T(8,128)(2,1)S(1)}, bf16[192,128]{1,0:T(8,128)(2,1)S(1)}) custom-call(bf16[128,384]{1,0:T(8,128)(2,1)S(1)} %collective-permute-done.13.refs_0_, bf16[128,384]{1,0:T(8,128)(2,1)S(1)} %collective-permute-done.14.refs_1_, bf16[128,384]{1,0:T(8,128)(2,1)S(1)} %collective-permute-done.15.refs_2_, ...), custom_call_target="tpu_custom_call" | custom-call | flops 226492416 | bytes 884736 | tf_op jit(solution)/shard_map/prepare/pallas_call | solution.py:252
  43.4 0.0 collective-permute-done.18.refs_1_
  43.4 0.1 collective-permute-done.20.refs_3_
  43.5 1.1 %prepare.7 = (bf16[128,768]{1,0:T(8,128)(2,1)S(1)}, bf16[256,512]{1,0:T(8,128)(2,1)S(1)}, bf16[192,128]{1,0:T(8,128)(2,1)S(1)}) custom-call(bf16[128,384]{1,0:T(8,128)(2,1)S(1)} %collective-permute-done.17.refs_0_, bf16[128,384]{1,0:T(8,128)(2,1)S(1)} %collective-permute-done.18.refs_1_, bf16[128,384]{1,0:T(8,128)(2,1)S(1)} %collective-permute-done.19.refs_2_, ...), custom_call_target="tpu_custom_call" | custom-call | flops 226492416 | bytes 884736 | tf_op jit(solution)/shard_map/prepare/pallas_call | solution.py:252
  44.6 3.7 %attend.1 = (f32[192,512]{1,0:T(8,128)S(1)}, f32[192,512]{1,0:T(8,128)S(1)}, bf16[384,512]{1,0:T(8,128)(2,1)S(1)}) custom-call(bf16[128,768]{1,0:T(8,128)(2,1)S(1)} %get-tuple-element.42.refs_0_, bf16[128,768]{1,0:T(8,128)(2,1)S(1)} %get-tuple-element.45.refs_1_, bf16[128,768]{1,0:T(8,128)(2,1)S(1)} %get-tuple-element.49.refs_2_, ...), custom_call_target="tpu_custom_call" | custom-call | flops 1207959552 | bytes 393216 | tf_op jit(solution)/shard_map/attend/pallas_call | solution.py:361
  48.4 0.4 collective-permute-start.21
  48.8 1.4 %collective-permute-done.21 = bf16[384,512]{1,0:T(8,128)(2,1)S(1)} collective-permute-done((bf16[384,512]{1,0:T(8,128)(2,1)S(1)}, bf16[384,512]{1,0:T(8,128)(2,1)S(1)}, u32[]{:S(2)}, u32[]{:S(2)}) %collective-permute-start.21) | collective-permute-done | bytes 393248 | tf_op jit(solution)/shard_map/ppermute | solution.py:406
  50.1 0.1 add_convert_fusion.1
  50.2 1.1 %collective-permute-start.22 = (bf16[192,512]{1,0:T(8,128)(2,1)S(1)}, bf16[192,512]{1,0:T(8,128)(2,1)S(1)}, u32[]{:S(2)}, u32[]{:S(2)}) collective-permute-start(bf16[192,512]{1,0:T(8,128)(2,1)S(1)} %add_convert_fusion.1), channel_id=1, source_target_pairs={{0,2},{1,3},{2,0},{3,1},{4,6},{5,7},{6,4},{7,5},{8,10},{9,11},{10,... | collective-permute-start | bytes 589832 | tf_op jit(solution)/shard_map/ppermute | solution.py:406
  51.3 6.1 %collective-permute-done.22 = bf16[192,512]{1,0:T(8,128)(2,1)S(1)} collective-permute-done((bf16[192,512]{1,0:T(8,128)(2,1)S(1)}, bf16[192,512]{1,0:T(8,128)(2,1)S(1)}, u32[]{:S(2)}, u32[]{:S(2)}) %collective-permute-start.22) | collective-permute-done | bytes 196640 | tf_op jit(solution)/shard_map/ppermute | solution.py:406
  57.4 0.8 %fusion = bf16[512,192]{0,1:T(8,128)(2,1)} fusion(bf16[192,512]{1,0:T(8,128)(2,1)S(1)} %collective-permute-done.22, f32[192,512]{1,0:T(8,128)S(1)} %get-tuple-element.62, bf16[384,512]{1,0:T(8,128)(2,1)S(1)} %collective-permute-done.21), kind=kLoop, calls=%fused_computation.2 | loop fusion | flops 491520 | bytes 983040 | tf_op jit(solution)/shard_map/transpose | solution.py:457
  (17 shorter events, 0.0 us)
Async XLA Ops:
  0.0 8.6 %copy-start = (bf16[1024,1536]{1,0:T(8,128)(2,1)S(1)}, bf16[1024,1536]{1,0:T(8,128)(2,1)}, u32[]{:S(2)}) copy-start(bf16[1024,1536]{1,0:T(8,128)(2,1)} %down_ref.3) | copy-start | bytes 9437188
  0.0 13.2 %copy-start.10 = (s32[256,1]{0,1:T(1,128)S(1)}, s32[256,1]{0,1:T(1,128)}, u32[]{:S(2)}) copy-start(s32[256,1]{0,1:T(1,128)} %param.15) | copy-start | bytes 3076
  0.0 22.9 %copy-start.8 = (f32[1536]{0:T(1024)S(1)}, f32[1536]{0:T(1024)}, u32[]{:S(2)}) copy-start(f32[1536]{0:T(1024)} %scale_ref.1) | copy-start | bytes 18436
  0.0 22.9 %copy-start.9 = (f32[1536]{0:T(1024)S(1)}, f32[1536]{0:T(1024)}, u32[]{:S(2)}) copy-start(f32[1536]{0:T(1024)} %gain_ref.3) | copy-start | bytes 18436
  6.5 3.7 %copy-start.5 = (bf16[1536,192]{0,1:T(8,128)(2,1)S(1)}, bf16[1536,192]{0,1:T(8,128)(2,1)}, u32[]{:S(2)}) copy-start(bf16[1536,192]{0,1:T(8,128)(2,1)} %param.22) | copy-start | bytes 1769476
  6.5 16.4 %copy-start.4 = (bf16[256,1536]{1,0:T(8,128)(2,1)S(1)}, bf16[256,1536]{1,0:T(8,128)(2,1)}, u32[]{:S(2)}) copy-start(bf16[256,1536]{1,0:T(8,128)(2,1)} %rows_ref.3) | copy-start | bytes 2359300
  6.5 2.1 %collective-permute-start = (bf16[128,1536]{1,0:T(8,128)(2,1)}, bf16[128,1536]{1,0:T(8,128)(2,1)S(1)}, u32[]{:S(2)}, u32[]{:S(2)}) collective-permute-start(bf16[128,1536]{1,0:T(8,128)(2,1)} %get-tuple-element.36), channel_id=1, source_target_pairs={{0,1},{1,0},{2,3},{3,2},{4,5},{5,4},{6,7},{7,6},{8,9},{9,8},{10,11... | collective-permute-start | bytes 1179656 | tf_op jit(solution)/shard_map/ppermute | solution.py:406
  8.6 1.0 %copy-start.6 = (bf16[128,1024]{1,0:T(8,128)(2,1)S(1)}, bf16[128,1024]{1,0:T(8,128)(2,1)}, u32[]{:S(2)}) copy-start(bf16[128,1024]{1,0:T(8,128)(2,1)} %get-tuple-element.35.hidden_ref) | copy-start | bytes 786436
  9.5 29.1 %copy-start.1 = (bf16[768,192]{0,1:T(8,128)(2,1)S(1)}, bf16[768,192]{0,1:T(8,128)(2,1)}, u32[]{:S(2)}) copy-start(bf16[768,192]{0,1:T(8,128)(2,1)} %param.24) | copy-start | bytes 884740
  9.5 29.1 %copy-start.2 = (bf16[768,192]{0,1:T(8,128)(2,1)S(1)}, bf16[768,192]{0,1:T(8,128)(2,1)}, u32[]{:S(2)}) copy-start(bf16[768,192]{0,1:T(8,128)(2,1)} %param.25) | copy-start | bytes 884740
  9.5 29.1 %copy-start.3 = (bf16[768,192]{0,1:T(8,128)(2,1)S(1)}, bf16[768,192]{0,1:T(8,128)(2,1)}, u32[]{:S(2)}) copy-start(bf16[768,192]{0,1:T(8,128)(2,1)} %param.26) | copy-start | bytes 884740
  9.5 29.1 %copy-start.7 = (f32[768]{0:T(1024)S(1)}, f32[768]{0:T(1024)}, u32[]{:S(2)}) copy-start(f32[768]{0:T(1024)} %refs_6_.7) | copy-start | bytes 9220
  10.2 12.7 %collective-permute-start.5 = (bf16[192,1536]{1,0:T(8,128)(2,1)S(1)}, bf16[192,1536]{1,0:T(8,128)(2,1)S(1)}, u32[]{:S(2)}, u32[]{:S(2)}) collective-permute-start(bf16[192,1536]{1,0:T(8,128)(2,1)S(1)} %bitcast.19), channel_id=1, source_target_pairs={{0,1},{1,0},{2,3},{3,2},{4,5},{5,4},{6,7},{7,6},{8,9},{9,8},{10,11... | collective-permute-start | bytes 1769480 | tf_op jit(solution)/shard_map/ppermute | solution.py:406
  10.6 12.3 %collective-permute-start.1 = (bf16[128,1536]{1,0:T(8,128)(2,1)S(1)}, bf16[128,1536]{1,0:T(8,128)(2,1)S(1)}, u32[]{:S(2)}, u32[]{:S(2)}) collective-permute-start(bf16[128,1536]{1,0:T(8,128)(2,1)S(1)} %gather_sums.1.here_ref), channel_id=1, source_target_pairs={{0,2},{1,3},{2,0},{3,1},{4,6},{5,7},{6,4},{7,5},{8,10},{9,11},{10,... | collective-permute-start | bytes 1179656 | tf_op jit(solution)/shard_map/ppermute | solution.py:406
  13.2 5.4 %collective-permute-start.4 = (s32[1,256]{1,0:T(1,128)S(1)}, s32[1,256]{1,0:T(1,128)S(1)}, u32[]{:S(2)}, u32[]{:S(2)}) collective-permute-start(s32[1,256]{1,0:T(1,128)S(1)} %bitcast.21), channel_id=1, source_target_pairs={{0,12},{4,8},{8,4},{12,0},{1,13},{5,9},{9,5},{13,1},{2,14},{6,10},... | collective-permute-start | bytes 3080 | tf_op jit(solution)/shard_map/ppermute | solution.py:409
  16.8 4.5 %collective-permute-start.3 = (s32[1,256]{1,0:T(1,128)S(1)}, s32[1,256]{1,0:T(1,128)S(1)}, u32[]{:S(2)}, u32[]{:S(2)}) collective-permute-start(s32[1,256]{1,0:T(1,128)S(1)} %bitcast.22), channel_id=1, source_target_pairs={{0,8},{4,12},{8,0},{12,4},{1,9},{5,13},{9,1},{13,5},{2,10},{6,14},... | collective-permute-start | bytes 3080 | tf_op jit(solution)/shard_map/ppermute | solution.py:409
  16.8 4.5 %collective-permute-start.2 = (s32[1,256]{1,0:T(1,128)S(1)}, s32[1,256]{1,0:T(1,128)S(1)}, u32[]{:S(2)}, u32[]{:S(2)}) collective-permute-start(s32[1,256]{1,0:T(1,128)S(1)} %bitcast.23), channel_id=1, source_target_pairs={{0,4},{4,0},{8,12},{12,8},{1,5},{5,1},{9,13},{13,9},{2,6},{6,2},{1... | collective-permute-start | bytes 3080 | tf_op jit(solution)/shard_map/ppermute | solution.py:409
  23.8 20.8 %copy-start.11 = (bf16[192,768]{1,0:T(8,128)(2,1)S(1)}, bf16[192,768]{1,0:T(8,128)(2,1)}, u32[]{:S(2)}) copy-start(bf16[192,768]{1,0:T(8,128)(2,1)} %refs_12_.1) | copy-start | bytes 884740
  23.8 6.0 %collective-permute-start.9 = (bf16[128,384]{1,0:T(8,128)(2,1)S(1)}, bf16[128,384]{1,0:T(8,128)(2,1)S(1)}, u32[]{:S(2)}, u32[]{:S(2)}) collective-permute-start(bf16[128,384]{1,0:T(8,128)(2,1)S(1)} %embed.1.refs_0_), channel_id=1, source_target_pairs={{0,4},{4,0},{8,12},{12,8},{1,5},{5,1},{9,13},{13,9},{2,6},{6,2},{1... | collective-permute-start | bytes 294920 | tf_op jit(solution)/shard_map/ppermute | solution.py:409
  25.7 9.1 %collective-permute-start.7 = (bf16[128,384]{1,0:T(8,128)(2,1)S(1)}, bf16[128,384]{1,0:T(8,128)(2,1)S(1)}, u32[]{:S(2)}, u32[]{:S(2)}) collective-permute-start(bf16[128,384]{1,0:T(8,128)(2,1)S(1)} %embed.1.refs_0_), channel_id=1, source_target_pairs={{0,2},{1,3},{2,0},{3,1},{4,6},{5,7},{6,4},{7,5},{8,10},{9,11},{10,... | collective-permute-start | bytes 294920 | tf_op jit(solution)/shard_map/ppermute | solution.py:406
  27.2 7.6 %collective-permute-start.13 = (bf16[128,384]{1,0:T(8,128)(2,1)S(1)}, bf16[128,384]{1,0:T(8,128)(2,1)S(1)}, u32[]{:S(2)}, u32[]{:S(2)}) collective-permute-start(bf16[128,384]{1,0:T(8,128)(2,1)S(1)} %embed.1.refs_0_), channel_id=1, source_target_pairs={{0,8},{4,12},{8,0},{12,4},{1,9},{5,13},{9,1},{13,5},{2,10},{6,14},... | collective-permute-start | bytes 294920 | tf_op jit(solution)/shard_map/ppermute | solution.py:409
  29.8 5.7 %collective-permute-start.6 = (bf16[128,384]{1,0:T(8,128)(2,1)S(1)}, bf16[128,384]{1,0:T(8,128)(2,1)S(1)}, u32[]{:S(2)}, u32[]{:S(2)}) collective-permute-start(bf16[128,384]{1,0:T(8,128)(2,1)S(1)} %embed.1.refs_0_), channel_id=1, source_target_pairs={{0,1},{1,0},{2,3},{3,2},{4,5},{5,4},{6,7},{7,6},{8,9},{9,8},{10,11... | collective-permute-start | bytes 294920 | tf_op jit(solution)/shard_map/ppermute | solution.py:406
  29.8 5.9 %collective-permute-start.11 = (bf16[128,384]{1,0:T(8,128)(2,1)S(1)}, bf16[128,384]{1,0:T(8,128)(2,1)S(1)}, u32[]{:S(2)}, u32[]{:S(2)}) collective-permute-start(bf16[128,384]{1,0:T(8,128)(2,1)S(1)} %collective-permute-done.9.refs_0_), channel_id=1, source_target_pairs={{0,2},{1,3},{2,0},{3,1},{4,6},{5,7},{6,4},{7,5},{8,10},{9,11},{10,... | collective-permute-start | bytes 294920 | tf_op jit(solution)/shard_map/ppermute | solution.py:406
  30.3 7.1 %collective-permute-start.17 = (bf16[128,384]{1,0:T(8,128)(2,1)S(1)}, bf16[128,384]{1,0:T(8,128)(2,1)S(1)}, u32[]{:S(2)}, u32[]{:S(2)}) collective-permute-start(bf16[128,384]{1,0:T(8,128)(2,1)S(1)} %embed.1.refs_0_), channel_id=1, source_target_pairs={{0,12},{4,8},{8,4},{12,0},{1,13},{5,9},{9,5},{13,1},{2,14},{6,10},... | collective-permute-start | bytes 294920 | tf_op jit(solution)/shard_map/ppermute | solution.py:409
  34.8 3.8 %collective-permute-start.8 = (bf16[128,384]{1,0:T(8,128)(2,1)S(1)}, bf16[128,384]{1,0:T(8,128)(2,1)S(1)}, u32[]{:S(2)}, u32[]{:S(2)}) collective-permute-start(bf16[128,384]{1,0:T(8,128)(2,1)S(1)} %collective-permute-done.7.refs_2_), channel_id=1, source_target_pairs={{0,1},{1,0},{2,3},{3,2},{4,5},{5,4},{6,7},{7,6},{8,9},{9,8},{10,11... | collective-permute-start | bytes 294920 | tf_op jit(solution)/shard_map/ppermute | solution.py:406
  34.8 5.7 %collective-permute-start.15 = (bf16[128,384]{1,0:T(8,128)(2,1)S(1)}, bf16[128,384]{1,0:T(8,128)(2,1)S(1)}, u32[]{:S(2)}, u32[]{:S(2)}) collective-permute-start(bf16[128,384]{1,0:T(8,128)(2,1)S(1)} %collective-permute-done.13.refs_0_), channel_id=1, source_target_pairs={{0,2},{1,3},{2,0},{3,1},{4,6},{5,7},{6,4},{7,5},{8,10},{9,11},{10,... | collective-permute-start | bytes 294920 | tf_op jit(solution)/shard_map/ppermute | solution.py:406
  35.5 5.0 %collective-permute-start.10 = (bf16[128,384]{1,0:T(8,128)(2,1)S(1)}, bf16[128,384]{1,0:T(8,128)(2,1)S(1)}, u32[]{:S(2)}, u32[]{:S(2)}) collective-permute-start(bf16[128,384]{1,0:T(8,128)(2,1)S(1)} %collective-permute-done.9.refs_0_), channel_id=1, source_target_pairs={{0,1},{1,0},{2,3},{3,2},{4,5},{5,4},{6,7},{7,6},{8,9},{9,8},{10,11... | collective-permute-start | bytes 294920 | tf_op jit(solution)/shard_map/ppermute | solution.py:406
  35.7 5.3 %collective-permute-start.12 = (bf16[128,384]{1,0:T(8,128)(2,1)S(1)}, bf16[128,384]{1,0:T(8,128)(2,1)S(1)}, u32[]{:S(2)}, u32[]{:S(2)}) collective-permute-start(bf16[128,384]{1,0:T(8,128)(2,1)S(1)} %collective-permute-done.11.refs_2_), channel_id=1, source_target_pairs={{0,1},{1,0},{2,3},{3,2},{4,5},{5,4},{6,7},{7,6},{8,9},{9,8},{10,11... | collective-permute-start | bytes 294920 | tf_op jit(solution)/shard_map/ppermute | solution.py:406
  37.5 4.7 %collective-permute-start.19 = (bf16[128,384]{1,0:T(8,128)(2,1)S(1)}, bf16[128,384]{1,0:T(8,128)(2,1)S(1)}, u32[]{:S(2)}, u32[]{:S(2)}) collective-permute-start(bf16[128,384]{1,0:T(8,128)(2,1)S(1)} %collective-permute-done.17.refs_0_), channel_id=1, source_target_pairs={{0,2},{1,3},{2,0},{3,1},{4,6},{5,7},{6,4},{7,5},{8,10},{9,11},{10,... | collective-permute-start | bytes 294920 | tf_op jit(solution)/shard_map/ppermute | solution.py:406
  38.6 4.7 %collective-permute-start.18 = (bf16[128,384]{1,0:T(8,128)(2,1)S(1)}, bf16[128,384]{1,0:T(8,128)(2,1)S(1)}, u32[]{:S(2)}, u32[]{:S(2)}) collective-permute-start(bf16[128,384]{1,0:T(8,128)(2,1)S(1)} %collective-permute-done.17.refs_0_), channel_id=1, source_target_pairs={{0,1},{1,0},{2,3},{3,2},{4,5},{5,4},{6,7},{7,6},{8,9},{9,8},{10,11... | collective-permute-start | bytes 294920 | tf_op jit(solution)/shard_map/ppermute | solution.py:406
  40.5 1.7 %collective-permute-start.14 = (bf16[128,384]{1,0:T(8,128)(2,1)S(1)}, bf16[128,384]{1,0:T(8,128)(2,1)S(1)}, u32[]{:S(2)}, u32[]{:S(2)}) collective-permute-start(bf16[128,384]{1,0:T(8,128)(2,1)S(1)} %collective-permute-done.13.refs_0_), channel_id=1, source_target_pairs={{0,1},{1,0},{2,3},{3,2},{4,5},{5,4},{6,7},{7,6},{8,9},{9,8},{10,11... | collective-permute-start | bytes 294920 | tf_op jit(solution)/shard_map/ppermute | solution.py:406
  40.5 1.7 %collective-permute-start.16 = (bf16[128,384]{1,0:T(8,128)(2,1)S(1)}, bf16[128,384]{1,0:T(8,128)(2,1)S(1)}, u32[]{:S(2)}, u32[]{:S(2)}) collective-permute-start(bf16[128,384]{1,0:T(8,128)(2,1)S(1)} %collective-permute-done.15.refs_2_), channel_id=1, source_target_pairs={{0,1},{1,0},{2,3},{3,2},{4,5},{5,4},{6,7},{7,6},{8,9},{9,8},{10,11... | collective-permute-start | bytes 294920 | tf_op jit(solution)/shard_map/ppermute | solution.py:406
  42.1 1.4 %collective-permute-start.20 = (bf16[128,384]{1,0:T(8,128)(2,1)S(1)}, bf16[128,384]{1,0:T(8,128)(2,1)S(1)}, u32[]{:S(2)}, u32[]{:S(2)}) collective-permute-start(bf16[128,384]{1,0:T(8,128)(2,1)S(1)} %collective-permute-done.19.refs_2_), channel_id=1, source_target_pairs={{0,1},{1,0},{2,3},{3,2},{4,5},{5,4},{6,7},{7,6},{8,9},{9,8},{10,11... | collective-permute-start | bytes 294920 | tf_op jit(solution)/shard_map/ppermute | solution.py:406
  48.4 1.8 %collective-permute-start.21 = (bf16[384,512]{1,0:T(8,128)(2,1)S(1)}, bf16[384,512]{1,0:T(8,128)(2,1)S(1)}, u32[]{:S(2)}, u32[]{:S(2)}) collective-permute-start(bf16[384,512]{1,0:T(8,128)(2,1)S(1)} %get-tuple-element.63), channel_id=1, source_target_pairs={{0,1},{1,0},{2,3},{3,2},{4,5},{5,4},{6,7},{7,6},{8,9},{9,8},{10,11... | collective-permute-start | bytes 1179656 | tf_op jit(solution)/shard_map/ppermute | solution.py:406
  50.2 7.2 %collective-permute-start.22 = (bf16[192,512]{1,0:T(8,128)(2,1)S(1)}, bf16[192,512]{1,0:T(8,128)(2,1)S(1)}, u32[]{:S(2)}, u32[]{:S(2)}) collective-permute-start(bf16[192,512]{1,0:T(8,128)(2,1)S(1)} %add_convert_fusion.1), channel_id=1, source_target_pairs={{0,2},{1,3},{2,0},{3,1},{4,6},{5,7},{6,4},{7,5},{8,10},{9,11},{10,... | collective-permute-start | bytes 589832 | tf_op jit(solution)/shard_map/ppermute | solution.py:406

commit v5 on v4

--- a/solution.py
+++ b/solution.py
@@ -72,9 +72,9 @@
     opened = opened * jax.nn.sigmoid(opened)
     copies[2].wait()
     hidden = (opened * dot(normed[...], upward[...])).astype(bf16)
-    keep_ref[...] = hidden[:half, :]
     copies[3].wait()
     send_ref[...] = dot(hidden[half:, :], down[...]).astype(bf16)
+    keep_ref[...] = dot(hidden[:half, :], down[...]).astype(bf16)
 
 
 def feed_forward(rows, gain, gate_weight, up_weight, down_weight):
@@ -86,7 +86,7 @@
         ffn_kernel,
         in_specs=[far, VMEM, far, far, far],
         out_specs=[VMEM, VMEM],
-        out_shape=[jax.ShapeDtypeStruct((half, hidden), bf16), jax.ShapeDtypeStruct((half, width), bf16)],
+        out_shape=[jax.ShapeDtypeStruct((half, width), bf16)] * 2,
         scratch_shapes=[
             pltpu.VMEM((tiles, width), bf16),
             pltpu.VMEM((width, hidden), bf16),
@@ -95,7 +95,7 @@
             pltpu.VMEM((tiles, width), bf16),
             pltpu.SemaphoreType.DMA((4,)),
         ],
-        compiler_params=pltpu.CompilerParams(vmem_limit_bytes=60 * MIB),
+        compiler_params=pltpu.CompilerParams(vmem_limit_bytes=105 * MIB // 2),
         cost_estimate=pl.CostEstimate(
             flops=6 * tiles * width * hidden, bytes_accessed=6 * width * hidden, transcendentals=tiles * hidden
         ),
@@ -103,19 +103,19 @@
     )(rows, gain, gate_weight, up_weight, down_weight)
 
 
-def gather_kernel(hidden_ref, down_ref, near_ref, out_ref):
-    out_ref[...] = (dot(hidden_ref[...], down_ref[...]) + near_ref[...].astype(f32)).astype(bf16)
-
-
-def gather_sums(hidden, down_weight, near):
+def gather_kernel(keep_ref, near_ref, out_ref):
+    out_ref[...] = (keep_ref[...].astype(f32) + near_ref[...].astype(f32)).astype(bf16)
+
+
+def gather_sums(keep, near):
     return pl.pallas_call(
         gather_kernel,
-        in_specs=[VMEM] * 3,
+        in_specs=[VMEM] * 2,
         out_specs=VMEM,
         out_shape=jax.ShapeDtypeStruct(near.shape, bf16),
         compiler_params=pltpu.CompilerParams(vmem_limit_bytes=16 * MIB),
         name="gather_sums",
-    )(hidden, down_weight, near)
+    )(keep, near)
 
 
 def embed_kernel(rows_ref, here_ref, far_ref, scale_ref, gain_ref, own, near, out_ref, blocks):
@@ -196,7 +196,7 @@
 
 def prepare_kernel(loose, *refs):
     pieces = refs[:loose]
-    chosen_ref, bias_ref, gain_ref, wq, wk, wv, local_ref, all_ref, residual_ref, block = refs[loose:]
+    chosen_ref, bias_ref, gain_ref, wq, wk, wv, local_ref, all_ref, block = refs[loose:]
     me = mdl_index()
     tiles, width = block.shape
     columns = wq.shape[0]
@@ -211,12 +211,6 @@
         rows = pieces[0][...]
     chosen = chosen_ref[...]
     cap = chosen.shape[0]
-    mine = (
-        lax.broadcasted_iota(jnp.int32, (columns, width), 1)
-        == lax.broadcasted_iota(jnp.int32, (columns, width), 0) + me * columns
-    )
-    picked = jnp.where(mine, 1.0, 0.0).astype(bf16)
-    residual_ref[...] = dot_t(dot_t(picked, rows).astype(bf16), chosen).astype(bf16)
     normed = layer_norm(rows.astype(f32), row(gain_ref)).astype(bf16)
     queries = dot_t(normed, wq[...]).astype(bf16)
     keys = dot_t(normed, wk[...]).astype(bf16)
@@ -248,7 +242,7 @@
             return pl.BlockSpec((None, *shape), lambda b: (b, 0, 0))
 
     first = [block(piece.shape[-2:]) for piece in pieces] + [block((cap, tiles)), block(bias.shape[-2:])]
-    outs = [((cap, 3 * LANES), bf16), ((tiles, 2 * LANES), bf16), ((columns, cap), bf16)]
+    outs = [((cap, 3 * LANES), bf16), ((tiles, 2 * LANES), bf16)]
     return pl.pallas_call(
         functools.partial(prepare_kernel, loose),
         grid=(count,),
@@ -267,8 +261,7 @@
 def attend_kernel(n, groups, columns, *refs):
     local = refs[:groups]
     every = refs[groups : 2 * groups]
-    residual = refs[2 * groups : 3 * groups]
-    out_weight, mine_ref, pass_ref, send_ref, scores_sc, blocks = refs[3 * groups :]
+    out_weight, mine_ref, pass_ref, send_ref, scores_sc, blocks = refs[2 * groups :]
     heads = columns // HD
     slots = mine_ref.shape[1]
     me, here = mdl_index(), seq_index()
@@ -339,7 +332,7 @@
     for k in range(4):
         blocks[k] = partial[k * columns : (k + 1) * columns, :]
     if groups == 1:
-        mine_ref[...] = blocks[me] + residual[0][...].astype(f32)
+        mine_ref[...] = blocks[me]
         pass_ref[...] = blocks[me ^ 2]
         send_ref[:columns, :] = blocks[me ^ 1].astype(bf16)
         send_ref[columns:, :] = blocks[me ^ 3].astype(bf16)
@@ -348,19 +341,19 @@
         for k in range(groups):
             there = pl.ds(pl.multiple_of((here ^ k) * cap, cap), cap)
             part = slice(k * cap, (k + 1) * cap)
-            mine_ref[:, there] = blocks[me, :, part] + residual[k][...].astype(f32)
+            mine_ref[:, there] = blocks[me, :, part]
             pass_ref[:, there] = blocks[me ^ 2, :, part]
             send_ref[:columns, there] = blocks[me ^ 1, :, part].astype(bf16)
             send_ref[columns:, there] = blocks[me ^ 3, :, part].astype(bf16)
 
 
-def attend(local, every, residual, out_weight, n, slots, columns):
+def attend(local, every, out_weight, n, slots, columns):
     groups = len(local)
     tiles = every[0].shape[-2]
     stored = (n, slots, tiles) if groups == 1 and n > 1 else (1, 8, 128)
     return pl.pallas_call(
         functools.partial(attend_kernel, n, groups, columns),
-        in_specs=[VMEM] * (3 * groups + 1),
+        in_specs=[VMEM] * (2 * groups + 1),
         out_specs=[VMEM] * 3,
         out_shape=[
             jax.ShapeDtypeStruct((columns, slots), f32),
@@ -375,7 +368,60 @@
             transcendentals=slots * (4 * slots + n * tiles),
         ),
         name="attend",
-    )(*local, *every, *residual, out_weight)
+    )(*local, *every, out_weight)
+
+
+def residual_kernel(groups, loose, *refs):
+    me, here = mdl_index(), seq_index()
+    out_ref = refs[-1]
+    columns = out_ref.shape[-2]
+    for k in range(groups):
+        chosen = refs[k][...]
+        cap, tiles = chosen.shape
+        pieces = refs[groups + k * loose : groups + (k + 1) * loose]
+        width = pieces[0].shape[-1]
+        shift = (me if loose == 1 else me & 1) * columns
+        mine = (
+            lax.broadcasted_iota(jnp.int32, (columns, width), 1)
+            == lax.broadcasted_iota(jnp.int32, (columns, width), 0) + shift
+        )
+        picked = jnp.where(mine, 1.0, 0.0).astype(bf16)
+        total = None
+        for j, piece in enumerate(pieces):
+            taken = chosen
+            if loose > 1:
+                half = tiles // 2
+                first = (me & 1) == j
+                taken = jnp.where(first, chosen[:, :half], chosen[:, half:])
+            part = dot_t(dot_t(picked, piece[...]).astype(bf16), taken)
+            total = part if total is None else total + part
+        if loose == 1:
+            out_ref[...] = total
+        else:
+            out_ref[:, pl.ds(pl.multiple_of((here ^ k) * cap, cap), cap)] = total
+
+
+def residual_of(chosen, pieces, columns):
+    groups, loose = len(chosen), len(pieces[0])
+    cap = chosen[0].shape[-2]
+    if loose > 1:
+        count, out, block = 1, (columns, groups * cap), whole
+    else:
+        count, out = chosen[0].shape[0], (columns, cap)
+
+        def block(shape):
+            return pl.BlockSpec((None, *shape), lambda b: (b, 0, 0))
+
+    args = [*chosen, *(piece for group in pieces for piece in group)]
+    return pl.pallas_call(
+        functools.partial(residual_kernel, groups, loose),
+        grid=(count,),
+        in_specs=[block(arg.shape[-2:]) for arg in args],
+        out_specs=block(out),
+        out_shape=jax.ShapeDtypeStruct(out if loose > 1 else (count, *out), f32),
+        compiler_params=pltpu.CompilerParams(vmem_limit_bytes=16 * MIB),
+        name="residual",
+    )(*args)
 
 
 def per_device(
@@ -414,9 +460,9 @@
     proj = proj_weight.T
     keep, send = feed_forward(class_rows, norm1_gain, gate_weight, up_weight, down_weight)
     near = over_mdl(send, 1)
-    summed = gather_sums(keep, down_weight, near)
+    summed = gather_sums(keep, near)
     far = over_mdl(summed, 2)
-    proj_near = over_mdl(after(proj, summed), 1)
+    proj_near = over_mdl(proj, 1)
     owner = after(destination, summed).reshape(1, tiles)
     if few:
         owners = [owner] + [over_seq(owner, k) for k in range(1, n)]
@@ -431,7 +477,7 @@
     if few:
         spare = after(embedded, embedded[:8, :128] + embedded[8:16, :128])
         owns = [spare] + [over_seq(spare if k == 1 else embedded, k) for k in range(1, n)]
-        ready = []
+        ready, kept = [], []
         for k in range(n):
             own = owns[k]
             across = over_mdl(own, 2)
@@ -440,20 +486,24 @@
             if k == 2:
                 across = after(across, ready[0][0])
             pieces = [own, over_mdl(own, 1), across, over_mdl(across, 1)]
+            kept.append(pieces[:2])
             ready.append(prepare(pieces, planned[k], norm3_gain, weights))
     else:
         sides = lax.all_gather(embedded, "mdl", axis=0).reshape(2, 2, tiles // 2, -1)
         block = sides.transpose(1, 2, 0, 3).reshape(tiles, -1)
         gathered = lax.all_gather(block, "seq", axis=0)
         ready = [prepare([gathered], planned[0], norm3_gain, weights)]
-
-    local, every, residual = (list(items) for items in zip(*ready))
+        kept = [[gathered]]
+
+    local, every = (list(items) for items in zip(*ready))
+    mine, passing, others = attend(local, every, out_weight, n, slots, columns)
+    chosen = [after(item[0], mine) for item in planned]
+    residual = residual_of(chosen, kept, columns)
     if not few:
-        residual = [residual[0].transpose(1, 0, 2).reshape(columns, slots)]
-    mine, passing, others = attend(local, every, residual, out_weight, n, slots, columns)
+        residual = residual.transpose(1, 0, 2).reshape(columns, slots)
     nearer = over_mdl(others, 1)
     farther = over_mdl((passing + nearer[columns:].astype(f32)).astype(bf16), 2)
-    total = mine + nearer[:columns].astype(f32) + farther.astype(f32)
+    total = mine + residual + nearer[:columns].astype(f32) + farther.astype(f32)
     return total.astype(bf16).T
 
 

time: 58.4 us -> 55.4 us (0.949)
  Pallas kernels: 16.5 us -> 15.1 us
  waiting for transfers between devices: 16.2 us -> 14.8 us
    pallas_call x1, Pallas kernels: 6.46 us -> 5.15 us  [feed_forward(): pl.pallas_call(ffn_kernel, in_specs=[far, VMEM, far, far, far], out_specs...]
    ppermute x17, waiting for transfers between devices: 11 us -> 9.72 us  [over_mdl(): return lax.ppermute(value, 'mdl', [(i, i ^ k) for i in range(4)])]
    ppermute x6, starting transfers between devices: 13.4 us -> 12.5 us  [over_seq(): return lax.ppermute(value, 'seq', [(i, i ^ k) for i in range(n)])]
    ppermute x17, starting transfers between devices: 10.1 us -> 10.9 us  [over_mdl(): return lax.ppermute(value, 'mdl', [(i, i ^ k) for i in range(4)])]
    pallas_call x4, Pallas kernels: 4.45 us -> 3.82 us  [prepare(): pl.pallas_call(functools.partial(prepare_kernel, loose), grid=(count,), i...]
  transfers between devices with their start and end apart: 23 -> 23, of which waited for: 9 -> 10; matrix products, arithmetic and copies ran while one was open for 0% -> 0% of each run, Pallas kernels for 6% -> 8%
where the time goes in v5:
time: 55.4 us; the launch traced here: 55.2 us
  starting transfers between devices  23.4 us (42%)
  Pallas kernels  15.1 us (27%)
  waiting for transfers between devices  14.8 us (27%)
  local copies, waits for them, and re-layouts  0.85 us (2%)
  other arithmetic  0.83 us (1%)
    ppermute x6, starting transfers between devices, over_seq(): return lax.ppermute(value, 'seq', [(i, i ^ k) for i in range(n)])  12.5 us
    ppermute x17, starting transfers between devices, over_mdl(): return lax.ppermute(value, 'mdl', [(i, i ^ k) for i in range(4)])  10.9 us
    ppermute x17, waiting for transfers between devices, over_mdl(): return lax.ppermute(value, 'mdl', [(i, i ^ k) for i in range(4)])  9.72 us
    pallas_call x1, Pallas kernels, feed_forward(): pl.pallas_call(ffn_kernel, in_specs=[far, VMEM, far, far, far], out_specs...  5.15 us
    ppermute x6, waiting for transfers between devices, over_seq(): return lax.ppermute(value, 'seq', [(i, i ^ k) for i in range(n)])  5.11 us
    pallas_call x4, Pallas kernels, prepare(): pl.pallas_call(functools.partial(prepare_kernel, loose), grid=(count,), i...  3.82 us
    pallas_call x1, Pallas kernels, attend(): pl.pallas_call(functools.partial(attend_kernel, n, groups, columns), in_s...  3.71 us
  transfers between devices with their start and end apart: 23, of which 10 were waited for; matrix products, arithmetic and copies ran while one was open for 0% of the time, Pallas kernels for 8%

profile of v5, /device:TPU:0, one launch (start us, length us, event | category | flops | bytes accessed | tf_op | source)
XLA Modules:
  0.0 55.2 jit_solution(1585038730252163801)
XLA Ops:
  0.0 0.8 %copy-done.8 = f32[1536]{0:T(1024)S(1)} copy-done((f32[1536]{0:T(1024)S(1)}, f32[1536]{0:T(1024)}, u32[]{:S(2)}) %copy-start.8) | copy-done | bytes 6168
  0.8 5.2 %feed_forward.1 = (bf16[128,1536]{1,0:T(8,128)(2,1)S(1)}, bf16[128,1536]{1,0:T(8,128)(2,1)S(1)}) custom-call(bf16[256,1536]{1,0:T(8,128)(2,1)} %rows_ref.3, f32[1536]{0:T(1024)S(1)} %copy-done.8, bf16[1536,1024]{1,0:T(8,128)(2,1)} %gate_ref.1, bf16[1536,1024]{1,0:T(8,128)(2,1)} %up_ref.1, bf16[1024,1536]{1,0:T(8,128)(2,1)} %down_ref.1), custom_call_target="tpu_custom_call" | custom-call | flops 2415919104 | bytes 9437184 | tf_op jit(solution)/shard_map/feed_forward/pallas_call | solution.py:85
  6.0 0.0 copy-start
  6.0 0.0 copy-start.1
  6.0 0.0 copy-start.2
  6.0 0.0 copy-start.5
  6.0 0.5 collective-permute-start
  6.6 0.1 collective-permute-start.5
  6.6 1.3 %collective-permute-done.near_ref = bf16[128,1536]{1,0:T(8,128)(2,1)S(1)} collective-permute-done((bf16[128,1536]{1,0:T(8,128)(2,1)S(1)}, bf16[128,1536]{1,0:T(8,128)(2,1)S(1)}, u32[]{:S(2)}, u32[]{:S(2)}) %collective-permute-start) | collective-permute-done | bytes 393248 | tf_op jit(solution)/shard_map/ppermute | solution.py:452
  7.9 0.1 gather_sums.1.here_ref
  8.0 2.9 %collective-permute-start.1 = (bf16[128,1536]{1,0:T(8,128)(2,1)S(1)}, bf16[128,1536]{1,0:T(8,128)(2,1)S(1)}, u32[]{:S(2)}, u32[]{:S(2)}) collective-permute-start(bf16[128,1536]{1,0:T(8,128)(2,1)S(1)} %gather_sums.1.here_ref), channel_id=1, source_target_pairs={{0,2},{1,3},{2,0},{3,1},{4,6},{5,7},{6,4},{7,5},{8,10},{9,11},{10,... | collective-permute-start | bytes 1179656 | tf_op jit(solution)/shard_map/ppermute | solution.py:452
  10.9 3.6 %collective-permute-start.4 = (s32[1,256]{1,0:T(1,128)S(1)}, s32[1,256]{1,0:T(1,128)S(1)}, u32[]{:S(2)}, u32[]{:S(2)}) collective-permute-start(s32[1,256]{1,0:T(1,128)S(1)} %bitcast.21), channel_id=1, source_target_pairs={{0,12},{4,8},{8,4},{12,0},{1,13},{5,9},{9,5},{13,1},{2,14},{6,10},... | collective-permute-start | bytes 3080 | tf_op jit(solution)/shard_map/ppermute | solution.py:455
  14.5 0.0 collective-permute-start.3
  14.5 0.8 %collective-permute-start.2 = (s32[1,256]{1,0:T(1,128)S(1)}, s32[1,256]{1,0:T(1,128)S(1)}, u32[]{:S(2)}, u32[]{:S(2)}) collective-permute-start(s32[1,256]{1,0:T(1,128)S(1)} %bitcast.23), channel_id=1, source_target_pairs={{0,4},{4,0},{8,12},{12,8},{1,5},{5,1},{9,13},{13,9},{2,6},{6,2},{1... | collective-permute-start | bytes 3080 | tf_op jit(solution)/shard_map/ppermute | solution.py:455
  15.3 1.0 %collective-permute-done.4.refs_3_ = s32[1,256]{1,0:T(1,128)S(1)} collective-permute-done((s32[1,256]{1,0:T(1,128)S(1)}, s32[1,256]{1,0:T(1,128)S(1)}, u32[]{:S(2)}, u32[]{:S(2)}) %collective-permute-start.4) | collective-permute-done | bytes 1056 | tf_op jit(solution)/shard_map/ppermute | solution.py:455
  16.3 2.7 %collective-permute-done.3.refs_2_ = s32[1,256]{1,0:T(1,128)S(1)} collective-permute-done((s32[1,256]{1,0:T(1,128)S(1)}, s32[1,256]{1,0:T(1,128)S(1)}, u32[]{:S(2)}, u32[]{:S(2)}) %collective-permute-start.3) | collective-permute-done | bytes 1056 | tf_op jit(solution)/shard_map/ppermute | solution.py:455
  19.0 0.0 collective-permute-done.2.refs_1_
  19.0 0.4 plan.1
  19.4 0.9 %collective-permute-done.1.far_ref = bf16[128,1536]{1,0:T(8,128)(2,1)S(1)} collective-permute-done((bf16[128,1536]{1,0:T(8,128)(2,1)S(1)}, bf16[128,1536]{1,0:T(8,128)(2,1)S(1)}, u32[]{:S(2)}, u32[]{:S(2)}) %collective-permute-start.1) | collective-permute-done | bytes 393248 | tf_op jit(solution)/shard_map/ppermute | solution.py:452
  20.3 0.0 collective-permute-done.5.near
  20.3 0.0 copy-done.3
  20.4 0.9 %embed.1.refs_0_.refs_4_ = bf16[128,384]{1,0:T(8,128)(2,1)S(1)} custom-call(bf16[256,1536]{1,0:T(8,128)(2,1)S(1)} %copy-done.3, bf16[128,1536]{1,0:T(8,128)(2,1)S(1)} %gather_sums.1.here_ref, bf16[128,1536]{1,0:T(8,128)(2,1)S(1)} %collective-permute-done.1.far_ref, f32[1536]{0:T(1024)S(1)} %copy-done.6, f32[1536]{0:T(1024)S(1)} %copy-done.7, ...), custom_call_target="tpu_custom_call" | custom-call | flops 150994944 | bytes 1179648 | tf_op jit(solution)/shard_map/embed/pallas_call | solution.py:137
  21.3 0.0 copy-start.10
  21.3 1.9 %collective-permute-start.9 = (bf16[128,384]{1,0:T(8,128)(2,1)S(1)}, bf16[128,384]{1,0:T(8,128)(2,1)S(1)}, u32[]{:S(2)}, u32[]{:S(2)}) collective-permute-start(bf16[128,384]{1,0:T(8,128)(2,1)S(1)} %embed.1.refs_0_.refs_4_), channel_id=1, source_target_pairs={{0,4},{4,0},{8,12},{12,8},{1,5},{5,1},{9,13},{13,9},{2,6},{6,2},{1... | collective-permute-start | bytes 294920 | tf_op jit(solution)/shard_map/ppermute | solution.py:455
  23.2 1.5 %collective-permute-start.7 = (bf16[128,384]{1,0:T(8,128)(2,1)S(1)}, bf16[128,384]{1,0:T(8,128)(2,1)S(1)}, u32[]{:S(2)}, u32[]{:S(2)}) collective-permute-start(bf16[128,384]{1,0:T(8,128)(2,1)S(1)} %embed.1.refs_0_.refs_4_), channel_id=1, source_target_pairs={{0,2},{1,3},{2,0},{3,1},{4,6},{5,7},{6,4},{7,5},{8,10},{9,11},{10,... | collective-permute-start | bytes 294920 | tf_op jit(solution)/shard_map/ppermute | solution.py:452
  24.7 2.6 %collective-permute-start.13 = (bf16[128,384]{1,0:T(8,128)(2,1)S(1)}, bf16[128,384]{1,0:T(8,128)(2,1)S(1)}, u32[]{:S(2)}, u32[]{:S(2)}) collective-permute-start(bf16[128,384]{1,0:T(8,128)(2,1)S(1)} %embed.1.refs_0_.refs_4_), channel_id=1, source_target_pairs={{0,8},{4,12},{8,0},{12,4},{1,9},{5,13},{9,1},{13,5},{2,10},{6,14},... | collective-permute-start | bytes 294920 | tf_op jit(solution)/shard_map/ppermute | solution.py:455
  27.3 0.0 collective-permute-start.6
  27.3 0.0 collective-permute-done.9.refs_0_.refs_6_
  27.3 1.2 %collective-permute-start.11 = (bf16[128,384]{1,0:T(8,128)(2,1)S(1)}, bf16[128,384]{1,0:T(8,128)(2,1)S(1)}, u32[]{:S(2)}, u32[]{:S(2)}) collective-permute-start(bf16[128,384]{1,0:T(8,128)(2,1)S(1)} %collective-permute-done.9.refs_0_.refs_6_), channel_id=1, source_target_pairs={{0,2},{1,3},{2,0},{3,1},{4,6},{5,7},{6,4},{7,5},{8,10},{9,11},{10,... | collective-permute-start | bytes 294920 | tf_op jit(solution)/shard_map/ppermute | solution.py:452
  28.4 3.6 %collective-permute-start.17 = (bf16[128,384]{1,0:T(8,128)(2,1)S(1)}, bf16[128,384]{1,0:T(8,128)(2,1)S(1)}, u32[]{:S(2)}, u32[]{:S(2)}) collective-permute-start(bf16[128,384]{1,0:T(8,128)(2,1)S(1)} %embed.1.refs_0_.refs_4_), channel_id=1, source_target_pairs={{0,12},{4,8},{8,4},{12,0},{1,13},{5,9},{9,5},{13,1},{2,14},{6,10},... | collective-permute-start | bytes 294920 | tf_op jit(solution)/shard_map/ppermute | solution.py:455
  32.0 0.0 collective-permute-done.7.refs_2_
  32.0 0.0 collective-permute-start.8
  32.0 0.0 collective-permute-done.13.refs_0_.refs_8_
  32.0 0.9 %collective-permute-start.15 = (bf16[128,384]{1,0:T(8,128)(2,1)S(1)}, bf16[128,384]{1,0:T(8,128)(2,1)S(1)}, u32[]{:S(2)}, u32[]{:S(2)}) collective-permute-start(bf16[128,384]{1,0:T(8,128)(2,1)S(1)} %collective-permute-done.13.refs_0_.refs_8_), channel_id=1, source_target_pairs={{0,2},{1,3},{2,0},{3,1},{4,6},{5,7},{6,4},{7,5},{8,10},{9,11},{10,... | collective-permute-start | bytes 294920 | tf_op jit(solution)/shard_map/ppermute | solution.py:452
  33.0 0.0 collective-permute-done.6.refs_1_.refs_5_
  33.0 0.2 collective-permute-start.10
  33.1 0.0 collective-permute-done.11.refs_2_
  33.1 0.3 collective-permute-start.12
  33.5 1.4 %collective-permute-done.17.refs_0_.refs_10_ = bf16[128,384]{1,0:T(8,128)(2,1)S(1)} collective-permute-done((bf16[128,384]{1,0:T(8,128)(2,1)S(1)}, bf16[128,384]{1,0:T(8,128)(2,1)S(1)}, u32[]{:S(2)}, u32[]{:S(2)}) %collective-permute-start.17) | collective-permute-done | bytes 98336 | tf_op jit(solution)/shard_map/ppermute | solution.py:455
  34.9 1.2 %collective-permute-start.19 = (bf16[128,384]{1,0:T(8,128)(2,1)S(1)}, bf16[128,384]{1,0:T(8,128)(2,1)S(1)}, u32[]{:S(2)}, u32[]{:S(2)}) collective-permute-start(bf16[128,384]{1,0:T(8,128)(2,1)S(1)} %collective-permute-done.17.refs_0_.refs_10_), channel_id=1, source_target_pairs={{0,2},{1,3},{2,0},{3,1},{4,6},{5,7},{6,4},{7,5},{8,10},{9,11},{10,... | collective-permute-start | bytes 294920 | tf_op jit(solution)/shard_map/ppermute | solution.py:452
  36.1 0.0 collective-permute-done.8.refs_3_
  36.1 0.0 collective-permute-start.18
  36.2 1.0 %prepare.4 = (bf16[128,768]{1,0:T(8,128)(2,1)S(1)}, bf16[256,512]{1,0:T(8,128)(2,1)S(1)}) custom-call(bf16[128,384]{1,0:T(8,128)(2,1)S(1)} %embed.1.refs_0_.refs_4_, bf16[128,384]{1,0:T(8,128)(2,1)S(1)} %collective-permute-done.6.refs_1_.refs_5_, bf16[128,384]{1,0:T(8,128)(2,1)S(1)} %collective-permute-done.7.refs_2_, ...), custom_call_target="tpu_custom_call" | custom-call | flops 226492416 | bytes 884736 | tf_op jit(solution)/shard_map/prepare/pallas_call | solution.py:246
  37.1 0.6 %collective-permute-done.15.refs_2_ = bf16[128,384]{1,0:T(8,128)(2,1)S(1)} collective-permute-done((bf16[128,384]{1,0:T(8,128)(2,1)S(1)}, bf16[128,384]{1,0:T(8,128)(2,1)S(1)}, u32[]{:S(2)}, u32[]{:S(2)}) %collective-permute-start.15) | collective-permute-done | bytes 98336 | tf_op jit(solution)/shard_map/ppermute | solution.py:452
  37.7 0.0 collective-permute-start.14
  37.7 0.0 collective-permute-done.10.refs_1_.refs_7_
  37.7 0.5 collective-permute-start.16
  38.2 0.0 collective-permute-done.12.refs_3_
  38.2 1.0 %prepare.5 = (bf16[128,768]{1,0:T(8,128)(2,1)S(1)}, bf16[256,512]{1,0:T(8,128)(2,1)S(1)}) custom-call(bf16[128,384]{1,0:T(8,128)(2,1)S(1)} %collective-permute-done.9.refs_0_.refs_6_, bf16[128,384]{1,0:T(8,128)(2,1)S(1)} %collective-permute-done.10.refs_1_.refs_7_, bf16[128,384]{1,0:T(8,128)(2,1)S(1)} %collective-permute-done.11.refs_2_, ...), custom_call_target="tpu_custom_call" | custom-call | flops 226492416 | bytes 884736 | tf_op jit(solution)/shard_map/prepare/pallas_call | solution.py:246
  39.2 0.4 collective-permute-done.19.refs_2_
  39.5 0.0 collective-permute-start.20
  39.5 0.0 collective-permute-done.14.refs_1_.refs_9_
  39.5 0.0 collective-permute-done.16.refs_3_
  39.5 1.0 %prepare.6 = (bf16[128,768]{1,0:T(8,128)(2,1)S(1)}, bf16[256,512]{1,0:T(8,128)(2,1)S(1)}) custom-call(bf16[128,384]{1,0:T(8,128)(2,1)S(1)} %collective-permute-done.13.refs_0_.refs_8_, bf16[128,384]{1,0:T(8,128)(2,1)S(1)} %collective-permute-done.14.refs_1_.refs_9_, bf16[128,384]{1,0:T(8,128)(2,1)S(1)} %collective-permute-done.15.refs_2_, ...), custom_call_target="tpu_custom_call" | custom-call | flops 226492416 | bytes 884736 | tf_op jit(solution)/shard_map/prepare/pallas_call | solution.py:246
  40.5 0.0 collective-permute-done.18.refs_1_.refs_11_
  40.5 0.3 collective-permute-done.20.refs_3_
  40.8 1.0 %prepare.7 = (bf16[128,768]{1,0:T(8,128)(2,1)S(1)}, bf16[256,512]{1,0:T(8,128)(2,1)S(1)}) custom-call(bf16[128,384]{1,0:T(8,128)(2,1)S(1)} %collective-permute-done.17.refs_0_.refs_10_, bf16[128,384]{1,0:T(8,128)(2,1)S(1)} %collective-permute-done.18.refs_1_.refs_11_, bf16[128,384]{1,0:T(8,128)(2,1)S(1)} %collective-permute-done.19.refs_2_, ...), custom_call_target="tpu_custom_call" | custom-call | flops 226492416 | bytes 884736 | tf_op jit(solution)/shard_map/prepare/pallas_call | solution.py:246
  41.8 3.7 %attend.1 = (f32[192,512]{1,0:T(8,128)S(1)}, f32[192,512]{1,0:T(8,128)S(1)}, bf16[384,512]{1,0:T(8,128)(2,1)S(1)}) custom-call(bf16[128,768]{1,0:T(8,128)(2,1)S(1)} %get-tuple-element.40.refs_0_, bf16[128,768]{1,0:T(8,128)(2,1)S(1)} %get-tuple-element.43.refs_1_, bf16[128,768]{1,0:T(8,128)(2,1)S(1)} %get-tuple-element.47.refs_2_, ...), custom_call_target="tpu_custom_call" | custom-call | flops 1207959552 | bytes 393216 | tf_op jit(solution)/shard_map/attend/pallas_call | solution.py:354
  45.5 0.3 collective-permute-start.21
  45.8 1.5 %collective-permute-done.21 = bf16[384,512]{1,0:T(8,128)(2,1)S(1)} collective-permute-done((bf16[384,512]{1,0:T(8,128)(2,1)S(1)}, bf16[384,512]{1,0:T(8,128)(2,1)S(1)}, u32[]{:S(2)}, u32[]{:S(2)}) %collective-permute-start.21) | collective-permute-done | bytes 393248 | tf_op jit(solution)/shard_map/ppermute | solution.py:452
  47.4 1.3 %collective-permute-start.22 = (bf16[192,512]{1,0:T(8,128)(2,1)S(1)}, bf16[192,512]{1,0:T(8,128)(2,1)S(1)}, u32[]{:S(2)}, u32[]{:S(2)}) collective-permute-start(bf16[192,512]{1,0:T(8,128)(2,1)S(1)} %add_convert_fusion.1), channel_id=1, source_target_pairs={{0,2},{1,3},{2,0},{3,1},{4,6},{5,7},{6,4},{7,5},{8,10},{9,11},{10,... | collective-permute-start | bytes 589832 | tf_op jit(solution)/shard_map/ppermute | solution.py:452
  48.6 1.1 %residual.1 = f32[192,512]{1,0:T(8,128)S(1)} custom-call(bf16[128,256]{1,0:T(8,128)(2,1)S(1)} %get-tuple-element.57.refs_4_.refs_0_, bf16[128,256]{1,0:T(8,128)(2,1)S(1)} %get-tuple-element.58.refs_4_.refs_1_, bf16[128,256]{1,0:T(8,128)(2,1)S(1)} %get-tuple-element.59.refs_4_.refs_2_, bf16[128,256]{1,0:T(8,128)(2,1)S(1)} %get-tuple-element.60.refs_4_.refs_3_, ...), custom_call_target="tpu_custom_call" | custom-call | tf_op jit(solution)/shard_map/residual/pallas_call | solution.py:416
  49.7 4.7 %collective-permute-done.22 = bf16[192,512]{1,0:T(8,128)(2,1)S(1)} collective-permute-done((bf16[192,512]{1,0:T(8,128)(2,1)S(1)}, bf16[192,512]{1,0:T(8,128)(2,1)S(1)}, u32[]{:S(2)}, u32[]{:S(2)}) %collective-permute-start.22) | collective-permute-done | bytes 196640 | tf_op jit(solution)/shard_map/ppermute | solution.py:452
  54.4 0.8 %fusion = bf16[512,192]{0,1:T(8,128)(2,1)} fusion(bf16[192,512]{1,0:T(8,128)(2,1)S(1)} %collective-permute-done.22, f32[192,512]{1,0:T(8,128)S(1)} %get-tuple-element.56, f32[192,512]{1,0:T(8,128)S(1)} %residual.1, bf16[384,512]{1,0:T(8,128)(2,1)S(1)} %collective-permute-done.21), kind=kLoop, calls=%fused_computation.2 | loop fusion | flops 589824 | bytes 1376256 | tf_op jit(solution)/shard_map/transpose | solution.py:507
  (16 shorter events, 0.1 us)
Async XLA Ops:
  0.0 20.3 %copy-start.3 = (bf16[256,1536]{1,0:T(8,128)(2,1)S(1)}, bf16[256,1536]{1,0:T(8,128)(2,1)}, u32[]{:S(2)}) copy-start(bf16[256,1536]{1,0:T(8,128)(2,1)} %rows_ref.3) | copy-start | bytes 2359300
  0.0 6.5 %copy-start.4 = (bf16[1536,192]{0,1:T(8,128)(2,1)S(1)}, bf16[1536,192]{0,1:T(8,128)(2,1)}, u32[]{:S(2)}) copy-start(bf16[1536,192]{0,1:T(8,128)(2,1)} %param.22) | copy-start | bytes 1769476
  0.0 20.3 %copy-start.7 = (f32[1536]{0:T(1024)S(1)}, f32[1536]{0:T(1024)}, u32[]{:S(2)}) copy-start(f32[1536]{0:T(1024)} %gain_ref.3) | copy-start | bytes 18436
  0.0 20.3 %copy-start.6 = (f32[1536]{0:T(1024)S(1)}, f32[1536]{0:T(1024)}, u32[]{:S(2)}) copy-start(f32[1536]{0:T(1024)} %scale_ref.1) | copy-start | bytes 18436
  0.0 0.8 %copy-start.8 = (f32[1536]{0:T(1024)S(1)}, f32[1536]{0:T(1024)}, u32[]{:S(2)}) copy-start(f32[1536]{0:T(1024)} %gain_ref.2) | copy-start | bytes 18436
  0.8 10.1 %copy-start.9 = (s32[256,1]{0,1:T(1,128)S(1)}, s32[256,1]{0,1:T(1,128)}, u32[]{:S(2)}) copy-start(s32[256,1]{0,1:T(1,128)} %param.15) | copy-start | bytes 3076
  6.0 30.2 %copy-start = (bf16[768,192]{0,1:T(8,128)(2,1)S(1)}, bf16[768,192]{0,1:T(8,128)(2,1)}, u32[]{:S(2)}) copy-start(bf16[768,192]{0,1:T(8,128)(2,1)} %param.24) | copy-start | bytes 884740
  6.0 30.1 %copy-start.1 = (bf16[768,192]{0,1:T(8,128)(2,1)S(1)}, bf16[768,192]{0,1:T(8,128)(2,1)}, u32[]{:S(2)}) copy-start(bf16[768,192]{0,1:T(8,128)(2,1)} %param.25) | copy-start | bytes 884740
  6.0 30.1 %copy-start.2 = (bf16[768,192]{0,1:T(8,128)(2,1)S(1)}, bf16[768,192]{0,1:T(8,128)(2,1)}, u32[]{:S(2)}) copy-start(bf16[768,192]{0,1:T(8,128)(2,1)} %param.26) | copy-start | bytes 884740
  6.0 30.1 %copy-start.5 = (f32[768]{0:T(1024)S(1)}, f32[768]{0:T(1024)}, u32[]{:S(2)}) copy-start(f32[768]{0:T(1024)} %refs_6_.7) | copy-start | bytes 9220
  6.0 1.9 %collective-permute-start = (bf16[128,1536]{1,0:T(8,128)(2,1)S(1)}, bf16[128,1536]{1,0:T(8,128)(2,1)S(1)}, u32[]{:S(2)}, u32[]{:S(2)}) collective-permute-start(bf16[128,1536]{1,0:T(8,128)(2,1)S(1)} %get-tuple-element.35), channel_id=1, source_target_pairs={{0,1},{1,0},{2,3},{3,2},{4,5},{5,4},{6,7},{7,6},{8,9},{9,8},{10,11... | collective-permute-start | bytes 1179656 | tf_op jit(solution)/shard_map/ppermute | solution.py:452
  6.6 13.8 %collective-permute-start.5 = (bf16[192,1536]{1,0:T(8,128)(2,1)S(1)}, bf16[192,1536]{1,0:T(8,128)(2,1)S(1)}, u32[]{:S(2)}, u32[]{:S(2)}) collective-permute-start(bf16[192,1536]{1,0:T(8,128)(2,1)S(1)} %bitcast.19), channel_id=1, source_target_pairs={{0,1},{1,0},{2,3},{3,2},{4,5},{5,4},{6,7},{7,6},{8,9},{9,8},{10,11... | collective-permute-start | bytes 1769480 | tf_op jit(solution)/shard_map/ppermute | solution.py:452
  8.0 12.3 %collective-permute-start.1 = (bf16[128,1536]{1,0:T(8,128)(2,1)S(1)}, bf16[128,1536]{1,0:T(8,128)(2,1)S(1)}, u32[]{:S(2)}, u32[]{:S(2)}) collective-permute-start(bf16[128,1536]{1,0:T(8,128)(2,1)S(1)} %gather_sums.1.here_ref), channel_id=1, source_target_pairs={{0,2},{1,3},{2,0},{3,1},{4,6},{5,7},{6,4},{7,5},{8,10},{9,11},{10,... | collective-permute-start | bytes 1179656 | tf_op jit(solution)/shard_map/ppermute | solution.py:452
  10.9 5.4 %collective-permute-start.4 = (s32[1,256]{1,0:T(1,128)S(1)}, s32[1,256]{1,0:T(1,128)S(1)}, u32[]{:S(2)}, u32[]{:S(2)}) collective-permute-start(s32[1,256]{1,0:T(1,128)S(1)} %bitcast.21), channel_id=1, source_target_pairs={{0,12},{4,8},{8,4},{12,0},{1,13},{5,9},{9,5},{13,1},{2,14},{6,10},... | collective-permute-start | bytes 3080 | tf_op jit(solution)/shard_map/ppermute | solution.py:455
  14.5 4.5 %collective-permute-start.3 = (s32[1,256]{1,0:T(1,128)S(1)}, s32[1,256]{1,0:T(1,128)S(1)}, u32[]{:S(2)}, u32[]{:S(2)}) collective-permute-start(s32[1,256]{1,0:T(1,128)S(1)} %bitcast.22), channel_id=1, source_target_pairs={{0,8},{4,12},{8,0},{12,4},{1,9},{5,13},{9,1},{13,5},{2,10},{6,14},... | collective-permute-start | bytes 3080 | tf_op jit(solution)/shard_map/ppermute | solution.py:455
  14.5 4.5 %collective-permute-start.2 = (s32[1,256]{1,0:T(1,128)S(1)}, s32[1,256]{1,0:T(1,128)S(1)}, u32[]{:S(2)}, u32[]{:S(2)}) collective-permute-start(s32[1,256]{1,0:T(1,128)S(1)} %bitcast.23), channel_id=1, source_target_pairs={{0,4},{4,0},{8,12},{12,8},{1,5},{5,1},{9,13},{13,9},{2,6},{6,2},{1... | collective-permute-start | bytes 3080 | tf_op jit(solution)/shard_map/ppermute | solution.py:455
  21.3 20.5 %copy-start.10 = (bf16[192,768]{1,0:T(8,128)(2,1)S(1)}, bf16[192,768]{1,0:T(8,128)(2,1)}, u32[]{:S(2)}) copy-start(bf16[192,768]{1,0:T(8,128)(2,1)} %refs_8_.1) | copy-start | bytes 884740
  21.3 6.0 %collective-permute-start.9 = (bf16[128,384]{1,0:T(8,128)(2,1)S(1)}, bf16[128,384]{1,0:T(8,128)(2,1)S(1)}, u32[]{:S(2)}, u32[]{:S(2)}) collective-permute-start(bf16[128,384]{1,0:T(8,128)(2,1)S(1)} %embed.1.refs_0_.refs_4_), channel_id=1, source_target_pairs={{0,4},{4,0},{8,12},{12,8},{1,5},{5,1},{9,13},{13,9},{2,6},{6,2},{1... | collective-permute-start | bytes 294920 | tf_op jit(solution)/shard_map/ppermute | solution.py:455
  23.2 8.8 %collective-permute-start.7 = (bf16[128,384]{1,0:T(8,128)(2,1)S(1)}, bf16[128,384]{1,0:T(8,128)(2,1)S(1)}, u32[]{:S(2)}, u32[]{:S(2)}) collective-permute-start(bf16[128,384]{1,0:T(8,128)(2,1)S(1)} %embed.1.refs_0_.refs_4_), channel_id=1, source_target_pairs={{0,2},{1,3},{2,0},{3,1},{4,6},{5,7},{6,4},{7,5},{8,10},{9,11},{10,... | collective-permute-start | bytes 294920 | tf_op jit(solution)/shard_map/ppermute | solution.py:452
  24.7 7.4 %collective-permute-start.13 = (bf16[128,384]{1,0:T(8,128)(2,1)S(1)}, bf16[128,384]{1,0:T(8,128)(2,1)S(1)}, u32[]{:S(2)}, u32[]{:S(2)}) collective-permute-start(bf16[128,384]{1,0:T(8,128)(2,1)S(1)} %embed.1.refs_0_.refs_4_), channel_id=1, source_target_pairs={{0,8},{4,12},{8,0},{12,4},{1,9},{5,13},{9,1},{13,5},{2,10},{6,14},... | collective-permute-start | bytes 294920 | tf_op jit(solution)/shard_map/ppermute | solution.py:455
  27.3 5.7 %collective-permute-start.6 = (bf16[128,384]{1,0:T(8,128)(2,1)S(1)}, bf16[128,384]{1,0:T(8,128)(2,1)S(1)}, u32[]{:S(2)}, u32[]{:S(2)}) collective-permute-start(bf16[128,384]{1,0:T(8,128)(2,1)S(1)} %embed.1.refs_0_.refs_4_), channel_id=1, source_target_pairs={{0,1},{1,0},{2,3},{3,2},{4,5},{5,4},{6,7},{7,6},{8,9},{9,8},{10,11... | collective-permute-start | bytes 294920 | tf_op jit(solution)/shard_map/ppermute | solution.py:452
  27.3 5.9 %collective-permute-start.11 = (bf16[128,384]{1,0:T(8,128)(2,1)S(1)}, bf16[128,384]{1,0:T(8,128)(2,1)S(1)}, u32[]{:S(2)}, u32[]{:S(2)}) collective-permute-start(bf16[128,384]{1,0:T(8,128)(2,1)S(1)} %collective-permute-done.9.refs_0_.refs_6_), channel_id=1, source_target_pairs={{0,2},{1,3},{2,0},{3,1},{4,6},{5,7},{6,4},{7,5},{8,10},{9,11},{10,... | collective-permute-start | bytes 294920 | tf_op jit(solution)/shard_map/ppermute | solution.py:452
  28.4 6.5 %collective-permute-start.17 = (bf16[128,384]{1,0:T(8,128)(2,1)S(1)}, bf16[128,384]{1,0:T(8,128)(2,1)S(1)}, u32[]{:S(2)}, u32[]{:S(2)}) collective-permute-start(bf16[128,384]{1,0:T(8,128)(2,1)S(1)} %embed.1.refs_0_.refs_4_), channel_id=1, source_target_pairs={{0,12},{4,8},{8,4},{12,0},{1,13},{5,9},{9,5},{13,1},{2,14},{6,10},... | collective-permute-start | bytes 294920 | tf_op jit(solution)/shard_map/ppermute | solution.py:455
  32.0 4.1 %collective-permute-start.8 = (bf16[128,384]{1,0:T(8,128)(2,1)S(1)}, bf16[128,384]{1,0:T(8,128)(2,1)S(1)}, u32[]{:S(2)}, u32[]{:S(2)}) collective-permute-start(bf16[128,384]{1,0:T(8,128)(2,1)S(1)} %collective-permute-done.7.refs_2_), channel_id=1, source_target_pairs={{0,1},{1,0},{2,3},{3,2},{4,5},{5,4},{6,7},{7,6},{8,9},{9,8},{10,11... | collective-permute-start | bytes 294920 | tf_op jit(solution)/shard_map/ppermute | solution.py:452
  32.0 5.7 %collective-permute-start.15 = (bf16[128,384]{1,0:T(8,128)(2,1)S(1)}, bf16[128,384]{1,0:T(8,128)(2,1)S(1)}, u32[]{:S(2)}, u32[]{:S(2)}) collective-permute-start(bf16[128,384]{1,0:T(8,128)(2,1)S(1)} %collective-permute-done.13.refs_0_.refs_8_), channel_id=1, source_target_pairs={{0,2},{1,3},{2,0},{3,1},{4,6},{5,7},{6,4},{7,5},{8,10},{9,11},{10,... | collective-permute-start | bytes 294920 | tf_op jit(solution)/shard_map/ppermute | solution.py:452
  33.0 4.7 %collective-permute-start.10 = (bf16[128,384]{1,0:T(8,128)(2,1)S(1)}, bf16[128,384]{1,0:T(8,128)(2,1)S(1)}, u32[]{:S(2)}, u32[]{:S(2)}) collective-permute-start(bf16[128,384]{1,0:T(8,128)(2,1)S(1)} %collective-permute-done.9.refs_0_.refs_6_), channel_id=1, source_target_pairs={{0,1},{1,0},{2,3},{3,2},{4,5},{5,4},{6,7},{7,6},{8,9},{9,8},{10,11... | collective-permute-start | bytes 294920 | tf_op jit(solution)/shard_map/ppermute | solution.py:452
  33.1 5.1 %collective-permute-start.12 = (bf16[128,384]{1,0:T(8,128)(2,1)S(1)}, bf16[128,384]{1,0:T(8,128)(2,1)S(1)}, u32[]{:S(2)}, u32[]{:S(2)}) collective-permute-start(bf16[128,384]{1,0:T(8,128)(2,1)S(1)} %collective-permute-done.11.refs_2_), channel_id=1, source_target_pairs={{0,1},{1,0},{2,3},{3,2},{4,5},{5,4},{6,7},{7,6},{8,9},{9,8},{10,11... | collective-permute-start | bytes 294920 | tf_op jit(solution)/shard_map/ppermute | solution.py:452
  34.9 4.6 %collective-permute-start.19 = (bf16[128,384]{1,0:T(8,128)(2,1)S(1)}, bf16[128,384]{1,0:T(8,128)(2,1)S(1)}, u32[]{:S(2)}, u32[]{:S(2)}) collective-permute-start(bf16[128,384]{1,0:T(8,128)(2,1)S(1)} %collective-permute-done.17.refs_0_.refs_10_), channel_id=1, source_target_pairs={{0,2},{1,3},{2,0},{3,1},{4,6},{5,7},{6,4},{7,5},{8,10},{9,11},{10,... | collective-permute-start | bytes 294920 | tf_op jit(solution)/shard_map/ppermute | solution.py:452
  36.1 4.4 %collective-permute-start.18 = (bf16[128,384]{1,0:T(8,128)(2,1)S(1)}, bf16[128,384]{1,0:T(8,128)(2,1)S(1)}, u32[]{:S(2)}, u32[]{:S(2)}) collective-permute-start(bf16[128,384]{1,0:T(8,128)(2,1)S(1)} %collective-permute-done.17.refs_0_.refs_10_), channel_id=1, source_target_pairs={{0,1},{1,0},{2,3},{3,2},{4,5},{5,4},{6,7},{7,6},{8,9},{9,8},{10,11... | collective-permute-start | bytes 294920 | tf_op jit(solution)/shard_map/ppermute | solution.py:452
  37.7 1.8 %collective-permute-start.14 = (bf16[128,384]{1,0:T(8,128)(2,1)S(1)}, bf16[128,384]{1,0:T(8,128)(2,1)S(1)}, u32[]{:S(2)}, u32[]{:S(2)}) collective-permute-start(bf16[128,384]{1,0:T(8,128)(2,1)S(1)} %collective-permute-done.13.refs_0_.refs_8_), channel_id=1, source_target_pairs={{0,1},{1,0},{2,3},{3,2},{4,5},{5,4},{6,7},{7,6},{8,9},{9,8},{10,11... | collective-permute-start | bytes 294920 | tf_op jit(solution)/shard_map/ppermute | solution.py:452
  37.7 1.8 %collective-permute-start.16 = (bf16[128,384]{1,0:T(8,128)(2,1)S(1)}, bf16[128,384]{1,0:T(8,128)(2,1)S(1)}, u32[]{:S(2)}, u32[]{:S(2)}) collective-permute-start(bf16[128,384]{1,0:T(8,128)(2,1)S(1)} %collective-permute-done.15.refs_2_), channel_id=1, source_target_pairs={{0,1},{1,0},{2,3},{3,2},{4,5},{5,4},{6,7},{7,6},{8,9},{9,8},{10,11... | collective-permute-start | bytes 294920 | tf_op jit(solution)/shard_map/ppermute | solution.py:452
  39.5 1.3 %collective-permute-start.20 = (bf16[128,384]{1,0:T(8,128)(2,1)S(1)}, bf16[128,384]{1,0:T(8,128)(2,1)S(1)}, u32[]{:S(2)}, u32[]{:S(2)}) collective-permute-start(bf16[128,384]{1,0:T(8,128)(2,1)S(1)} %collective-permute-done.19.refs_2_), channel_id=1, source_target_pairs={{0,1},{1,0},{2,3},{3,2},{4,5},{5,4},{6,7},{7,6},{8,9},{9,8},{10,11... | collective-permute-start | bytes 294920 | tf_op jit(solution)/shard_map/ppermute | solution.py:452
  45.5 1.8 %collective-permute-start.21 = (bf16[384,512]{1,0:T(8,128)(2,1)S(1)}, bf16[384,512]{1,0:T(8,128)(2,1)S(1)}, u32[]{:S(2)}, u32[]{:S(2)}) collective-permute-start(bf16[384,512]{1,0:T(8,128)(2,1)S(1)} %get-tuple-element.61), channel_id=1, source_target_pairs={{0,1},{1,0},{2,3},{3,2},{4,5},{5,4},{6,7},{7,6},{8,9},{9,8},{10,11... | collective-permute-start | bytes 1179656 | tf_op jit(solution)/shard_map/ppermute | solution.py:452
  47.4 7.1 %collective-permute-start.22 = (bf16[192,512]{1,0:T(8,128)(2,1)S(1)}, bf16[192,512]{1,0:T(8,128)(2,1)S(1)}, u32[]{:S(2)}, u32[]{:S(2)}) collective-permute-start(bf16[192,512]{1,0:T(8,128)(2,1)S(1)} %add_convert_fusion.1), channel_id=1, source_target_pairs={{0,2},{1,3},{2,0},{3,1},{4,6},{5,7},{6,4},{7,5},{8,10},{9,11},{10,... | collective-permute-start | bytes 589832 | tf_op jit(solution)/shard_map/ppermute | solution.py:452

commit v6 on v5

--- a/solution.py
+++ b/solution.py
@@ -212,13 +212,14 @@
     chosen = chosen_ref[...]
     cap = chosen.shape[0]
     normed = layer_norm(rows.astype(f32), row(gain_ref)).astype(bf16)
-    queries = dot_t(normed, wq[...]).astype(bf16)
+    queries = (dot_t(normed, wq[...]) * (HD ** (-0.5) * LOG2E)).astype(bf16)
     keys = dot_t(normed, wk[...]).astype(bf16)
     values = dot_t(normed, wv[...]).astype(bf16)
     occupied = jnp.sum(chosen.astype(f32), axis=1, keepdims=True)
     all_ref[:, :columns] = keys
     all_ref[:, columns:LANES] = bias_ref[...]
     all_ref[:, LANES : LANES + columns] = values
+    all_ref[:, LANES + columns :] = jnp.ones((tiles, LANES - columns), bf16)
     local_ref[:, :columns] = dot(chosen, queries).astype(bf16)
     local_ref[:, columns:LANES] = jnp.zeros((cap, LANES - columns), bf16)
     local_ref[:, LANES : LANES + columns] = dot(chosen, keys).astype(bf16)
@@ -226,6 +227,7 @@
         jnp.where(occupied > 0.5, 0.0, MASKED), (cap, LANES - columns)
     ).astype(bf16)
     local_ref[:, 2 * LANES : 2 * LANES + columns] = dot(chosen, values).astype(bf16)
+    local_ref[:, 2 * LANES + columns :] = jnp.ones((cap, LANES - columns), bf16)
 
 
 def prepare(pieces, planned, gain, weights):
@@ -265,7 +267,6 @@
     heads = columns // HD
     slots = mine_ref.shape[1]
     me, here = mdl_index(), seq_index()
-    factor = HD ** (-0.5) * LOG2E
     zero, one = jnp.zeros((), bf16), jnp.ones((), bf16)
 
     def taken(sources, start, size):
@@ -274,7 +275,7 @@
 
     q = taken(local, 0, LANES)
     key_local = taken(local, LANES, LANES)
-    value_local = taken(local, 2 * LANES, columns)
+    value_local = taken(local, 2 * LANES, LANES)
     lane = lax.broadcasted_iota(jnp.int32, (slots, LANES), 1)
     head_lane = lane // HD
     head_of = head_lane[:, :columns]
@@ -284,12 +285,12 @@
     picked = jnp.where(class_lane == row_class, jnp.where(inside, q, one), zero)
     stored = groups == 1 and n > 1
     if not stored:
-        scores_sparse = dot_t(picked, taken(every, 0, LANES)) * factor
+        scores_sparse = dot_t(picked, taken(every, 0, LANES))
         peak_sparse = jnp.max(scores_sparse, axis=1, keepdims=True)
     else:
 
         def first(b, peak):
-            scores_sc[b] = dot_t(picked, every[0][b, :, :LANES]) * factor
+            scores_sc[b] = dot_t(picked, every[0][b, :, :LANES])
             return jnp.maximum(peak, jnp.max(scores_sc[b], axis=1, keepdims=True))
 
         peak_sparse = lax.fori_loop(0, n, first, jnp.full((slots, 1), MASKED, f32))
@@ -300,32 +301,28 @@
     peak_shared = peak_sparse
     for h in range(heads):
         query = jnp.where(head_lane == h, q, ones)
-        scores = dot_t(query, key_local) * factor
+        scores = dot_t(query, key_local)
         peak = jnp.max(scores, axis=1, keepdims=True)
         has = row_class == (h & (RATE - 1))
         peak = jnp.where(has, jnp.maximum(peak, peak_sparse), peak)
         peak_shared = jnp.where(has, peak, peak_shared)
         weights = jnp.exp2(scores - peak)
-        total = jnp.sum(weights, axis=1, keepdims=True)
-        numerator = jnp.where(head_of == h, dot(weights.astype(bf16), value_local), numerator)
-        denominator = jnp.where(head_of == h, total, denominator)
+        summed = dot(weights.astype(bf16), value_local)
+        numerator = jnp.where(head_of == h, summed[:, :columns], numerator)
+        denominator = jnp.where(head_of == h, summed[:, columns : columns + 1], denominator)
     if not stored:
         weights = jnp.exp2(scores_sparse - peak_shared)
-        total = jnp.sum(weights, axis=1, keepdims=True)
-        summed = dot(weights.astype(bf16), taken(every, LANES, columns))
+        summed = dot(weights.astype(bf16), taken(every, LANES, LANES))
     else:
 
         def second(b, carry):
             weights = jnp.exp2(scores_sc[b] - peak_shared)
-            values = every[0][b, :, LANES : LANES + columns]
-            return carry[0] + jnp.sum(weights, axis=1, keepdims=True), carry[1] + dot(weights.astype(bf16), values)
-
-        total, summed = lax.fori_loop(
-            0, n, second, (jnp.zeros((slots, 1), f32), jnp.zeros((slots, columns), f32))
-        )
+            return carry + dot(weights.astype(bf16), every[0][b, :, LANES:])
+
+        summed = lax.fori_loop(0, n, second, jnp.zeros((slots, LANES), f32))
     own_class = (head_of & (RATE - 1)) == row_class
-    numerator = numerator + jnp.where(own_class, summed, 0.0)
-    denominator = denominator + jnp.where(own_class, total, 0.0)
+    numerator = numerator + jnp.where(own_class, summed[:, :columns], 0.0)
+    denominator = denominator + jnp.where(own_class, summed[:, columns : columns + 1], 0.0)
     occupied = key_local[:, columns : columns + 1].astype(f32) > -1.0
     attended = jnp.where(occupied, numerator / denominator, 0.0).T.astype(bf16)
     partial = lax.dot_general(out_weight[...], attended, (((0,), (0,)), ((), ())), preferred_element_type=f32)

time: 55.4 us -> 55.2 us (level)
  no operation moved by 1% of the time
where the time goes in v6:
time: 55.2 us; the launch traced here: 55 us
  starting transfers between devices  23.4 us (42%)
  Pallas kernels  14.9 us (27%)
  waiting for transfers between devices  14.8 us (27%)
  local copies, waits for them, and re-layouts  0.85 us (2%)
  other arithmetic  0.83 us (2%)
    ppermute x6, starting transfers between devices, over_seq(): return lax.ppermute(value, 'seq', [(i, i ^ k) for i in range(n)])  12.5 us
    ppermute x17, starting transfers between devices, over_mdl(): return lax.ppermute(value, 'mdl', [(i, i ^ k) for i in range(4)])  10.9 us
    ppermute x17, waiting for transfers between devices, over_mdl(): return lax.ppermute(value, 'mdl', [(i, i ^ k) for i in range(4)])  9.69 us
    pallas_call x1, Pallas kernels, feed_forward(): pl.pallas_call(ffn_kernel, in_specs=[far, VMEM, far, far, far], out_specs...  5.15 us
    ppermute x6, waiting for transfers between devices, over_seq(): return lax.ppermute(value, 'seq', [(i, i ^ k) for i in range(n)])  5.11 us
    pallas_call x4, Pallas kernels, prepare(): pl.pallas_call(functools.partial(prepare_kernel, loose), grid=(count,), i...  3.84 us
    pallas_call x1, Pallas kernels, attend(): pl.pallas_call(functools.partial(attend_kernel, n, groups, columns), in_s...  3.44 us
  transfers between devices with their start and end apart: 23, of which 10 were waited for; matrix products, arithmetic and copies ran while one was open for 0% of the time, Pallas kernels for 8%

profile of v6, /device:TPU:0, one launch (start us, length us, event | category | flops | bytes accessed | tf_op | source)
XLA Modules:
  0.0 55.0 jit_solution(10189623775859934339)
XLA Ops:
  0.0 0.8 %copy-done.8 = f32[1536]{0:T(1024)S(1)} copy-done((f32[1536]{0:T(1024)S(1)}, f32[1536]{0:T(1024)}, u32[]{:S(2)}) %copy-start.8) | copy-done | bytes 6168
  0.8 5.2 %feed_forward.1 = (bf16[128,1536]{1,0:T(8,128)(2,1)S(1)}, bf16[128,1536]{1,0:T(8,128)(2,1)S(1)}) custom-call(bf16[256,1536]{1,0:T(8,128)(2,1)} %rows_ref.3, f32[1536]{0:T(1024)S(1)} %copy-done.8, bf16[1536,1024]{1,0:T(8,128)(2,1)} %gate_ref.1, bf16[1536,1024]{1,0:T(8,128)(2,1)} %up_ref.1, bf16[1024,1536]{1,0:T(8,128)(2,1)} %down_ref.1), custom_call_target="tpu_custom_call" | custom-call | flops 2415919104 | bytes 9437184 | tf_op jit(solution)/shard_map/feed_forward/pallas_call | solution.py:85
  6.0 0.0 copy-start
  6.0 0.0 copy-start.1
  6.0 0.0 copy-start.2
  6.0 0.0 copy-start.5
  6.0 0.5 collective-permute-start
  6.6 0.1 collective-permute-start.5
  6.6 1.3 %collective-permute-done.near_ref = bf16[128,1536]{1,0:T(8,128)(2,1)S(1)} collective-permute-done((bf16[128,1536]{1,0:T(8,128)(2,1)S(1)}, bf16[128,1536]{1,0:T(8,128)(2,1)S(1)}, u32[]{:S(2)}, u32[]{:S(2)}) %collective-permute-start) | collective-permute-done | bytes 393248 | tf_op jit(solution)/shard_map/ppermute | solution.py:449
  7.9 0.1 gather_sums.1.here_ref
  8.0 2.9 %collective-permute-start.1 = (bf16[128,1536]{1,0:T(8,128)(2,1)S(1)}, bf16[128,1536]{1,0:T(8,128)(2,1)S(1)}, u32[]{:S(2)}, u32[]{:S(2)}) collective-permute-start(bf16[128,1536]{1,0:T(8,128)(2,1)S(1)} %gather_sums.1.here_ref), channel_id=1, source_target_pairs={{0,2},{1,3},{2,0},{3,1},{4,6},{5,7},{6,4},{7,5},{8,10},{9,11},{10,... | collective-permute-start | bytes 1179656 | tf_op jit(solution)/shard_map/ppermute | solution.py:449
  10.9 3.6 %collective-permute-start.4 = (s32[1,256]{1,0:T(1,128)S(1)}, s32[1,256]{1,0:T(1,128)S(1)}, u32[]{:S(2)}, u32[]{:S(2)}) collective-permute-start(s32[1,256]{1,0:T(1,128)S(1)} %bitcast.21), channel_id=1, source_target_pairs={{0,12},{4,8},{8,4},{12,0},{1,13},{5,9},{9,5},{13,1},{2,14},{6,10},... | collective-permute-start | bytes 3080 | tf_op jit(solution)/shard_map/ppermute | solution.py:452
  14.5 0.0 collective-permute-start.3
  14.5 0.8 %collective-permute-start.2 = (s32[1,256]{1,0:T(1,128)S(1)}, s32[1,256]{1,0:T(1,128)S(1)}, u32[]{:S(2)}, u32[]{:S(2)}) collective-permute-start(s32[1,256]{1,0:T(1,128)S(1)} %bitcast.23), channel_id=1, source_target_pairs={{0,4},{4,0},{8,12},{12,8},{1,5},{5,1},{9,13},{13,9},{2,6},{6,2},{1... | collective-permute-start | bytes 3080 | tf_op jit(solution)/shard_map/ppermute | solution.py:452
  15.3 1.0 %collective-permute-done.4.refs_3_ = s32[1,256]{1,0:T(1,128)S(1)} collective-permute-done((s32[1,256]{1,0:T(1,128)S(1)}, s32[1,256]{1,0:T(1,128)S(1)}, u32[]{:S(2)}, u32[]{:S(2)}) %collective-permute-start.4) | collective-permute-done | bytes 1056 | tf_op jit(solution)/shard_map/ppermute | solution.py:452
  16.3 2.7 %collective-permute-done.3.refs_2_ = s32[1,256]{1,0:T(1,128)S(1)} collective-permute-done((s32[1,256]{1,0:T(1,128)S(1)}, s32[1,256]{1,0:T(1,128)S(1)}, u32[]{:S(2)}, u32[]{:S(2)}) %collective-permute-start.3) | collective-permute-done | bytes 1056 | tf_op jit(solution)/shard_map/ppermute | solution.py:452
  19.0 0.0 collective-permute-done.2.refs_1_
  19.0 0.4 plan.1
  19.4 0.9 %collective-permute-done.1.far_ref = bf16[128,1536]{1,0:T(8,128)(2,1)S(1)} collective-permute-done((bf16[128,1536]{1,0:T(8,128)(2,1)S(1)}, bf16[128,1536]{1,0:T(8,128)(2,1)S(1)}, u32[]{:S(2)}, u32[]{:S(2)}) %collective-permute-start.1) | collective-permute-done | bytes 393248 | tf_op jit(solution)/shard_map/ppermute | solution.py:449
  20.3 0.0 collective-permute-done.5.near
  20.3 0.0 copy-done.6
  20.4 0.9 %embed.1.refs_0_.refs_4_ = bf16[128,384]{1,0:T(8,128)(2,1)S(1)} custom-call(bf16[256,1536]{1,0:T(8,128)(2,1)S(1)} %copy-done.3, bf16[128,1536]{1,0:T(8,128)(2,1)S(1)} %gather_sums.1.here_ref, bf16[128,1536]{1,0:T(8,128)(2,1)S(1)} %collective-permute-done.1.far_ref, f32[1536]{0:T(1024)S(1)} %copy-done.6, f32[1536]{0:T(1024)S(1)} %copy-done.7, ...), custom_call_target="tpu_custom_call" | custom-call | flops 150994944 | bytes 1179648 | tf_op jit(solution)/shard_map/embed/pallas_call | solution.py:137
  21.3 0.0 copy-start.10
  21.3 1.9 %collective-permute-start.9 = (bf16[128,384]{1,0:T(8,128)(2,1)S(1)}, bf16[128,384]{1,0:T(8,128)(2,1)S(1)}, u32[]{:S(2)}, u32[]{:S(2)}) collective-permute-start(bf16[128,384]{1,0:T(8,128)(2,1)S(1)} %embed.1.refs_0_.refs_4_), channel_id=1, source_target_pairs={{0,4},{4,0},{8,12},{12,8},{1,5},{5,1},{9,13},{13,9},{2,6},{6,2},{1... | collective-permute-start | bytes 294920 | tf_op jit(solution)/shard_map/ppermute | solution.py:452
  23.2 1.5 %collective-permute-start.7 = (bf16[128,384]{1,0:T(8,128)(2,1)S(1)}, bf16[128,384]{1,0:T(8,128)(2,1)S(1)}, u32[]{:S(2)}, u32[]{:S(2)}) collective-permute-start(bf16[128,384]{1,0:T(8,128)(2,1)S(1)} %embed.1.refs_0_.refs_4_), channel_id=1, source_target_pairs={{0,2},{1,3},{2,0},{3,1},{4,6},{5,7},{6,4},{7,5},{8,10},{9,11},{10,... | collective-permute-start | bytes 294920 | tf_op jit(solution)/shard_map/ppermute | solution.py:449
  24.7 2.6 %collective-permute-start.13 = (bf16[128,384]{1,0:T(8,128)(2,1)S(1)}, bf16[128,384]{1,0:T(8,128)(2,1)S(1)}, u32[]{:S(2)}, u32[]{:S(2)}) collective-permute-start(bf16[128,384]{1,0:T(8,128)(2,1)S(1)} %embed.1.refs_0_.refs_4_), channel_id=1, source_target_pairs={{0,8},{4,12},{8,0},{12,4},{1,9},{5,13},{9,1},{13,5},{2,10},{6,14},... | collective-permute-start | bytes 294920 | tf_op jit(solution)/shard_map/ppermute | solution.py:452
  27.3 0.0 collective-permute-start.6
  27.3 0.0 collective-permute-done.9.refs_0_.refs_6_
  27.3 1.2 %collective-permute-start.11 = (bf16[128,384]{1,0:T(8,128)(2,1)S(1)}, bf16[128,384]{1,0:T(8,128)(2,1)S(1)}, u32[]{:S(2)}, u32[]{:S(2)}) collective-permute-start(bf16[128,384]{1,0:T(8,128)(2,1)S(1)} %collective-permute-done.9.refs_0_.refs_6_), channel_id=1, source_target_pairs={{0,2},{1,3},{2,0},{3,1},{4,6},{5,7},{6,4},{7,5},{8,10},{9,11},{10,... | collective-permute-start | bytes 294920 | tf_op jit(solution)/shard_map/ppermute | solution.py:449
  28.4 3.6 %collective-permute-start.17 = (bf16[128,384]{1,0:T(8,128)(2,1)S(1)}, bf16[128,384]{1,0:T(8,128)(2,1)S(1)}, u32[]{:S(2)}, u32[]{:S(2)}) collective-permute-start(bf16[128,384]{1,0:T(8,128)(2,1)S(1)} %embed.1.refs_0_.refs_4_), channel_id=1, source_target_pairs={{0,12},{4,8},{8,4},{12,0},{1,13},{5,9},{9,5},{13,1},{2,14},{6,10},... | collective-permute-start | bytes 294920 | tf_op jit(solution)/shard_map/ppermute | solution.py:452
  32.0 0.0 collective-permute-done.7.refs_2_
  32.0 0.0 collective-permute-start.8
  32.0 0.0 collective-permute-done.13.refs_0_.refs_8_
  32.0 0.9 %collective-permute-start.15 = (bf16[128,384]{1,0:T(8,128)(2,1)S(1)}, bf16[128,384]{1,0:T(8,128)(2,1)S(1)}, u32[]{:S(2)}, u32[]{:S(2)}) collective-permute-start(bf16[128,384]{1,0:T(8,128)(2,1)S(1)} %collective-permute-done.13.refs_0_.refs_8_), channel_id=1, source_target_pairs={{0,2},{1,3},{2,0},{3,1},{4,6},{5,7},{6,4},{7,5},{8,10},{9,11},{10,... | collective-permute-start | bytes 294920 | tf_op jit(solution)/shard_map/ppermute | solution.py:449
  33.0 0.0 collective-permute-done.6.refs_1_.refs_5_
  33.0 0.2 collective-permute-start.10
  33.1 0.0 collective-permute-done.11.refs_2_
  33.1 0.3 collective-permute-start.12
  33.5 1.4 %collective-permute-done.17.refs_0_.refs_10_ = bf16[128,384]{1,0:T(8,128)(2,1)S(1)} collective-permute-done((bf16[128,384]{1,0:T(8,128)(2,1)S(1)}, bf16[128,384]{1,0:T(8,128)(2,1)S(1)}, u32[]{:S(2)}, u32[]{:S(2)}) %collective-permute-start.17) | collective-permute-done | bytes 98336 | tf_op jit(solution)/shard_map/ppermute | solution.py:452
  34.9 1.2 %collective-permute-start.19 = (bf16[128,384]{1,0:T(8,128)(2,1)S(1)}, bf16[128,384]{1,0:T(8,128)(2,1)S(1)}, u32[]{:S(2)}, u32[]{:S(2)}) collective-permute-start(bf16[128,384]{1,0:T(8,128)(2,1)S(1)} %collective-permute-done.17.refs_0_.refs_10_), channel_id=1, source_target_pairs={{0,2},{1,3},{2,0},{3,1},{4,6},{5,7},{6,4},{7,5},{8,10},{9,11},{10,... | collective-permute-start | bytes 294920 | tf_op jit(solution)/shard_map/ppermute | solution.py:449
  36.1 0.0 collective-permute-done.8.refs_3_
  36.1 0.0 collective-permute-start.18
  36.2 1.0 %prepare.4 = (bf16[128,768]{1,0:T(8,128)(2,1)S(1)}, bf16[256,512]{1,0:T(8,128)(2,1)S(1)}) custom-call(bf16[128,384]{1,0:T(8,128)(2,1)S(1)} %embed.1.refs_0_.refs_4_, bf16[128,384]{1,0:T(8,128)(2,1)S(1)} %collective-permute-done.6.refs_1_.refs_5_, bf16[128,384]{1,0:T(8,128)(2,1)S(1)} %collective-permute-done.7.refs_2_, ...), custom_call_target="tpu_custom_call" | custom-call | flops 226492416 | bytes 884736 | tf_op jit(solution)/shard_map/prepare/pallas_call | solution.py:248
  37.1 0.6 %collective-permute-done.15.refs_2_ = bf16[128,384]{1,0:T(8,128)(2,1)S(1)} collective-permute-done((bf16[128,384]{1,0:T(8,128)(2,1)S(1)}, bf16[128,384]{1,0:T(8,128)(2,1)S(1)}, u32[]{:S(2)}, u32[]{:S(2)}) %collective-permute-start.15) | collective-permute-done | bytes 98336 | tf_op jit(solution)/shard_map/ppermute | solution.py:449
  37.7 0.0 collective-permute-start.14
  37.7 0.0 collective-permute-done.10.refs_1_.refs_7_
  37.7 0.5 collective-permute-start.16
  38.2 0.0 collective-permute-done.12.refs_3_
  38.2 1.0 %prepare.5 = (bf16[128,768]{1,0:T(8,128)(2,1)S(1)}, bf16[256,512]{1,0:T(8,128)(2,1)S(1)}) custom-call(bf16[128,384]{1,0:T(8,128)(2,1)S(1)} %collective-permute-done.9.refs_0_.refs_6_, bf16[128,384]{1,0:T(8,128)(2,1)S(1)} %collective-permute-done.10.refs_1_.refs_7_, bf16[128,384]{1,0:T(8,128)(2,1)S(1)} %collective-permute-done.11.refs_2_, ...), custom_call_target="tpu_custom_call" | custom-call | flops 226492416 | bytes 884736 | tf_op jit(solution)/shard_map/prepare/pallas_call | solution.py:248
  39.2 0.3 collective-permute-done.19.refs_2_
  39.5 0.0 collective-permute-start.20
  39.5 0.0 collective-permute-done.14.refs_1_.refs_9_
  39.5 0.0 collective-permute-done.16.refs_3_
  39.5 1.0 %prepare.6 = (bf16[128,768]{1,0:T(8,128)(2,1)S(1)}, bf16[256,512]{1,0:T(8,128)(2,1)S(1)}) custom-call(bf16[128,384]{1,0:T(8,128)(2,1)S(1)} %collective-permute-done.13.refs_0_.refs_8_, bf16[128,384]{1,0:T(8,128)(2,1)S(1)} %collective-permute-done.14.refs_1_.refs_9_, bf16[128,384]{1,0:T(8,128)(2,1)S(1)} %collective-permute-done.15.refs_2_, ...), custom_call_target="tpu_custom_call" | custom-call | flops 226492416 | bytes 884736 | tf_op jit(solution)/shard_map/prepare/pallas_call | solution.py:248
  40.5 0.0 collective-permute-done.18.refs_1_.refs_11_
  40.5 0.3 collective-permute-done.20.refs_3_
  40.8 1.0 %prepare.7 = (bf16[128,768]{1,0:T(8,128)(2,1)S(1)}, bf16[256,512]{1,0:T(8,128)(2,1)S(1)}) custom-call(bf16[128,384]{1,0:T(8,128)(2,1)S(1)} %collective-permute-done.17.refs_0_.refs_10_, bf16[128,384]{1,0:T(8,128)(2,1)S(1)} %collective-permute-done.18.refs_1_.refs_11_, bf16[128,384]{1,0:T(8,128)(2,1)S(1)} %collective-permute-done.19.refs_2_, ...), custom_call_target="tpu_custom_call" | custom-call | flops 226492416 | bytes 884736 | tf_op jit(solution)/shard_map/prepare/pallas_call | solution.py:248
  41.8 3.4 %attend.1 = (f32[192,512]{1,0:T(8,128)S(1)}, f32[192,512]{1,0:T(8,128)S(1)}, bf16[384,512]{1,0:T(8,128)(2,1)S(1)}) custom-call(bf16[128,768]{1,0:T(8,128)(2,1)S(1)} %get-tuple-element.40.refs_0_, bf16[128,768]{1,0:T(8,128)(2,1)S(1)} %get-tuple-element.43.refs_1_, bf16[128,768]{1,0:T(8,128)(2,1)S(1)} %get-tuple-element.47.refs_2_, ...), custom_call_target="tpu_custom_call" | custom-call | flops 1207959552 | bytes 393216 | tf_op jit(solution)/shard_map/attend/pallas_call | solution.py:351
  45.3 0.3 collective-permute-start.21
  45.5 1.5 %collective-permute-done.21 = bf16[384,512]{1,0:T(8,128)(2,1)S(1)} collective-permute-done((bf16[384,512]{1,0:T(8,128)(2,1)S(1)}, bf16[384,512]{1,0:T(8,128)(2,1)S(1)}, u32[]{:S(2)}, u32[]{:S(2)}) %collective-permute-start.21) | collective-permute-done | bytes 393248 | tf_op jit(solution)/shard_map/ppermute | solution.py:449
  47.1 1.3 %collective-permute-start.22 = (bf16[192,512]{1,0:T(8,128)(2,1)S(1)}, bf16[192,512]{1,0:T(8,128)(2,1)S(1)}, u32[]{:S(2)}, u32[]{:S(2)}) collective-permute-start(bf16[192,512]{1,0:T(8,128)(2,1)S(1)} %add_convert_fusion.1), channel_id=1, source_target_pairs={{0,2},{1,3},{2,0},{3,1},{4,6},{5,7},{6,4},{7,5},{8,10},{9,11},{10,... | collective-permute-start | bytes 589832 | tf_op jit(solution)/shard_map/ppermute | solution.py:449
  48.4 1.1 %residual.1 = f32[192,512]{1,0:T(8,128)S(1)} custom-call(bf16[128,256]{1,0:T(8,128)(2,1)S(1)} %get-tuple-element.57.refs_4_.refs_0_, bf16[128,256]{1,0:T(8,128)(2,1)S(1)} %get-tuple-element.58.refs_4_.refs_1_, bf16[128,256]{1,0:T(8,128)(2,1)S(1)} %get-tuple-element.59.refs_4_.refs_2_, bf16[128,256]{1,0:T(8,128)(2,1)S(1)} %get-tuple-element.60.refs_4_.refs_3_, ...), custom_call_target="tpu_custom_call" | custom-call | tf_op jit(solution)/shard_map/residual/pallas_call | solution.py:413
  49.4 4.7 %collective-permute-done.22 = bf16[192,512]{1,0:T(8,128)(2,1)S(1)} collective-permute-done((bf16[192,512]{1,0:T(8,128)(2,1)S(1)}, bf16[192,512]{1,0:T(8,128)(2,1)S(1)}, u32[]{:S(2)}, u32[]{:S(2)}) %collective-permute-start.22) | collective-permute-done | bytes 196640 | tf_op jit(solution)/shard_map/ppermute | solution.py:449
  54.2 0.8 %fusion = bf16[512,192]{0,1:T(8,128)(2,1)} fusion(bf16[192,512]{1,0:T(8,128)(2,1)S(1)} %collective-permute-done.22, f32[192,512]{1,0:T(8,128)S(1)} %get-tuple-element.56, f32[192,512]{1,0:T(8,128)S(1)} %residual.1, bf16[384,512]{1,0:T(8,128)(2,1)S(1)} %collective-permute-done.21), kind=kLoop, calls=%fused_computation.2 | loop fusion | flops 589824 | bytes 1376256 | tf_op jit(solution)/shard_map/transpose | solution.py:504
  (16 shorter events, 0.1 us)
Async XLA Ops:
  0.0 20.3 %copy-start.3 = (bf16[256,1536]{1,0:T(8,128)(2,1)S(1)}, bf16[256,1536]{1,0:T(8,128)(2,1)}, u32[]{:S(2)}) copy-start(bf16[256,1536]{1,0:T(8,128)(2,1)} %rows_ref.3) | copy-start | bytes 2359300
  0.0 6.5 %copy-start.4 = (bf16[1536,192]{0,1:T(8,128)(2,1)S(1)}, bf16[1536,192]{0,1:T(8,128)(2,1)}, u32[]{:S(2)}) copy-start(bf16[1536,192]{0,1:T(8,128)(2,1)} %param.22) | copy-start | bytes 1769476
  0.0 20.3 %copy-start.7 = (f32[1536]{0:T(1024)S(1)}, f32[1536]{0:T(1024)}, u32[]{:S(2)}) copy-start(f32[1536]{0:T(1024)} %gain_ref.3) | copy-start | bytes 18436
  0.0 20.3 %copy-start.6 = (f32[1536]{0:T(1024)S(1)}, f32[1536]{0:T(1024)}, u32[]{:S(2)}) copy-start(f32[1536]{0:T(1024)} %scale_ref.1) | copy-start | bytes 18436
  0.0 0.8 %copy-start.8 = (f32[1536]{0:T(1024)S(1)}, f32[1536]{0:T(1024)}, u32[]{:S(2)}) copy-start(f32[1536]{0:T(1024)} %gain_ref.2) | copy-start | bytes 18436
  0.8 10.1 %copy-start.9 = (s32[256,1]{0,1:T(1,128)S(1)}, s32[256,1]{0,1:T(1,128)}, u32[]{:S(2)}) copy-start(s32[256,1]{0,1:T(1,128)} %param.15) | copy-start | bytes 3076
  6.0 30.2 %copy-start = (bf16[768,192]{0,1:T(8,128)(2,1)S(1)}, bf16[768,192]{0,1:T(8,128)(2,1)}, u32[]{:S(2)}) copy-start(bf16[768,192]{0,1:T(8,128)(2,1)} %param.24) | copy-start | bytes 884740
  6.0 30.1 %copy-start.1 = (bf16[768,192]{0,1:T(8,128)(2,1)S(1)}, bf16[768,192]{0,1:T(8,128)(2,1)}, u32[]{:S(2)}) copy-start(bf16[768,192]{0,1:T(8,128)(2,1)} %param.25) | copy-start | bytes 884740
  6.0 30.1 %copy-start.2 = (bf16[768,192]{0,1:T(8,128)(2,1)S(1)}, bf16[768,192]{0,1:T(8,128)(2,1)}, u32[]{:S(2)}) copy-start(bf16[768,192]{0,1:T(8,128)(2,1)} %param.26) | copy-start | bytes 884740
  6.0 30.1 %copy-start.5 = (f32[768]{0:T(1024)S(1)}, f32[768]{0:T(1024)}, u32[]{:S(2)}) copy-start(f32[768]{0:T(1024)} %refs_6_.7) | copy-start | bytes 9220
  6.0 1.9 %collective-permute-start = (bf16[128,1536]{1,0:T(8,128)(2,1)S(1)}, bf16[128,1536]{1,0:T(8,128)(2,1)S(1)}, u32[]{:S(2)}, u32[]{:S(2)}) collective-permute-start(bf16[128,1536]{1,0:T(8,128)(2,1)S(1)} %get-tuple-element.35), channel_id=1, source_target_pairs={{0,1},{1,0},{2,3},{3,2},{4,5},{5,4},{6,7},{7,6},{8,9},{9,8},{10,11... | collective-permute-start | bytes 1179656 | tf_op jit(solution)/shard_map/ppermute | solution.py:449
  6.6 13.8 %collective-permute-start.5 = (bf16[192,1536]{1,0:T(8,128)(2,1)S(1)}, bf16[192,1536]{1,0:T(8,128)(2,1)S(1)}, u32[]{:S(2)}, u32[]{:S(2)}) collective-permute-start(bf16[192,1536]{1,0:T(8,128)(2,1)S(1)} %bitcast.19), channel_id=1, source_target_pairs={{0,1},{1,0},{2,3},{3,2},{4,5},{5,4},{6,7},{7,6},{8,9},{9,8},{10,11... | collective-permute-start | bytes 1769480 | tf_op jit(solution)/shard_map/ppermute | solution.py:449
  8.0 12.3 %collective-permute-start.1 = (bf16[128,1536]{1,0:T(8,128)(2,1)S(1)}, bf16[128,1536]{1,0:T(8,128)(2,1)S(1)}, u32[]{:S(2)}, u32[]{:S(2)}) collective-permute-start(bf16[128,1536]{1,0:T(8,128)(2,1)S(1)} %gather_sums.1.here_ref), channel_id=1, source_target_pairs={{0,2},{1,3},{2,0},{3,1},{4,6},{5,7},{6,4},{7,5},{8,10},{9,11},{10,... | collective-permute-start | bytes 1179656 | tf_op jit(solution)/shard_map/ppermute | solution.py:449
  10.9 5.4 %collective-permute-start.4 = (s32[1,256]{1,0:T(1,128)S(1)}, s32[1,256]{1,0:T(1,128)S(1)}, u32[]{:S(2)}, u32[]{:S(2)}) collective-permute-start(s32[1,256]{1,0:T(1,128)S(1)} %bitcast.21), channel_id=1, source_target_pairs={{0,12},{4,8},{8,4},{12,0},{1,13},{5,9},{9,5},{13,1},{2,14},{6,10},... | collective-permute-start | bytes 3080 | tf_op jit(solution)/shard_map/ppermute | solution.py:452
  14.5 4.5 %collective-permute-start.3 = (s32[1,256]{1,0:T(1,128)S(1)}, s32[1,256]{1,0:T(1,128)S(1)}, u32[]{:S(2)}, u32[]{:S(2)}) collective-permute-start(s32[1,256]{1,0:T(1,128)S(1)} %bitcast.22), channel_id=1, source_target_pairs={{0,8},{4,12},{8,0},{12,4},{1,9},{5,13},{9,1},{13,5},{2,10},{6,14},... | collective-permute-start | bytes 3080 | tf_op jit(solution)/shard_map/ppermute | solution.py:452
  14.5 4.5 %collective-permute-start.2 = (s32[1,256]{1,0:T(1,128)S(1)}, s32[1,256]{1,0:T(1,128)S(1)}, u32[]{:S(2)}, u32[]{:S(2)}) collective-permute-start(s32[1,256]{1,0:T(1,128)S(1)} %bitcast.23), channel_id=1, source_target_pairs={{0,4},{4,0},{8,12},{12,8},{1,5},{5,1},{9,13},{13,9},{2,6},{6,2},{1... | collective-permute-start | bytes 3080 | tf_op jit(solution)/shard_map/ppermute | solution.py:452
  21.3 20.5 %copy-start.10 = (bf16[192,768]{1,0:T(8,128)(2,1)S(1)}, bf16[192,768]{1,0:T(8,128)(2,1)}, u32[]{:S(2)}) copy-start(bf16[192,768]{1,0:T(8,128)(2,1)} %refs_8_.1) | copy-start | bytes 884740
  21.3 6.0 %collective-permute-start.9 = (bf16[128,384]{1,0:T(8,128)(2,1)S(1)}, bf16[128,384]{1,0:T(8,128)(2,1)S(1)}, u32[]{:S(2)}, u32[]{:S(2)}) collective-permute-start(bf16[128,384]{1,0:T(8,128)(2,1)S(1)} %embed.1.refs_0_.refs_4_), channel_id=1, source_target_pairs={{0,4},{4,0},{8,12},{12,8},{1,5},{5,1},{9,13},{13,9},{2,6},{6,2},{1... | collective-permute-start | bytes 294920 | tf_op jit(solution)/shard_map/ppermute | solution.py:452
  23.2 8.8 %collective-permute-start.7 = (bf16[128,384]{1,0:T(8,128)(2,1)S(1)}, bf16[128,384]{1,0:T(8,128)(2,1)S(1)}, u32[]{:S(2)}, u32[]{:S(2)}) collective-permute-start(bf16[128,384]{1,0:T(8,128)(2,1)S(1)} %embed.1.refs_0_.refs_4_), channel_id=1, source_target_pairs={{0,2},{1,3},{2,0},{3,1},{4,6},{5,7},{6,4},{7,5},{8,10},{9,11},{10,... | collective-permute-start | bytes 294920 | tf_op jit(solution)/shard_map/ppermute | solution.py:449
  24.7 7.4 %collective-permute-start.13 = (bf16[128,384]{1,0:T(8,128)(2,1)S(1)}, bf16[128,384]{1,0:T(8,128)(2,1)S(1)}, u32[]{:S(2)}, u32[]{:S(2)}) collective-permute-start(bf16[128,384]{1,0:T(8,128)(2,1)S(1)} %embed.1.refs_0_.refs_4_), channel_id=1, source_target_pairs={{0,8},{4,12},{8,0},{12,4},{1,9},{5,13},{9,1},{13,5},{2,10},{6,14},... | collective-permute-start | bytes 294920 | tf_op jit(solution)/shard_map/ppermute | solution.py:452
  27.3 5.7 %collective-permute-start.6 = (bf16[128,384]{1,0:T(8,128)(2,1)S(1)}, bf16[128,384]{1,0:T(8,128)(2,1)S(1)}, u32[]{:S(2)}, u32[]{:S(2)}) collective-permute-start(bf16[128,384]{1,0:T(8,128)(2,1)S(1)} %embed.1.refs_0_.refs_4_), channel_id=1, source_target_pairs={{0,1},{1,0},{2,3},{3,2},{4,5},{5,4},{6,7},{7,6},{8,9},{9,8},{10,11... | collective-permute-start | bytes 294920 | tf_op jit(solution)/shard_map/ppermute | solution.py:449
  27.3 5.9 %collective-permute-start.11 = (bf16[128,384]{1,0:T(8,128)(2,1)S(1)}, bf16[128,384]{1,0:T(8,128)(2,1)S(1)}, u32[]{:S(2)}, u32[]{:S(2)}) collective-permute-start(bf16[128,384]{1,0:T(8,128)(2,1)S(1)} %collective-permute-done.9.refs_0_.refs_6_), channel_id=1, source_target_pairs={{0,2},{1,3},{2,0},{3,1},{4,6},{5,7},{6,4},{7,5},{8,10},{9,11},{10,... | collective-permute-start | bytes 294920 | tf_op jit(solution)/shard_map/ppermute | solution.py:449
  28.4 6.5 %collective-permute-start.17 = (bf16[128,384]{1,0:T(8,128)(2,1)S(1)}, bf16[128,384]{1,0:T(8,128)(2,1)S(1)}, u32[]{:S(2)}, u32[]{:S(2)}) collective-permute-start(bf16[128,384]{1,0:T(8,128)(2,1)S(1)} %embed.1.refs_0_.refs_4_), channel_id=1, source_target_pairs={{0,12},{4,8},{8,4},{12,0},{1,13},{5,9},{9,5},{13,1},{2,14},{6,10},... | collective-permute-start | bytes 294920 | tf_op jit(solution)/shard_map/ppermute | solution.py:452
  32.0 4.1 %collective-permute-start.8 = (bf16[128,384]{1,0:T(8,128)(2,1)S(1)}, bf16[128,384]{1,0:T(8,128)(2,1)S(1)}, u32[]{:S(2)}, u32[]{:S(2)}) collective-permute-start(bf16[128,384]{1,0:T(8,128)(2,1)S(1)} %collective-permute-done.7.refs_2_), channel_id=1, source_target_pairs={{0,1},{1,0},{2,3},{3,2},{4,5},{5,4},{6,7},{7,6},{8,9},{9,8},{10,11... | collective-permute-start | bytes 294920 | tf_op jit(solution)/shard_map/ppermute | solution.py:449
  32.0 5.7 %collective-permute-start.15 = (bf16[128,384]{1,0:T(8,128)(2,1)S(1)}, bf16[128,384]{1,0:T(8,128)(2,1)S(1)}, u32[]{:S(2)}, u32[]{:S(2)}) collective-permute-start(bf16[128,384]{1,0:T(8,128)(2,1)S(1)} %collective-permute-done.13.refs_0_.refs_8_), channel_id=1, source_target_pairs={{0,2},{1,3},{2,0},{3,1},{4,6},{5,7},{6,4},{7,5},{8,10},{9,11},{10,... | collective-permute-start | bytes 294920 | tf_op jit(solution)/shard_map/ppermute | solution.py:449
  33.0 4.7 %collective-permute-start.10 = (bf16[128,384]{1,0:T(8,128)(2,1)S(1)}, bf16[128,384]{1,0:T(8,128)(2,1)S(1)}, u32[]{:S(2)}, u32[]{:S(2)}) collective-permute-start(bf16[128,384]{1,0:T(8,128)(2,1)S(1)} %collective-permute-done.9.refs_0_.refs_6_), channel_id=1, source_target_pairs={{0,1},{1,0},{2,3},{3,2},{4,5},{5,4},{6,7},{7,6},{8,9},{9,8},{10,11... | collective-permute-start | bytes 294920 | tf_op jit(solution)/shard_map/ppermute | solution.py:449
  33.1 5.1 %collective-permute-start.12 = (bf16[128,384]{1,0:T(8,128)(2,1)S(1)}, bf16[128,384]{1,0:T(8,128)(2,1)S(1)}, u32[]{:S(2)}, u32[]{:S(2)}) collective-permute-start(bf16[128,384]{1,0:T(8,128)(2,1)S(1)} %collective-permute-done.11.refs_2_), channel_id=1, source_target_pairs={{0,1},{1,0},{2,3},{3,2},{4,5},{5,4},{6,7},{7,6},{8,9},{9,8},{10,11... | collective-permute-start | bytes 294920 | tf_op jit(solution)/shard_map/ppermute | solution.py:449
  34.9 4.6 %collective-permute-start.19 = (bf16[128,384]{1,0:T(8,128)(2,1)S(1)}, bf16[128,384]{1,0:T(8,128)(2,1)S(1)}, u32[]{:S(2)}, u32[]{:S(2)}) collective-permute-start(bf16[128,384]{1,0:T(8,128)(2,1)S(1)} %collective-permute-done.17.refs_0_.refs_10_), channel_id=1, source_target_pairs={{0,2},{1,3},{2,0},{3,1},{4,6},{5,7},{6,4},{7,5},{8,10},{9,11},{10,... | collective-permute-start | bytes 294920 | tf_op jit(solution)/shard_map/ppermute | solution.py:449
  36.1 4.4 %collective-permute-start.18 = (bf16[128,384]{1,0:T(8,128)(2,1)S(1)}, bf16[128,384]{1,0:T(8,128)(2,1)S(1)}, u32[]{:S(2)}, u32[]{:S(2)}) collective-permute-start(bf16[128,384]{1,0:T(8,128)(2,1)S(1)} %collective-permute-done.17.refs_0_.refs_10_), channel_id=1, source_target_pairs={{0,1},{1,0},{2,3},{3,2},{4,5},{5,4},{6,7},{7,6},{8,9},{9,8},{10,11... | collective-permute-start | bytes 294920 | tf_op jit(solution)/shard_map/ppermute | solution.py:449
  37.7 1.8 %collective-permute-start.14 = (bf16[128,384]{1,0:T(8,128)(2,1)S(1)}, bf16[128,384]{1,0:T(8,128)(2,1)S(1)}, u32[]{:S(2)}, u32[]{:S(2)}) collective-permute-start(bf16[128,384]{1,0:T(8,128)(2,1)S(1)} %collective-permute-done.13.refs_0_.refs_8_), channel_id=1, source_target_pairs={{0,1},{1,0},{2,3},{3,2},{4,5},{5,4},{6,7},{7,6},{8,9},{9,8},{10,11... | collective-permute-start | bytes 294920 | tf_op jit(solution)/shard_map/ppermute | solution.py:449
  37.7 1.8 %collective-permute-start.16 = (bf16[128,384]{1,0:T(8,128)(2,1)S(1)}, bf16[128,384]{1,0:T(8,128)(2,1)S(1)}, u32[]{:S(2)}, u32[]{:S(2)}) collective-permute-start(bf16[128,384]{1,0:T(8,128)(2,1)S(1)} %collective-permute-done.15.refs_2_), channel_id=1, source_target_pairs={{0,1},{1,0},{2,3},{3,2},{4,5},{5,4},{6,7},{7,6},{8,9},{9,8},{10,11... | collective-permute-start | bytes 294920 | tf_op jit(solution)/shard_map/ppermute | solution.py:449
  39.5 1.3 %collective-permute-start.20 = (bf16[128,384]{1,0:T(8,128)(2,1)S(1)}, bf16[128,384]{1,0:T(8,128)(2,1)S(1)}, u32[]{:S(2)}, u32[]{:S(2)}) collective-permute-start(bf16[128,384]{1,0:T(8,128)(2,1)S(1)} %collective-permute-done.19.refs_2_), channel_id=1, source_target_pairs={{0,1},{1,0},{2,3},{3,2},{4,5},{5,4},{6,7},{7,6},{8,9},{9,8},{10,11... | collective-permute-start | bytes 294920 | tf_op jit(solution)/shard_map/ppermute | solution.py:449
  45.3 1.8 %collective-permute-start.21 = (bf16[384,512]{1,0:T(8,128)(2,1)S(1)}, bf16[384,512]{1,0:T(8,128)(2,1)S(1)}, u32[]{:S(2)}, u32[]{:S(2)}) collective-permute-start(bf16[384,512]{1,0:T(8,128)(2,1)S(1)} %get-tuple-element.61), channel_id=1, source_target_pairs={{0,1},{1,0},{2,3},{3,2},{4,5},{5,4},{6,7},{7,6},{8,9},{9,8},{10,11... | collective-permute-start | bytes 1179656 | tf_op jit(solution)/shard_map/ppermute | solution.py:449
  47.1 7.1 %collective-permute-start.22 = (bf16[192,512]{1,0:T(8,128)(2,1)S(1)}, bf16[192,512]{1,0:T(8,128)(2,1)S(1)}, u32[]{:S(2)}, u32[]{:S(2)}) collective-permute-start(bf16[192,512]{1,0:T(8,128)(2,1)S(1)} %add_convert_fusion.1), channel_id=1, source_target_pairs={{0,2},{1,3},{2,0},{3,1},{4,6},{5,7},{6,4},{7,5},{8,10},{9,11},{10,... | collective-permute-start | bytes 589832 | tf_op jit(solution)/shard_map/ppermute | solution.py:449
